TPU v7x, 32 devices: a whole 2x2x4 slice. The times are simulated.
32 devices in a mesh: qx: 8 (over y, x, core), qy: 4 (over z).
Axes of the slice: x: 2, y: 2, z: 4, core: 2. Of those that a mesh axis runs over, the one named last changes fastest.
Arguments:
- image_tiles: bfloat16 [8, 4, 256, 64, 128], P('qx', 'qy'), may hold values from -6 to 6
- observed: bfloat16 [8, 4, 256, 64, 128], P('qx', 'qy'), may hold values from -6 to 6
- phases: float32 [8, 4, 256, 64, 128], P('qx', 'qy'), may hold values from -3.140625 to 3.140625
- interpolate: bfloat16 [64, 64], replicated, may hold values from -0.75 to 0.75
- local_weights: bfloat16 [8, 4, 2, 4, 4, 64, 64], P('qx', 'qy'), may hold values from -0.375 to 0.375
- merge_weights: bfloat16 [8, 4, 2, 4, 4, 64, 64], P('qx', 'qy'), may hold values from -0.375 to 0.375
- output_weight: bfloat16 [64, 64], replicated, may hold values from -0.75 to 0.75
Outputs:
- gradient: bfloat16 [8, 4, 256, 64, 128], P('qx', 'qy')
All inputs are finite; a program needn't handle non-finite values.
Results may differ from a plain program's by a relative error of at most 0.02.
Values may be sent and summed in bfloat16 or wider, within the bound.
No kernel may reach another device: no remote copies, remote signals or barrier semaphores. Data moves between devices by JAX's collectives and lax.ppermute only.
A program may use at most 128 MiB of HBM per device.

v0:
```python
import jax
import jax.numpy as jnp
from jax import lax
from jax.sharding import PartitionSpec as P


def partner(value, axis, apart):
    mask = 2**apart
    pairs = [(source, source ^ mask) for source in range(lax.axis_size(axis))]
    return lax.ppermute(value, axis, pairs)


def mixing(weight, data, form):
    return jnp.einsum(form, weight, data, preferred_element_type=jnp.float32).astype(jnp.bfloat16)


def level_bit(axis_count, level_index, depth):
    total_bits = axis_count.bit_length() - 1
    return level_index * (total_bits - 1) // max(depth - 1, 1)


def choose_pair(stacked, own_bit, axis_number):
    kept = lax.dynamic_index_in_dim(stacked, own_bit, axis_number, keepdims=False)
    outgoing = lax.dynamic_index_in_dim(stacked, 1 - own_bit, axis_number, keepdims=False)
    return (kept, outgoing)


def place_pair(kept, received, own_bit):
    paired = jnp.stack([kept, received])
    return jnp.where(own_bit == 0, paired, jnp.flip(paired, 0))


def forward_across_step(stacked, own_bit, swap_bit, axis_number):
    kept, outgoing = choose_pair(stacked, own_bit, axis_number)
    received = partner(outgoing, "qx", swap_bit)
    return place_pair(kept, received, own_bit)


def forward_down_step(stacked, own_bit, swap_bit, axis_number):
    kept, outgoing = choose_pair(stacked, own_bit, axis_number)
    received = partner(outgoing, "qy", swap_bit)
    return place_pair(kept, received, own_bit)


def adjoint_across_step(stacked, own_bit, swap_bit, axis_number):
    kept, outgoing = choose_pair(stacked, own_bit, axis_number)
    received = partner(outgoing, "qx", swap_bit)
    return place_pair(kept, received, own_bit)


def adjoint_down_step(stacked, own_bit, swap_bit, axis_number):
    kept, outgoing = choose_pair(stacked, own_bit, axis_number)
    received = partner(outgoing, "qy", swap_bit)
    return place_pair(kept, received, own_bit)


def route_level(data, across_bit, down_bit, across_level, down_level, across_step, down_step):
    layout = data.shape
    halves = data.reshape((2, 2) + layout[1:])
    first_step = across_step(halves, across_bit, across_level, 0)
    second_step = down_step(first_step, down_bit, down_level, 1)
    sources = jnp.swapaxes(second_step, 0, 1)
    return sources.reshape(layout)


def local(image_tiles, observed, phases, interpolate, local_weights, merge_weights, output_weight):
    groups = image_tiles.shape[2]
    rank_size = image_tiles.shape[3]
    inner_boxes = image_tiles.shape[4]
    local_depth = local_weights.shape[2]
    merge_depth = merge_weights.shape[2]
    quarter_size = groups // 4
    levels = local_weights[0, 0]
    merges = merge_weights[0, 0]
    across_index = lax.axis_index("qx")
    down_index = lax.axis_index("qy")
    across_count = lax.axis_size("qx")
    down_count = lax.axis_size("qy")
    current = mixing(interpolate, image_tiles[0, 0], "op,gpl->gol")
    for section_index in range(local_depth):
        stride_size = 4**section_index
        blocked = current.reshape(
            groups // (4 * stride_size), 4, stride_size, rank_size, inner_boxes
        )
        current = mixing(levels[section_index], blocked, "kcor,acbrl->akbol").reshape(
            groups, rank_size, inner_boxes
        )
    current = current.reshape(4, quarter_size, rank_size, inner_boxes)
    for level_index in range(merge_depth):
        across_level = level_bit(across_count, level_index, merge_depth)
        down_level = level_bit(down_count, level_index, merge_depth)
        across_bit = jnp.right_shift(across_index, across_level) & 1
        down_bit = jnp.right_shift(down_index, down_level) & 1
        pieces = route_level(
            current,
            across_bit,
            down_bit,
            across_level,
            down_level,
            forward_across_step,
            forward_down_step,
        )
        current = mixing(merges[level_index], pieces, "scor,chrl->shol")
    merged_y = current.reshape(groups, rank_size, inner_boxes)
    cas_wave = jnp.cos(phases[0, 0]) + jnp.sin(phases[0, 0])
    predicted = jnp.einsum(
        "or,grl->gol", output_weight, merged_y, preferred_element_type=jnp.float32
    )
    residual = (cas_wave * predicted - observed[0, 0].astype(jnp.float32)).astype(jnp.bfloat16)
    weighted = (cas_wave * residual.astype(jnp.float32)).astype(jnp.bfloat16)
    back = mixing(output_weight, weighted, "or,gol->grl")
    back = back.reshape(4, quarter_size, rank_size, inner_boxes)
    for level_index in reversed(range(merge_depth)):
        across_level = level_bit(across_count, level_index, merge_depth)
        down_level = level_bit(down_count, level_index, merge_depth)
        across_bit = jnp.right_shift(across_index, across_level) & 1
        down_bit = jnp.right_shift(down_index, down_level) & 1
        terms = mixing(merges[level_index], back, "scor,shol->chrl")
        back = route_level(
            terms,
            across_bit,
            down_bit,
            across_level,
            down_level,
            adjoint_across_step,
            adjoint_down_step,
        )
    current = back.reshape(groups, rank_size, inner_boxes)
    for section_index in reversed(range(local_depth)):
        stride_size = 4**section_index
        blocked = current.reshape(
            groups // (4 * stride_size), 4, stride_size, rank_size, inner_boxes
        )
        current = mixing(levels[section_index], blocked, "kcor,akbol->acbrl").reshape(
            groups, rank_size, inner_boxes
        )
    gradient = mixing(interpolate, current, "op,gol->gpl")
    return gradient[None, None]


def solution(mesh):
    placed = (
        P("qx", "qy", None, None, None),
        P("qx", "qy", None, None, None),
        P("qx", "qy", None, None, None),
        P(),
        P("qx", "qy", None, None, None, None, None),
        P("qx", "qy", None, None, None, None, None),
        P(),
    )
    return jax.shard_map(
        local,
        mesh=mesh,
        in_specs=placed,
        out_specs=P("qx", "qy", None, None, None),
        check_vma=False,
    )
```

profile of v0, /device:TPU:0, one launch (start us, length us, event | category | flops | bytes accessed | tf_op | source)
XLA Modules:
  0.0 494.0 jit_solution(827614676385230291)
XLA Ops:
  0.7 3.5 fusion.22
  7.3 3.0 copy.17
  10.3 5.0 %constant_dynamic-slice_fusion.4 = (bf16[1,2,64,64,128]{4,3,2,1,0:T(8,128)(2,1)S(1)}, bf16[2,64,64,128]{3,2,1,0:T(8,128)(2,1)}) fusion(bf16[2,2,64,64,128]{4,3,2,1,0:T(8,128)(2,1)} %bitcast.240, s32[]{:T(128)S(6)} %select_n.80, s32[]{:T(128)S(6)} %select_n.81), kind=kLoop, calls=%fused_computation.79 | loop fusion | bytes 8388616 | tf_op jit(solution)/shard_map/jit(dynamic_index_in_dim)/dynamic_slice | solution.py:23
  15.8 4.1 collective-permute-done
  23.5 2.3 dynamic-slice_bitcast_fusion.9
  25.8 2.9 collective-permute-start.1
  28.8 46.2 %collective-permute-done.1 = bf16[2,64,64,128]{3,2,1,0:T(8,128)(2,1)} collective-permute-done((bf16[2,64,64,128]{3,2,1,0:T(8,128)(2,1)}, bf16[2,64,64,128]{3,2,1,0:T(8,128)(2,1)}, u32[]{:S(2)}, u32[]{:S(2)}) %collective-permute-start.1) | collective-permute-done | bytes 2097184 | tf_op jit(solution)/shard_map/ppermute | solution.py:10
  80.6 2.3 constant_dynamic-slice_fusion.3
  84.6 45.8 %collective-permute-done.2 = bf16[2,64,64,128]{3,2,0,1:T(8,128)(2,1)} collective-permute-done((bf16[2,64,64,128]{3,2,0,1:T(8,128)(2,1)}, bf16[2,64,64,128]{3,2,0,1:T(8,128)(2,1)}, u32[]{:S(2)}, u32[]{:S(2)}) %collective-permute-start.2) | collective-permute-done | bytes 2097184 | tf_op jit(solution)/shard_map/ppermute | solution.py:10
  132.4 2.1 reverse_select_fusion.5
  134.5 2.3 dynamic-slice_bitcast_fusion.6
  136.8 2.4 collective-permute-start.3
  139.2 90.0 %collective-permute-done.3 = bf16[2,64,64,128]{3,2,0,1:T(8,128)(2,1)} collective-permute-done((bf16[2,64,64,128]{3,2,0,1:T(8,128)(2,1)}, bf16[2,64,64,128]{3,2,0,1:T(8,128)(2,1)}, u32[]{:S(2)}, u32[]{:S(2)}) %collective-permute-start.3) | collective-permute-done | bytes 2097184 | tf_op jit(solution)/shard_map/ppermute | solution.py:10
  231.2 2.0 reverse_select_fusion.4
  234.8 3.0 copy.19
  237.8 37.1 %fusion.19 = bf16[256,128,64]{1,2,0:T(8,128)(2,1)} fusion(f32[1,1,256,64,128]{4,3,2,1,0:T(8,128)} %param.9, bf16[1,1,256,64,128]{4,3,2,1,0:T(8,128)(2,1)} %param.8, bf16[256,64,128]{2,1,0:T(8,128)(2,1)} %bitcast.238, bf16[64,64]{1,0:T(8,128)(2,1)S(1)} %copy-done.3), kind=kOutput, calls=%fused_computation.46 | convolution fusion | flops 555745280 | bytes 20979712 | tf_op jit(solution)/shard_map/or,gol->grl/dot_general | solution.py:14
  274.9 3.5 bitcast_convert_fusion.3
  281.3 45.9 %collective-permute-done.4 = bf16[2,64,64,128]{3,2,0,1:T(8,128)(2,1)S(1)} collective-permute-done((bf16[2,64,64,128]{3,2,0,1:T(8,128)(2,1)S(1)}, bf16[2,64,64,128]{3,2,0,1:T(8,128)(2,1)S(1)}, u32[]{:S(2)}, u32[]{:S(2)}) %collective-permute-start.4) | collective-permute-done | bytes 2097184 | tf_op jit(solution)/shard_map/ppermute | solution.py:10
  327.7 2.1 reverse_select_fusion.3
  330.9 91.9 %collective-permute-done.5 = bf16[2,64,64,128]{3,2,0,1:T(8,128)(2,1)S(1)} collective-permute-done((bf16[2,64,64,128]{3,2,0,1:T(8,128)(2,1)S(1)}, bf16[2,64,64,128]{3,2,0,1:T(8,128)(2,1)S(1)}, u32[]{:S(2)}, u32[]{:S(2)}) %collective-permute-start.5) | collective-permute-done | bytes 2097184 | tf_op jit(solution)/shard_map/ppermute | solution.py:10
  423.2 2.0 reverse_select_fusion.2
  428.6 4.1 collective-permute-done.6
  436.7 47.7 %collective-permute-done.7 = bf16[2,64,64,128]{3,2,1,0:T(8,128)(2,1)S(1)} collective-permute-done((bf16[2,64,64,128]{3,2,1,0:T(8,128)(2,1)S(1)}, bf16[2,64,64,128]{3,2,1,0:T(8,128)(2,1)S(1)}, u32[]{:S(2)}, u32[]{:S(2)}) %collective-permute-start.7) | collective-permute-done | bytes 2097184 | tf_op jit(solution)/shard_map/ppermute | solution.py:10
  490.5 3.3 convert_bitcast_fusion
  (39 shorter events, 38.9 us)
Async XLA Ops:
  0.0 0.7 copy-start
  0.7 3.5 copy-start.2
  15.3 4.6 collective-permute-start
  25.8 49.2 %collective-permute-start.1 = (bf16[2,64,64,128]{3,2,1,0:T(8,128)(2,1)}, bf16[2,64,64,128]{3,2,1,0:T(8,128)(2,1)}, u32[]{:S(2)}, u32[]{:S(2)}) collective-permute-start(bf16[2,64,64,128]{3,2,1,0:T(8,128)(2,1)} %get-tuple-element.18), channel_id=1, source_target_pairs={{0,1},{1,0},{2,3},{3,2},{4,5},{5,4},{6,7},{7,6},{8,9},{9,8},{10,11... | collective-permute-start | bytes 6291464 | tf_op jit(solution)/shard_map/ppermute | solution.py:10
  77.0 1.7 copy-start.1
  82.9 47.5 %collective-permute-start.2 = (bf16[2,64,64,128]{3,2,0,1:T(8,128)(2,1)}, bf16[2,64,64,128]{3,2,0,1:T(8,128)(2,1)}, u32[]{:S(2)}, u32[]{:S(2)}) collective-permute-start(bf16[2,64,64,128]{3,2,0,1:T(8,128)(2,1)} %get-tuple-element.16), channel_id=1, source_target_pairs={{0,16},{4,20},{8,24},{12,28},{16,0},{20,4},{24,8},{28,12},{1,17},{... | collective-permute-start | bytes 6291464 | tf_op jit(solution)/shard_map/ppermute | solution.py:10
  136.8 92.4 %collective-permute-start.3 = (bf16[2,64,64,128]{3,2,0,1:T(8,128)(2,1)}, bf16[2,64,64,128]{3,2,0,1:T(8,128)(2,1)}, u32[]{:S(2)}, u32[]{:S(2)}) collective-permute-start(bf16[2,64,64,128]{3,2,0,1:T(8,128)(2,1)} %get-tuple-element.14), channel_id=1, source_target_pairs={{0,2},{1,3},{2,0},{3,1},{4,6},{5,7},{6,4},{7,5},{8,10},{9,11},{10,... | collective-permute-start | bytes 6291464 | tf_op jit(solution)/shard_map/ppermute | solution.py:10
  234.8 3.0 copy-start.3
  280.3 47.0 %collective-permute-start.4 = (bf16[2,64,64,128]{3,2,0,1:T(8,128)(2,1)S(1)}, bf16[2,64,64,128]{3,2,0,1:T(8,128)(2,1)S(1)}, u32[]{:S(2)}, u32[]{:S(2)}) collective-permute-start(bf16[2,64,64,128]{3,2,0,1:T(8,128)(2,1)S(1)} %get-tuple-element.12), channel_id=1, source_target_pairs={{0,16},{4,20},{8,24},{12,28},{16,0},{20,4},{24,8},{28,12},{1,17},{... | collective-permute-start | bytes 6291464 | tf_op jit(solution)/shard_map/ppermute | solution.py:10
  330.8 91.9 %collective-permute-start.5 = (bf16[2,64,64,128]{3,2,0,1:T(8,128)(2,1)S(1)}, bf16[2,64,64,128]{3,2,0,1:T(8,128)(2,1)S(1)}, u32[]{:S(2)}, u32[]{:S(2)}) collective-permute-start(bf16[2,64,64,128]{3,2,0,1:T(8,128)(2,1)S(1)} %get-tuple-element.10), channel_id=1, source_target_pairs={{0,2},{1,3},{2,0},{3,1},{4,6},{5,7},{6,4},{7,5},{8,10},{9,11},{10,... | collective-permute-start | bytes 6291464 | tf_op jit(solution)/shard_map/ppermute | solution.py:10
  428.5 4.2 collective-permute-start.6
  436.6 47.7 %collective-permute-start.7 = (bf16[2,64,64,128]{3,2,1,0:T(8,128)(2,1)S(1)}, bf16[2,64,64,128]{3,2,1,0:T(8,128)(2,1)S(1)}, u32[]{:S(2)}, u32[]{:S(2)}) collective-permute-start(bf16[2,64,64,128]{3,2,1,0:T(8,128)(2,1)S(1)} %get-tuple-element.6), channel_id=1, source_target_pairs={{0,1},{1,0},{2,3},{3,2},{4,5},{5,4},{6,7},{7,6},{8,9},{9,8},{10,11... | collective-permute-start | bytes 6291464 | tf_op jit(solution)/shard_map/ppermute | solution.py:10
where the time goes:
time: 501 us; the launch traced here: 494 us
  waiting for transfers between devices  376 us (75%)
  matrix products  57.9 us (12%)
  local copies, waits for them, and re-layouts  25.8 us (5%)
  other arithmetic  25.3 us (5%)
  starting transfers between devices  8.82 us (2%)
    ppermute x8, waiting for transfers between devices, partner(): return lax.ppermute(value, axis, pairs)  376 us
    dot_general x11, matrix products, mixing(): jnp.einsum(form, weight, data, preferred_element_type=jnp.float32)  57.9 us
    select_n x8, other arithmetic, place_pair(): return jnp.where(own_bit == 0, paired, jnp.flip(paired, 0))  15.2 us
    dynamic_slice x4, local copies, waits for them, and re-layouts, choose_pair(): lax.dynamic_index_in_dim(stacked, own_bit, axis_number, keepdims=False)  11 us
    another operation x8, other arithmetic, place_pair(): paired = jnp.stack([kept, received])  10.1 us
  transfers between devices with their start and end apart: 8, of which 8 were waited for; matrix products, arithmetic and copies ran while one was open for 0% of the time, Pallas kernels for 0%

commit v1 on v0

v1 whole, which is shorter than its diff:
```python
import functools

import jax
import jax.numpy as jnp
import numpy as np
from jax import lax
from jax.experimental import pallas as pl
from jax.experimental.pallas import tpu as pltpu
from jax.sharding import PartitionSpec as P

PIECES = ((4, 12), (16,), (16,), (12, 4))
ROOT2 = float(np.sqrt(2.0))
QUARTER_PI = float(np.pi / 4)
INV_PI = float(1.0 / np.pi)
PI_HIGH = 3.140625
PI_MID = float(np.float32(np.pi - 3.140625))
PI_LOW = float(np.pi - 3.140625 - float(np.float32(np.pi - 3.140625)))


def level_bit(axis_count, level_index, depth):
    total_bits = axis_count.bit_length() - 1
    return level_index * (total_bits - 1) // max(depth - 1, 1)


def dot(a, b):
    return jnp.dot(a, b, preferred_element_type=jnp.float32)


def cas(angle):
    turns = jnp.floor(angle * INV_PI + 0.75)
    rest = ((angle - turns * PI_HIGH) - turns * PI_MID) - turns * PI_LOW + QUARTER_PI
    square = rest * rest
    poly = jnp.float32(-2.5052108e-8)
    for c in (2.7557319e-6, -1.9841270e-4, 8.3333333e-3, -1.6666667e-1, 1.0):
        poly = poly * square + jnp.float32(c)
    half = turns * 0.5
    odd = half - jnp.floor(half)
    sign = ROOT2 - (4.0 * ROOT2) * odd
    return poly * rest * sign


def stacked(columns):
    return jnp.concatenate([jnp.concatenate(row, axis=1) for row in columns], axis=0)


def tile(y, i, j, r, n):
    return y[i * r : (i + 1) * r, j * n : (j + 1) * n]


def prep_local_kernel(lw_ref, ip_ref, w0_ref, w1_ref, w0t_ref, w1t_ref):
    r = ip_ref.shape[0]
    ip = ip_ref[...]
    for k in range(4):
        rows = pl.ds(k * r, r)
        for c in range(4):
            cols = pl.ds(c * r, r)
            a = dot(lw_ref[0, k, c], ip)
            b = lw_ref[1, k, c]
            w0_ref[rows, cols] = a.astype(jnp.bfloat16)
            w1_ref[rows, cols] = b
            w0t_ref[cols, rows] = a.T.astype(jnp.bfloat16)
            w1t_ref[cols, rows] = b.astype(jnp.float32).T.astype(jnp.bfloat16)


def prep_merge_kernel(bits_ref, mw_ref, ow_ref, a_ref, at_ref, b_ref, bt_ref):
    r = ow_ref.shape[0]
    ow = ow_ref[...]
    k0, k1 = bits_ref[0], bits_ref[1]
    for s in range(4):
        rows = pl.ds(s * r, r)
        for c in range(4):
            cols = pl.ds(c * r, r)
            a = mw_ref[0, k1 ^ s, k0 ^ c]
            b = dot(ow, mw_ref[1, s, k1 ^ c])
            a_ref[rows, cols] = a
            at_ref[cols, rows] = a.astype(jnp.float32).T.astype(jnp.bfloat16)
            b_ref[rows, cols] = b.astype(jnp.bfloat16)
            bt_ref[cols, rows] = b.T.astype(jnp.bfloat16)


def forward_local_kernel(sizes, bits_ref, image_ref, w0_ref, w1_ref, *outs):
    r, n = image_ref.shape[-2:]
    w0, w1 = w0_ref[...], w1_ref[...]
    for d in range(4):
        q = bits_ref[0] ^ d
        x = stacked([[image_ref[q, 0, 4 * a + c] for a in range(4)] for c in range(4)])
        y = dot(w0, x).astype(jnp.bfloat16)
        x = stacked([[tile(y, e, a, r, n) for e in range(4)] for a in range(4)])
        y = dot(w1, x).astype(jnp.bfloat16)
        start = 0
        for piece, size in enumerate(sizes):
            for h in range(size):
                a, e = divmod(start + h, 4)
                outs[4 * piece + d][h] = tile(y, a, e, r, n)
            start += size


def adjoint_local_kernel(sizes, bits_ref, w0t_ref, w1t_ref, *refs):
    ins, out_ref = refs[: 4 * len(sizes)], refs[-1]
    r, n = out_ref.shape[-2:]
    w0t, w1t = w0t_ref[...], w1t_ref[...]
    places = [(piece, h) for piece, size in enumerate(sizes) for h in range(size)]
    for d in range(4):
        q = bits_ref[0] ^ d

        def piece_of(a, e):
            piece, h = places[4 * a + e]
            return ins[4 * piece + d][h]

        x = stacked([[piece_of(a, e) for e in range(4)] for a in range(4)])
        y = dot(w1t, x).astype(jnp.bfloat16)
        x = stacked([[tile(y, a, e, r, n) for a in range(4)] for e in range(4)])
        y = dot(w0t, x).astype(jnp.bfloat16)
        for a in range(4):
            for c in range(4):
                out_ref[q, 0, 4 * a + c] = tile(y, c, a, r, n)


def merge_kernel(w_ref, *refs):
    ins, outs = refs[:4], refs[4:]
    size, r, n = ins[0].shape
    w = w_ref[...]
    for i in range(0, size, 4):
        x = stacked([[ref[i + j] for j in range(4)] for ref in ins])
        y = dot(w, x).astype(jnp.bfloat16)
        for d in range(4):
            for j in range(4):
                outs[d][i + j] = tile(y, d, j, r, n)


def residual_kernel(b_ref, bt_ref, phases_ref, observed_ref, *refs):
    ins, outs = refs[:4], refs[4:]
    size, r, n = ins[0].shape
    x = stacked([[ref[j] for j in range(size)] for ref in ins])
    predicted = dot(b_ref[...], x)
    weighted = []
    for s in range(4):
        row = []
        for j in range(size):
            wave = cas(phases_ref[s, j])
            residual = wave * tile(predicted, s, j, r, n) - observed_ref[s, j].astype(jnp.float32)
            residual = residual.astype(jnp.bfloat16).astype(jnp.float32)
            row.append((wave * residual).astype(jnp.bfloat16))
        weighted.append(row)
    y = dot(bt_ref[...], stacked(weighted)).astype(jnp.bfloat16)
    for d in range(4):
        for j in range(size):
            outs[d][j] = tile(y, d, j, r, n)


SMEM = pl.BlockSpec(memory_space=pltpu.SMEM)
VMEM = pl.BlockSpec(memory_space=pltpu.VMEM)
PARAMS = pltpu.CompilerParams(vmem_limit_bytes=40 * 2**20)


def cost(levels, columns, byte_count):
    return pl.CostEstimate(
        flops=levels * 2 * 256 * 256 * columns, bytes_accessed=byte_count, transcendentals=0
    )


def exchange(blocks, mask_x, mask_y):
    count_x, count_y = lax.axis_size("qx"), lax.axis_size("qy")
    along_y = [(s, s ^ mask_y) for s in range(count_y)]
    along_x = [(s, s ^ mask_x) for s in range(count_x)]
    both = [
        (x * count_y + y, (x ^ mask_x) * count_y + (y ^ mask_y))
        for x in range(count_x)
        for y in range(count_y)
    ]
    return (
        blocks[0],
        lax.ppermute(blocks[1], "qy", along_y),
        lax.ppermute(blocks[2], "qx", along_x),
        lax.ppermute(blocks[3], ("qx", "qy"), both),
    )


def local(image_tiles, observed, phases, interpolate, local_weights, merge_weights, output_weight):
    groups, r, n = image_tiles.shape[2:]
    depth = merge_weights.shape[2]
    chunks = len(PIECES)
    quarter = groups // 4
    chunk = quarter // chunks
    bf16 = jnp.bfloat16
    box = r * n * 2

    masks, own = [], []
    for level in range(depth):
        bit_x = level_bit(lax.axis_size("qx"), level, depth)
        bit_y = level_bit(lax.axis_size("qy"), level, depth)
        masks.append((2**bit_x, 2**bit_y))
        own.append(
            2 * (jnp.right_shift(lax.axis_index("qx"), bit_x) & 1)
            + (jnp.right_shift(lax.axis_index("qy"), bit_y) & 1)
        )
    bits = jnp.stack(own).astype(jnp.int32)
    square = jax.ShapeDtypeStruct((4 * r, 4 * r), bf16)

    with jax.named_scope("prep_local"):
        w0, w1, w0t, w1t = pl.pallas_call(
            prep_local_kernel,
            out_shape=[square] * 4,
            in_specs=[VMEM] * 2,
            out_specs=[VMEM] * 4,
            cost_estimate=cost(0, 0, 10 * 4 * r * 4 * r),
        )(local_weights[0, 0], interpolate)
    with jax.named_scope("prep_merge"):
        m0, m0t, m1, m1t = pl.pallas_call(
            prep_merge_kernel,
            out_shape=[square] * 4,
            in_specs=[SMEM, VMEM, VMEM],
            out_specs=[VMEM] * 4,
            cost_estimate=cost(0, 0, 10 * 4 * r * 4 * r),
        )(bits, merge_weights[0, 0], output_weight)

    image = image_tiles.reshape(4, chunks, chunk, r, n)
    phase4 = phases.reshape(4, quarter, r, n)
    observed4 = observed.reshape(4, quarter, r, n)

    def merge(weight, blocks):
        size = blocks[0].shape[0]
        return pl.pallas_call(
            merge_kernel,
            out_shape=[jax.ShapeDtypeStruct((size, r, n), bf16)] * 4,
            in_specs=[VMEM] * 5,
            out_specs=[VMEM] * 4,
            compiler_params=PARAMS,
            cost_estimate=cost(1, size * n, 8 * size * box),
        )(weight, *blocks)

    def through_data(blocks, start):
        size = blocks[0].shape[0]
        step = 4
        small = pl.BlockSpec((step, r, n), lambda i: (i, 0, 0))
        large = pl.BlockSpec((4, step, r, n), lambda i: (0, start // step + i, 0, 0))
        whole = pl.BlockSpec((4 * r, 4 * r), lambda i: (0, 0))
        return pl.pallas_call(
            residual_kernel,
            grid=(size // step,),
            out_shape=[jax.ShapeDtypeStruct((size, r, n), bf16)] * 4,
            in_specs=[whole, whole, large, large] + [small] * 4,
            out_specs=[small] * 4,
            compiler_params=PARAMS,
            cost_estimate=cost(6, size * n, 20 * size * box),
        )(m1, m1t, phase4, observed4, *blocks)

    pieces = []
    for index, sizes in enumerate(PIECES):
        with jax.named_scope(f"local_forward_{index}"):
            outs = pl.pallas_call(
                functools.partial(forward_local_kernel, sizes),
                grid=(1,),
                out_shape=[
                    jax.ShapeDtypeStruct((size, r, n), bf16) for size in sizes for _ in range(4)
                ],
                in_specs=[
                    SMEM,
                    pl.BlockSpec((4, 1, chunk, r, n), lambda i, index=index: (0, index, 0, 0, 0)),
                    pl.BlockSpec((4 * r, 4 * r), lambda i: (0, 0)),
                    pl.BlockSpec((4 * r, 4 * r), lambda i: (0, 0)),
                ],
                out_specs=[
                    pl.BlockSpec((size, r, n), lambda i: (0, 0, 0))
                    for size in sizes
                    for _ in range(4)
                ],
                compiler_params=PARAMS,
                cost_estimate=cost(2, chunk * n, 8 * chunk * box),
            )(bits, image, w0, w1)
        start = index * chunk
        for piece, size in enumerate(sizes):
            pieces.append((index, start, outs[4 * piece : 4 * piece + 4]))
            start += size

    returned = [[] for _ in PIECES]
    for index, start, blocks in pieces:
        with jax.named_scope(f"merges_{start}"):
            blocks = exchange(blocks, *masks[0])
            blocks = merge(m0, blocks)
            blocks = exchange(blocks, *masks[1])
            blocks = through_data(blocks, start)
            blocks = exchange(blocks, *masks[1])
            blocks = merge(m0t, blocks)
            returned[index].extend(exchange(blocks, *masks[0]))

    gradient = None
    for index, sizes in enumerate(PIECES):
        with jax.named_scope(f"local_adjoint_{index}"):
            blocks = returned[index]
            operands = [bits, w0t, w1t, *blocks]
            in_specs = [
                SMEM,
                pl.BlockSpec((4 * r, 4 * r), lambda i: (0, 0)),
                pl.BlockSpec((4 * r, 4 * r), lambda i: (0, 0)),
            ] + [pl.BlockSpec(b.shape, lambda i: (0, 0, 0)) for b in blocks]
            aliases = {}
            if gradient is not None:
                aliases = {len(operands): 0}
                operands.append(gradient)
                in_specs.append(pl.BlockSpec(memory_space=pl.ANY))
            gradient = pl.pallas_call(
                functools.partial(adjoint_local_kernel, sizes),
                grid=(1,),
                out_shape=jax.ShapeDtypeStruct((4, chunks, chunk, r, n), bf16),
                in_specs=in_specs,
                out_specs=pl.BlockSpec(
                    (4, 1, chunk, r, n), lambda i, index=index: (0, index, 0, 0, 0)
                ),
                input_output_aliases=aliases,
                compiler_params=PARAMS,
                cost_estimate=cost(2, chunk * n, 8 * chunk * box),
            )(*operands)
    return gradient.reshape(1, 1, groups, r, n)


def solution(mesh):
    split = P("qx", "qy", None, None, None)
    weights = P("qx", "qy", None, None, None, None, None)
    return jax.shard_map(
        local,
        mesh=mesh,
        in_specs=(split, split, split, P(), weights, weights, P()),
        out_specs=split,
        check_vma=False,
    )
```

time: 501 us -> 293 us (0.58); the launches traced: 494 us -> 292 us
  waiting for transfers between devices: 376 us -> 163 us
  starting transfers between devices: 8.82 us -> 67.5 us
  matrix products: 57.9 us -> 0 us
  Pallas kernels: 0 us -> 44.5 us
  other arithmetic: 25.3 us -> 0.08 us
  local copies, waits for them, and re-layouts: 25.8 us -> 16.7 us
    ppermute x8 -> x72, waiting for transfers between devices: 376 us -> 163 us  [the longest x24 87 us: exchange(): lax.ppermute(blocks[3], ('qx', 'qy'), both)]
    ppermute x8 -> x72, starting transfers between devices: 8.82 us -> 67.5 us  [the longest x24 33.5 us: exchange(): lax.ppermute(blocks[1], 'qy', along_y)]
    dot_general x11 -> x0, matrix products: 57.9 us -> none  [mixing(): jnp.einsum(form, weight, data, preferred_element_type=jnp.float32)]
    pallas_call x0 -> x28, Pallas kernels: none -> 44.5 us  [the longest x6 17 us: through_data(): pl.pallas_call(residual_kernel, grid=(size // step,), out_shape=[jax.Shap...]
    unnamed x8 -> x44, local copies, waits for them, and re-layouts: 0.73 us -> 16.7 us
    select_n x8 -> x0, other arithmetic: 15.2 us -> none  [place_pair(): return jnp.where(own_bit == 0, paired, jnp.flip(paired, 0))]
    dynamic_slice x5 -> x0, local copies, waits for them, and re-layouts: 11.1 us -> none  [the longest x4 11 us: choose_pair(): lax.dynamic_index_in_dim(stacked, own_bit, axis_number, keepdims=False)]
    another operation x8 -> x1, other arithmetic: 10.1 us -> 0.07 us  [local(): bits = jnp.stack(own).astype(jnp.int32)]
  transfers between devices with their start and end apart: 8 -> 72, of which waited for: 8 -> 30; matrix products, arithmetic and copies ran while one was open for 0% -> 0% of each run, Pallas kernels for 0% -> 13%
where the time goes in v1:
time: 293 us; the launch traced here: 292 us
  waiting for transfers between devices  163 us (56%)
  starting transfers between devices  67.5 us (23%)
  Pallas kernels  44.5 us (15%)
  local copies, waits for them, and re-layouts  16.7 us (6%)
    ppermute x24, waiting for transfers between devices, exchange(): lax.ppermute(blocks[3], ('qx', 'qy'), both)  87 us
    ppermute x24, waiting for transfers between devices, exchange(): lax.ppermute(blocks[1], 'qy', along_y)  76 us
    ppermute x24, starting transfers between devices, exchange(): lax.ppermute(blocks[1], 'qy', along_y)  33.5 us
    ppermute x24, starting transfers between devices, exchange(): lax.ppermute(blocks[3], ('qx', 'qy'), both)  21.4 us
    pallas_call x6, Pallas kernels, through_data(): pl.pallas_call(residual_kernel, grid=(size // step,), out_shape=[jax.Shap...  17 us
    unnamed x44, local copies, waits for them, and re-layouts  16.7 us
    ppermute x24, starting transfers between devices, exchange(): lax.ppermute(blocks[2], 'qx', along_x)  12.6 us
    pallas_call x4, Pallas kernels, local(): pl.pallas_call(functools.partial(adjoint_local_kernel, sizes), grid=(1,),...  11.1 us
  transfers between devices with their start and end apart: 72, of which 30 were waited for; matrix products, arithmetic and copies ran while one was open for 0% of the time, Pallas kernels for 13%

profile of v1, /device:TPU:0, one launch (start us, length us, event | category | flops | bytes accessed | tf_op | source)
XLA Modules:
  0.0 292.4 jit_solution(9340572367203667199)
XLA Ops:
  42.8 3.5 %collective-permute-start.56 = (bf16[4,64,128]{2,1,0:T(8,128)(2,1)S(1)}, bf16[4,64,128]{2,1,0:T(8,128)(2,1)S(1)}, u32[]{:S(2)}, u32[]{:S(2)}) collective-permute-start(bf16[4,64,128]{2,1,0:T(8,128)(2,1)S(1)} %get-tuple-element.192), channel_id=1, source_target_pairs={{0,18},{1,19},{2,16},{3,17},{4,22},{5,23},{6,20},{7,21},{8,26},{9,... | collective-permute-start | bytes 196616 | tf_op jit(solution)/shard_map/merges_0/ppermute | solution.py:175
  48.9 3.5 %collective-permute-start.20 = (bf16[4,64,128]{2,1,0:T(8,128)(2,1)S(1)}, bf16[4,64,128]{2,1,0:T(8,128)(2,1)S(1)}, u32[]{:S(2)}, u32[]{:S(2)}) collective-permute-start(bf16[4,64,128]{2,1,0:T(8,128)(2,1)S(1)} %get-tuple-element.144), channel_id=1, source_target_pairs={{0,18},{1,19},{2,16},{3,17},{4,22},{5,23},{6,20},{7,21},{8,26},{9,... | collective-permute-start | bytes 196616 | tf_op jit(solution)/shard_map/merges_60/ppermute | solution.py:175
  65.8 3.6 %collective-permute-done.2.refs_3_ = bf16[12,64,128]{2,1,0:T(8,128)(2,1)S(1)} collective-permute-done((bf16[12,64,128]{2,1,0:T(8,128)(2,1)S(1)}, bf16[12,64,128]{2,1,0:T(8,128)(2,1)S(1)}, u32[]{:S(2)}, u32[]{:S(2)}) %collective-permute-start.2) | collective-permute-done | bytes 196640 | tf_op jit(solution)/shard_map/merges_48/ppermute | solution.py:175
  80.5 8.0 %collective-permute-done.38.refs_3_ = bf16[16,64,128]{2,1,0:T(8,128)(2,1)S(1)} collective-permute-done((bf16[16,64,128]{2,1,0:T(8,128)(2,1)S(1)}, bf16[16,64,128]{2,1,0:T(8,128)(2,1)S(1)}, u32[]{:S(2)}, u32[]{:S(2)}) %collective-permute-start.38) | collective-permute-done | bytes 262176 | tf_op jit(solution)/shard_map/merges_16/ppermute | solution.py:175
  88.8 6.0 %collective-permute-done.24.refs_1_ = bf16[16,64,128]{2,1,0:T(8,128)(2,1)S(1)} collective-permute-done((bf16[16,64,128]{2,1,0:T(8,128)(2,1)S(1)}, bf16[16,64,128]{2,1,0:T(8,128)(2,1)S(1)}, u32[]{:S(2)}, u32[]{:S(2)}) %collective-permute-start.24) | collective-permute-done | bytes 262176 | tf_op jit(solution)/shard_map/merges_32/ppermute | solution.py:173
  108.4 14.3 %collective-permute-done.65.refs_3_ = bf16[12,64,128]{2,1,0:T(8,128)(2,1)S(1)} collective-permute-done((bf16[12,64,128]{2,1,0:T(8,128)(2,1)S(1)}, bf16[12,64,128]{2,1,0:T(8,128)(2,1)S(1)}, u32[]{:S(2)}, u32[]{:S(2)}) %collective-permute-start.65) | collective-permute-done | bytes 196640 | tf_op jit(solution)/shard_map/merges_4/ppermute | solution.py:175
  129.8 12.5 %collective-permute-done.5.refs_3_ = bf16[12,64,128]{2,1,0:T(8,128)(2,1)S(1)} collective-permute-done((bf16[12,64,128]{2,1,0:T(8,128)(2,1)S(1)}, bf16[12,64,128]{2,1,0:T(8,128)(2,1)S(1)}, u32[]{:S(2)}, u32[]{:S(2)}) %collective-permute-start.5) | collective-permute-done | bytes 196640 | tf_op jit(solution)/shard_map/merges_48/ppermute | solution.py:175
  153.7 9.7 %collective-permute-done.41.refs_3_ = bf16[16,64,128]{2,1,0:T(8,128)(2,1)S(1)} collective-permute-done((bf16[16,64,128]{2,1,0:T(8,128)(2,1)S(1)}, bf16[16,64,128]{2,1,0:T(8,128)(2,1)S(1)}, u32[]{:S(2)}, u32[]{:S(2)}) %collective-permute-start.41) | collective-permute-done | bytes 262176 | tf_op jit(solution)/shard_map/merges_16/ppermute | solution.py:175
  164.8 4.2 %collective-permute-done.27.refs_1_ = bf16[16,64,128]{2,1,0:T(8,128)(2,1)S(1)} collective-permute-done((bf16[16,64,128]{2,1,0:T(8,128)(2,1)S(1)}, bf16[16,64,128]{2,1,0:T(8,128)(2,1)S(1)}, u32[]{:S(2)}, u32[]{:S(2)}) %collective-permute-start.27) | collective-permute-done | bytes 262176 | tf_op jit(solution)/shard_map/merges_32/ppermute | solution.py:173
  172.0 4.8 %merges_16.4 = (bf16[16,64,128]{2,1,0:T(8,128)(2,1)S(1)}, bf16[16,64,128]{2,1,0:T(8,128)(2,1)S(1)}, bf16[16,64,128]{2,1,0:T(8,128)(2,1)S(1)}, bf16[16,64,128]{2,1,0:T(8,128)(2,1)S(1)}) custom-call(bf16[256,256]{1,0:T(8,128)(2,1)S(1)} %copy-done.6, bf16[256,256]{1,0:T(8,128)(2,1)S(1)} %copy-done.8, f32[4,64,64,128]{3,2,1,0:T(8,128)} %bitcast.8, ...), custom_call_target="tpu_custom_call" | custom-call | flops 1610612736 | bytes 5242880 | tf_op jit(solution)/shard_map/merges_16/pallas_call | solution.py:238
  176.8 6.3 %collective-permute-done.29.refs_3_ = bf16[16,64,128]{2,1,0:T(8,128)(2,1)S(1)} collective-permute-done((bf16[16,64,128]{2,1,0:T(8,128)(2,1)S(1)}, bf16[16,64,128]{2,1,0:T(8,128)(2,1)S(1)}, u32[]{:S(2)}, u32[]{:S(2)}) %collective-permute-start.29) | collective-permute-done | bytes 262176 | tf_op jit(solution)/shard_map/merges_32/ppermute | solution.py:175
  183.1 9.8 %collective-permute-done.66.refs_1_ = bf16[12,64,128]{2,1,0:T(8,128)(2,1)S(1)} collective-permute-done((bf16[12,64,128]{2,1,0:T(8,128)(2,1)S(1)}, bf16[12,64,128]{2,1,0:T(8,128)(2,1)S(1)}, u32[]{:S(2)}, u32[]{:S(2)}) %collective-permute-start.66) | collective-permute-done | bytes 196640 | tf_op jit(solution)/shard_map/merges_4/ppermute | solution.py:173
  193.5 4.8 %merges_32.4 = (bf16[16,64,128]{2,1,0:T(8,128)(2,1)S(1)}, bf16[16,64,128]{2,1,0:T(8,128)(2,1)S(1)}, bf16[16,64,128]{2,1,0:T(8,128)(2,1)S(1)}, bf16[16,64,128]{2,1,0:T(8,128)(2,1)S(1)}) custom-call(bf16[256,256]{1,0:T(8,128)(2,1)S(1)} %copy-done.6, bf16[256,256]{1,0:T(8,128)(2,1)S(1)} %copy-done.8, f32[4,64,64,128]{3,2,1,0:T(8,128)} %bitcast.9, ...), custom_call_target="tpu_custom_call" | custom-call | flops 1610612736 | bytes 5242880 | tf_op jit(solution)/shard_map/merges_32/pallas_call | solution.py:238
  199.8 12.7 %collective-permute-done.6.refs_1_ = bf16[12,64,128]{2,1,0:T(8,128)(2,1)S(1)} collective-permute-done((bf16[12,64,128]{2,1,0:T(8,128)(2,1)S(1)}, bf16[12,64,128]{2,1,0:T(8,128)(2,1)S(1)}, u32[]{:S(2)}, u32[]{:S(2)}) %collective-permute-start.6) | collective-permute-done | bytes 196640 | tf_op jit(solution)/shard_map/merges_48/ppermute | solution.py:173
  213.1 14.8 %collective-permute-done.42.refs_1_ = bf16[16,64,128]{2,1,0:T(8,128)(2,1)S(1)} collective-permute-done((bf16[16,64,128]{2,1,0:T(8,128)(2,1)S(1)}, bf16[16,64,128]{2,1,0:T(8,128)(2,1)S(1)}, u32[]{:S(2)}, u32[]{:S(2)}) %collective-permute-start.42) | collective-permute-done | bytes 262176 | tf_op jit(solution)/shard_map/merges_16/ppermute | solution.py:173
  228.4 3.9 %collective-permute-start.8 = (bf16[12,64,128]{2,1,0:T(8,128)(2,1)S(1)}, bf16[12,64,128]{2,1,0:T(8,128)(2,1)S(1)}, u32[]{:S(2)}, u32[]{:S(2)}) collective-permute-start(bf16[12,64,128]{2,1,0:T(8,128)(2,1)S(1)} %get-tuple-element.128), channel_id=1, source_target_pairs={{0,18},{1,19},{2,16},{3,17},{4,22},{5,23},{6,20},{7,21},{8,26},{9,... | collective-permute-start | bytes 589832 | tf_op jit(solution)/shard_map/merges_48/ppermute | solution.py:175
  233.6 5.7 %collective-permute-done.30.refs_1_ = bf16[16,64,128]{2,1,0:T(8,128)(2,1)S(1)} collective-permute-done((bf16[16,64,128]{2,1,0:T(8,128)(2,1)S(1)}, bf16[16,64,128]{2,1,0:T(8,128)(2,1)S(1)}, u32[]{:S(2)}, u32[]{:S(2)}) %collective-permute-start.30) | collective-permute-done | bytes 262176 | tf_op jit(solution)/shard_map/merges_32/ppermute | solution.py:173
  239.8 5.1 %collective-permute-done.32.refs_3_ = bf16[16,64,128]{2,1,0:T(8,128)(2,1)S(1)} collective-permute-done((bf16[16,64,128]{2,1,0:T(8,128)(2,1)S(1)}, bf16[16,64,128]{2,1,0:T(8,128)(2,1)S(1)}, u32[]{:S(2)}, u32[]{:S(2)}) %collective-permute-start.32) | collective-permute-done | bytes 262176 | tf_op jit(solution)/shard_map/merges_32/ppermute | solution.py:175
  245.4 3.7 %collective-permute-done.8.refs_3_ = bf16[12,64,128]{2,1,0:T(8,128)(2,1)S(1)} collective-permute-done((bf16[12,64,128]{2,1,0:T(8,128)(2,1)S(1)}, bf16[12,64,128]{2,1,0:T(8,128)(2,1)S(1)}, u32[]{:S(2)}, u32[]{:S(2)}) %collective-permute-start.8) | collective-permute-done | bytes 196640 | tf_op jit(solution)/shard_map/merges_48/ppermute | solution.py:175
  249.1 4.1 %collective-permute-done.69.refs_5_ = bf16[12,64,128]{2,1,0:T(8,128)(2,1)S(1)} collective-permute-done((bf16[12,64,128]{2,1,0:T(8,128)(2,1)S(1)}, bf16[12,64,128]{2,1,0:T(8,128)(2,1)S(1)}, u32[]{:S(2)}, u32[]{:S(2)}) %collective-permute-start.69) | collective-permute-done | bytes 196640 | tf_op jit(solution)/shard_map/merges_4/ppermute | solution.py:173
  254.8 8.1 %collective-permute-done.71.refs_7_ = bf16[12,64,128]{2,1,0:T(8,128)(2,1)S(1)} collective-permute-done((bf16[12,64,128]{2,1,0:T(8,128)(2,1)S(1)}, bf16[12,64,128]{2,1,0:T(8,128)(2,1)S(1)}, u32[]{:S(2)}, u32[]{:S(2)}) %collective-permute-start.71) | collective-permute-done | bytes 196640 | tf_op jit(solution)/shard_map/merges_4/ppermute | solution.py:175
  263.9 4.6 %collective-permute-done.47.refs_3_ = bf16[16,64,128]{2,1,0:T(8,128)(2,1)S(1)} collective-permute-done((bf16[16,64,128]{2,1,0:T(8,128)(2,1)S(1)}, bf16[16,64,128]{2,1,0:T(8,128)(2,1)S(1)}, u32[]{:S(2)}, u32[]{:S(2)}) %collective-permute-start.47) | collective-permute-done | bytes 262176 | tf_op jit(solution)/shard_map/merges_16/ppermute | solution.py:175
  268.5 5.8 %collective-permute-done.33.refs_1_ = bf16[16,64,128]{2,1,0:T(8,128)(2,1)S(1)} collective-permute-done((bf16[16,64,128]{2,1,0:T(8,128)(2,1)S(1)}, bf16[16,64,128]{2,1,0:T(8,128)(2,1)S(1)}, u32[]{:S(2)}, u32[]{:S(2)}) %collective-permute-start.33) | collective-permute-done | bytes 262176 | tf_op jit(solution)/shard_map/merges_32/ppermute | solution.py:173
  285.3 4.3 %collective-permute-done.23.refs_7_ = bf16[4,64,128]{2,1,0:T(8,128)(2,1)S(1)} collective-permute-done((bf16[4,64,128]{2,1,0:T(8,128)(2,1)S(1)}, bf16[4,64,128]{2,1,0:T(8,128)(2,1)S(1)}, u32[]{:S(2)}, u32[]{:S(2)}) %collective-permute-start.23) | collective-permute-done | bytes 65568 | tf_op jit(solution)/shard_map/merges_60/ppermute | solution.py:175
  (194 shorter events, 128.1 us)
Async XLA Ops:
  28.5 27.1 %collective-permute-start.60 = (bf16[12,64,128]{2,1,0:T(8,128)(2,1)S(1)}, bf16[12,64,128]{2,1,0:T(8,128)(2,1)S(1)}, u32[]{:S(2)}, u32[]{:S(2)}) collective-permute-start(bf16[12,64,128]{2,1,0:T(8,128)(2,1)S(1)} %get-tuple-element.198), channel_id=1, source_target_pairs={{0,1},{1,0},{2,3},{3,2},{4,5},{5,4},{6,7},{7,6},{8,9},{9,8},{10,11... | collective-permute-start | bytes 589832 | tf_op jit(solution)/shard_map/merges_4/ppermute | solution.py:173
  77.9 21.9 %collective-permute-start.26 = (bf16[16,64,128]{2,1,0:T(8,128)(2,1)S(1)}, bf16[16,64,128]{2,1,0:T(8,128)(2,1)S(1)}, u32[]{:S(2)}, u32[]{:S(2)}) collective-permute-start(bf16[16,64,128]{2,1,0:T(8,128)(2,1)S(1)} %get-tuple-element.152), channel_id=1, source_target_pairs={{0,5},{1,4},{2,7},{3,6},{4,1},{5,0},{6,3},{7,2},{8,13},{9,12},{10,... | collective-permute-start | bytes 786440 | tf_op jit(solution)/shard_map/merges_32/ppermute | solution.py:175
  78.9 24.9 %collective-permute-start.63 = (bf16[12,64,128]{2,1,0:T(8,128)(2,1)S(1)}, bf16[12,64,128]{2,1,0:T(8,128)(2,1)S(1)}, u32[]{:S(2)}, u32[]{:S(2)}) collective-permute-start(bf16[12,64,128]{2,1,0:T(8,128)(2,1)S(1)} %get-tuple-element.202), channel_id=1, source_target_pairs={{0,2},{1,3},{2,0},{3,1},{4,6},{5,7},{6,4},{7,5},{8,10},{9,11},{10,... | collective-permute-start | bytes 589832 | tf_op jit(solution)/shard_map/merges_4/ppermute | solution.py:173
  94.8 27.9 %collective-permute-start.65 = (bf16[12,64,128]{2,1,0:T(8,128)(2,1)S(1)}, bf16[12,64,128]{2,1,0:T(8,128)(2,1)S(1)}, u32[]{:S(2)}, u32[]{:S(2)}) collective-permute-start(bf16[12,64,128]{2,1,0:T(8,128)(2,1)S(1)} %get-tuple-element.204), channel_id=1, source_target_pairs={{0,18},{1,19},{2,16},{3,17},{4,22},{5,23},{6,20},{7,21},{8,26},{9,... | collective-permute-start | bytes 589832 | tf_op jit(solution)/shard_map/merges_4/ppermute | solution.py:175
  99.8 27.0 %collective-permute-start.3 = (bf16[12,64,128]{2,1,0:T(8,128)(2,1)S(1)}, bf16[12,64,128]{2,1,0:T(8,128)(2,1)S(1)}, u32[]{:S(2)}, u32[]{:S(2)}) collective-permute-start(bf16[12,64,128]{2,1,0:T(8,128)(2,1)S(1)} %get-tuple-element.122), channel_id=1, source_target_pairs={{0,2},{1,3},{2,0},{3,1},{4,6},{5,7},{6,4},{7,5},{8,10},{9,11},{10,... | collective-permute-start | bytes 589832 | tf_op jit(solution)/shard_map/merges_48/ppermute | solution.py:173
  103.5 23.4 %collective-permute-start.4 = (bf16[12,64,128]{2,1,0:T(8,128)(2,1)S(1)}, bf16[12,64,128]{2,1,0:T(8,128)(2,1)S(1)}, u32[]{:S(2)}, u32[]{:S(2)}) collective-permute-start(bf16[12,64,128]{2,1,0:T(8,128)(2,1)S(1)} %get-tuple-element.123), channel_id=1, source_target_pairs={{0,16},{4,20},{8,24},{12,28},{16,0},{20,4},{24,8},{28,12},{1,17},{... | collective-permute-start | bytes 589832 | tf_op jit(solution)/shard_map/merges_48/ppermute | solution.py:174
  103.8 38.5 %collective-permute-start.5 = (bf16[12,64,128]{2,1,0:T(8,128)(2,1)S(1)}, bf16[12,64,128]{2,1,0:T(8,128)(2,1)S(1)}, u32[]{:S(2)}, u32[]{:S(2)}) collective-permute-start(bf16[12,64,128]{2,1,0:T(8,128)(2,1)S(1)} %get-tuple-element.124), channel_id=1, source_target_pairs={{0,18},{1,19},{2,16},{3,17},{4,22},{5,23},{6,20},{7,21},{8,26},{9,... | collective-permute-start | bytes 589832 | tf_op jit(solution)/shard_map/merges_48/ppermute | solution.py:175
  107.5 40.5 %collective-permute-start.39 = (bf16[16,64,128]{2,1,0:T(8,128)(2,1)S(1)}, bf16[16,64,128]{2,1,0:T(8,128)(2,1)S(1)}, u32[]{:S(2)}, u32[]{:S(2)}) collective-permute-start(bf16[16,64,128]{2,1,0:T(8,128)(2,1)S(1)} %get-tuple-element.170), channel_id=1, source_target_pairs={{0,2},{1,3},{2,0},{3,1},{4,6},{5,7},{6,4},{7,5},{8,10},{9,11},{10,... | collective-permute-start | bytes 786440 | tf_op jit(solution)/shard_map/merges_16/ppermute | solution.py:173
  122.7 25.2 %collective-permute-start.40 = (bf16[16,64,128]{2,1,0:T(8,128)(2,1)S(1)}, bf16[16,64,128]{2,1,0:T(8,128)(2,1)S(1)}, u32[]{:S(2)}, u32[]{:S(2)}) collective-permute-start(bf16[16,64,128]{2,1,0:T(8,128)(2,1)S(1)} %get-tuple-element.171), channel_id=1, source_target_pairs={{0,16},{4,20},{8,24},{12,28},{16,0},{20,4},{24,8},{28,12},{1,17},{... | collective-permute-start | bytes 786440 | tf_op jit(solution)/shard_map/merges_16/ppermute | solution.py:174
  126.8 36.6 %collective-permute-start.41 = (bf16[16,64,128]{2,1,0:T(8,128)(2,1)S(1)}, bf16[16,64,128]{2,1,0:T(8,128)(2,1)S(1)}, u32[]{:S(2)}, u32[]{:S(2)}) collective-permute-start(bf16[16,64,128]{2,1,0:T(8,128)(2,1)S(1)} %get-tuple-element.172), channel_id=1, source_target_pairs={{0,18},{1,19},{2,16},{3,17},{4,22},{5,23},{6,20},{7,21},{8,26},{9,... | collective-permute-start | bytes 786440 | tf_op jit(solution)/shard_map/merges_16/ppermute | solution.py:175
  126.9 42.1 %collective-permute-start.27 = (bf16[16,64,128]{2,1,0:T(8,128)(2,1)S(1)}, bf16[16,64,128]{2,1,0:T(8,128)(2,1)S(1)}, u32[]{:S(2)}, u32[]{:S(2)}) collective-permute-start(bf16[16,64,128]{2,1,0:T(8,128)(2,1)S(1)} %get-tuple-element.154), channel_id=1, source_target_pairs={{0,2},{1,3},{2,0},{3,1},{4,6},{5,7},{6,4},{7,5},{8,10},{9,11},{10,... | collective-permute-start | bytes 786440 | tf_op jit(solution)/shard_map/merges_32/ppermute | solution.py:173
  142.3 26.6 %collective-permute-start.28 = (bf16[16,64,128]{2,1,0:T(8,128)(2,1)S(1)}, bf16[16,64,128]{2,1,0:T(8,128)(2,1)S(1)}, u32[]{:S(2)}, u32[]{:S(2)}) collective-permute-start(bf16[16,64,128]{2,1,0:T(8,128)(2,1)S(1)} %get-tuple-element.155), channel_id=1, source_target_pairs={{0,16},{4,20},{8,24},{12,28},{16,0},{20,4},{24,8},{28,12},{1,17},{... | collective-permute-start | bytes 786440 | tf_op jit(solution)/shard_map/merges_32/ppermute | solution.py:174
  147.9 35.2 %collective-permute-start.29 = (bf16[16,64,128]{2,1,0:T(8,128)(2,1)S(1)}, bf16[16,64,128]{2,1,0:T(8,128)(2,1)S(1)}, u32[]{:S(2)}, u32[]{:S(2)}) collective-permute-start(bf16[16,64,128]{2,1,0:T(8,128)(2,1)S(1)} %get-tuple-element.156), channel_id=1, source_target_pairs={{0,18},{1,19},{2,16},{3,17},{4,22},{5,23},{6,20},{7,21},{8,26},{9,... | collective-permute-start | bytes 786440 | tf_op jit(solution)/shard_map/merges_32/ppermute | solution.py:175
  147.9 44.9 %collective-permute-start.66 = (bf16[12,64,128]{2,1,0:T(8,128)(2,1)S(1)}, bf16[12,64,128]{2,1,0:T(8,128)(2,1)S(1)}, u32[]{:S(2)}, u32[]{:S(2)}) collective-permute-start(bf16[12,64,128]{2,1,0:T(8,128)(2,1)S(1)} %get-tuple-element.206), channel_id=1, source_target_pairs={{0,2},{1,3},{2,0},{3,1},{4,6},{5,7},{6,4},{7,5},{8,10},{9,11},{10,... | collective-permute-start | bytes 589832 | tf_op jit(solution)/shard_map/merges_4/ppermute | solution.py:173
  163.4 34.9 %collective-permute-start.67 = (bf16[12,64,128]{2,1,0:T(8,128)(2,1)S(1)}, bf16[12,64,128]{2,1,0:T(8,128)(2,1)S(1)}, u32[]{:S(2)}, u32[]{:S(2)}) collective-permute-start(bf16[12,64,128]{2,1,0:T(8,128)(2,1)S(1)} %get-tuple-element.207), channel_id=1, source_target_pairs={{0,16},{4,20},{8,24},{12,28},{16,0},{20,4},{24,8},{28,12},{1,17},{... | collective-permute-start | bytes 589832 | tf_op jit(solution)/shard_map/merges_4/ppermute | solution.py:174
  169.0 30.8 %collective-permute-start.68 = (bf16[12,64,128]{2,1,0:T(8,128)(2,1)S(1)}, bf16[12,64,128]{2,1,0:T(8,128)(2,1)S(1)}, u32[]{:S(2)}, u32[]{:S(2)}) collective-permute-start(bf16[12,64,128]{2,1,0:T(8,128)(2,1)S(1)} %get-tuple-element.208), channel_id=1, source_target_pairs={{0,18},{1,19},{2,16},{3,17},{4,22},{5,23},{6,20},{7,21},{8,26},{9,... | collective-permute-start | bytes 589832 | tf_op jit(solution)/shard_map/merges_4/ppermute | solution.py:175
  169.0 43.5 %collective-permute-start.6 = (bf16[12,64,128]{2,1,0:T(8,128)(2,1)S(1)}, bf16[12,64,128]{2,1,0:T(8,128)(2,1)S(1)}, u32[]{:S(2)}, u32[]{:S(2)}) collective-permute-start(bf16[12,64,128]{2,1,0:T(8,128)(2,1)S(1)} %get-tuple-element.126), channel_id=1, source_target_pairs={{0,2},{1,3},{2,0},{3,1},{4,6},{5,7},{6,4},{7,5},{8,10},{9,11},{10,... | collective-permute-start | bytes 589832 | tf_op jit(solution)/shard_map/merges_48/ppermute | solution.py:173
  183.1 44.9 %collective-permute-start.42 = (bf16[16,64,128]{2,1,0:T(8,128)(2,1)S(1)}, bf16[16,64,128]{2,1,0:T(8,128)(2,1)S(1)}, u32[]{:S(2)}, u32[]{:S(2)}) collective-permute-start(bf16[16,64,128]{2,1,0:T(8,128)(2,1)S(1)} %get-tuple-element.174), channel_id=1, source_target_pairs={{0,2},{1,3},{2,0},{3,1},{4,6},{5,7},{6,4},{7,5},{8,10},{9,11},{10,... | collective-permute-start | bytes 786440 | tf_op jit(solution)/shard_map/merges_16/ppermute | solution.py:173
  198.3 30.0 %collective-permute-start.43 = (bf16[16,64,128]{2,1,0:T(8,128)(2,1)S(1)}, bf16[16,64,128]{2,1,0:T(8,128)(2,1)S(1)}, u32[]{:S(2)}, u32[]{:S(2)}) collective-permute-start(bf16[16,64,128]{2,1,0:T(8,128)(2,1)S(1)} %get-tuple-element.175), channel_id=1, source_target_pairs={{0,16},{4,20},{8,24},{12,28},{16,0},{20,4},{24,8},{28,12},{1,17},{... | collective-permute-start | bytes 786440 | tf_op jit(solution)/shard_map/merges_16/ppermute | solution.py:174
  199.8 33.9 %collective-permute-start.44 = (bf16[16,64,128]{2,1,0:T(8,128)(2,1)S(1)}, bf16[16,64,128]{2,1,0:T(8,128)(2,1)S(1)}, u32[]{:S(2)}, u32[]{:S(2)}) collective-permute-start(bf16[16,64,128]{2,1,0:T(8,128)(2,1)S(1)} %get-tuple-element.176), channel_id=1, source_target_pairs={{0,18},{1,19},{2,16},{3,17},{4,22},{5,23},{6,20},{7,21},{8,26},{9,... | collective-permute-start | bytes 786440 | tf_op jit(solution)/shard_map/merges_16/ppermute | solution.py:175
  212.5 26.8 %collective-permute-start.30 = (bf16[16,64,128]{2,1,0:T(8,128)(2,1)S(1)}, bf16[16,64,128]{2,1,0:T(8,128)(2,1)S(1)}, u32[]{:S(2)}, u32[]{:S(2)}) collective-permute-start(bf16[16,64,128]{2,1,0:T(8,128)(2,1)S(1)} %get-tuple-element.158), channel_id=1, source_target_pairs={{0,2},{1,3},{2,0},{3,1},{4,6},{5,7},{6,4},{7,5},{8,10},{9,11},{10,... | collective-permute-start | bytes 786440 | tf_op jit(solution)/shard_map/merges_32/ppermute | solution.py:173
  212.5 27.2 %collective-permute-start.31 = (bf16[16,64,128]{2,1,0:T(8,128)(2,1)S(1)}, bf16[16,64,128]{2,1,0:T(8,128)(2,1)S(1)}, u32[]{:S(2)}, u32[]{:S(2)}) collective-permute-start(bf16[16,64,128]{2,1,0:T(8,128)(2,1)S(1)} %get-tuple-element.159), channel_id=1, source_target_pairs={{0,16},{4,20},{8,24},{12,28},{16,0},{20,4},{24,8},{28,12},{1,17},{... | collective-permute-start | bytes 786440 | tf_op jit(solution)/shard_map/merges_32/ppermute | solution.py:174
  239.8 23.4 %collective-permute-start.45 = (bf16[16,64,128]{2,1,0:T(8,128)(2,1)S(1)}, bf16[16,64,128]{2,1,0:T(8,128)(2,1)S(1)}, u32[]{:S(2)}, u32[]{:S(2)}) collective-permute-start(bf16[16,64,128]{2,1,0:T(8,128)(2,1)S(1)} %get-tuple-element.178), channel_id=1, source_target_pairs={{0,1},{1,0},{2,3},{3,2},{4,5},{5,4},{6,7},{7,6},{8,9},{9,8},{10,11... | collective-permute-start | bytes 786440 | tf_op jit(solution)/shard_map/merges_16/ppermute | solution.py:173
  263.6 26.0 %collective-permute-start.10 = (bf16[12,64,128]{2,1,0:T(8,128)(2,1)S(1)}, bf16[12,64,128]{2,1,0:T(8,128)(2,1)S(1)}, u32[]{:S(2)}, u32[]{:S(2)}) collective-permute-start(bf16[12,64,128]{2,1,0:T(8,128)(2,1)S(1)} %get-tuple-element.131), channel_id=1, source_target_pairs={{0,4},{4,0},{8,12},{12,8},{16,20},{20,16},{24,28},{28,24},{1,5},{5... | collective-permute-start | bytes 589832 | tf_op jit(solution)/shard_map/merges_48/ppermute | solution.py:174
  (70 other events, 1185.6 us)

commit v2 on v1

v2 whole, which is shorter than its diff:
```python
import functools

import jax
import jax.numpy as jnp
import numpy as np
from jax import lax
from jax.experimental import pallas as pl
from jax.experimental.pallas import tpu as pltpu
from jax.sharding import PartitionSpec as P

PIECES = ((16,), (16,), (16,), (16,))
ACTIONS = (
    ".K10_", "+X00d", "+X00x", "+X00z", ".K13_", "+X03x", ".K12_", "+X02x", ".K11_", ".PM0_",
    "-X00d", "+X01x", "-X00x", "+X01z", "-X00z", ".X10_", "+X10d", "-X03x", "+X01d", "-X02x",
    "+X10x", "-X01x", "+X10z", "-X01z", "-X10d", "-X01d", ".X11_", "+X11d", "+X02z", "-X10x",
    "-X10z", ".Y10_", "+Y10x", "+X11x", "+X11z", "-X11d", "+Y10z", "-X02z", "+X02d", ".PA0_",
    "-Y10x", "+Y10d", "-X11x", "+X03z", "-X11z", ".Y11_", "+Y11d", "-Y10z", "+Y11x", "-X02d",
    ".X12_", "+X12x", "-Y10d", "+X12z", "-X03z", "+X03d", ".Y00_", "-Y11d", "+X12d", "-Y11x",
    "+Y00z", "-X12x", "+Y00d", "-X12z", "+Y11z", "-X03d", ".X13_", "+X13d", "-X12d", ".Y12_",
    "+Y12d", "-Y00z", "+X13x", "-Y00d", "+Y00x", "-Y11z", ".Y01_", "+Y01d", "-X13d", "+X13z",
    "-Y12d", "+Y01x", "-X13x", "+Y12x", "-Y00x", "+Y01z", "-Y01d", "+Y12z", ".K50_", "-X13z",
    ".Y13_", "+Y13x", "-Y01x", "+Y13d", "-Y12x", "+Y13z", "-Y01z", ".K51_", "-Y12z", ".Y02_",
    "+Y02z", "+Y02d", "-Y13x", "+Y02x", "-Y13d", "-Y13z", ".Y03_", "+Y03d", "+Y03x", "-Y02z",
    "+Y03z", "-Y02d", "-Y02x", ".K52_", "-Y03d", "-Y03x", "-Y03z", ".K53_",
)
VMEM_GRANT = 16 * 2**20
TOKEN = jax.ShapeDtypeStruct((8, 128), jnp.float32)
ROOT2 = float(np.sqrt(2.0))
QUARTER_PI = float(np.pi / 4)
INV_PI = float(1.0 / np.pi)
PI_HIGH = 3.140625
PI_MID = float(np.float32(np.pi - 3.140625))
PI_LOW = float(np.pi - 3.140625 - float(np.float32(np.pi - 3.140625)))


def level_bit(axis_count, level_index, depth):
    total_bits = axis_count.bit_length() - 1
    return level_index * (total_bits - 1) // max(depth - 1, 1)


def dot(a, b):
    return jnp.dot(a, b, preferred_element_type=jnp.float32)


def cas(angle):
    turns = jnp.floor(angle * INV_PI + 0.75)
    rest = ((angle - turns * PI_HIGH) - turns * PI_MID) - turns * PI_LOW + QUARTER_PI
    square = rest * rest
    poly = jnp.float32(-2.5052108e-8)
    for c in (2.7557319e-6, -1.9841270e-4, 8.3333333e-3, -1.6666667e-1, 1.0):
        poly = poly * square + jnp.float32(c)
    half = turns * 0.5
    odd = half - jnp.floor(half)
    sign = ROOT2 - (4.0 * ROOT2) * odd
    return poly * rest * sign


def stacked(columns):
    return jnp.concatenate([jnp.concatenate(row, axis=1) for row in columns], axis=0)


def tile(y, i, j, r, n):
    return y[i * r : (i + 1) * r, j * n : (j + 1) * n]


def own_index(masks):
    x, y = lax.axis_index("qx"), lax.axis_index("qy")
    return [
        2 * jnp.where(x & mask_x != 0, 1, 0) + jnp.where(y & mask_y != 0, 1, 0)
        for mask_x, mask_y in masks
    ]


def blocks_of(stack, r):
    return [
        jnp.concatenate([stack[4 * k + c] for c in range(4)], axis=1) for k in range(4)
    ]


def prep_adjoint_kernel(lw_ref, ip_ref, *refs):
    r = ip_ref.shape[0]
    w0t_ref, w1t_ref = refs[-3:-1]
    ip = ip_ref[...]
    for k in range(4):
        cols = pl.ds(k * r, r)
        for c in range(4):
            rows = pl.ds(c * r, r)
            w0t_ref[rows, cols] = dot(lw_ref[0, k, c], ip).T.astype(jnp.bfloat16)
            w1t_ref[rows, cols] = lw_ref[1, k, c].astype(jnp.float32).T.astype(jnp.bfloat16)


def prep_merge_kernel(masks, mw_ref, ow_ref, *refs):
    r = ow_ref.shape[0]
    a_ref, at_ref, b_ref, bt_ref = refs[-5:-1]
    ow = ow_ref[...]
    k0, k1 = own_index(masks)
    for s in range(4):
        rows = pl.ds(s * r, r)
        for c in range(4):
            cols = pl.ds(c * r, r)
            a = mw_ref[0, k1 ^ s, k0 ^ c]
            b = dot(ow, mw_ref[1, s, k1 ^ c])
            a_ref[rows, cols] = a
            at_ref[cols, rows] = a.astype(jnp.float32).T.astype(jnp.bfloat16)
            b_ref[rows, cols] = b.astype(jnp.bfloat16)
            bt_ref[cols, rows] = b.T.astype(jnp.bfloat16)


def gate_kernel(*refs):
    pass


def forward_local_kernel(masks, sizes, index, first, *refs):
    image_ref, first_ref, second_ref = refs[:3]
    refs, (tiles, sems, *held) = (refs[:-4], refs[-4:]) if first else (refs[:-2], refs[-2:])
    copies = []
    k0 = own_index(masks)[0]
    for i, (source, target) in enumerate(zip((first_ref, second_ref), held)):
        copies.append(pltpu.make_async_copy(source, target, sems.at[4 + i]))
    for d in range(4):
        copies.append(
            pltpu.make_async_copy(image_ref.at[k0 ^ d, index], tiles.at[d], sems.at[d])
        )
    for copy in copies:
        copy.start()
    if first:
        w0_ref, w1_ref = refs[-3:-1]
        outs = refs[-3 - 4 * len(sizes) : -3]
        levels, inner = held
        r = inner.shape[0]
        for copy in copies[:2]:
            copy.wait()
        copies = copies[2:]
        folded = dot(levels[0].reshape(16 * r, r), inner[...]).astype(jnp.bfloat16)
        w0 = jnp.concatenate(blocks_of(folded.reshape(16, r, r), r), axis=0)
        w1 = jnp.concatenate(blocks_of(levels[1].reshape(16, r, r), r), axis=0)
        w0_ref[...], w1_ref[...] = w0, w1
    else:
        w0, w1 = first_ref[...], second_ref[...]
        outs = refs[-1 - 4 * len(sizes) : -1]
    r, n = tiles.shape[-2:]
    for d in range(4):
        copies[d].wait()
        x = stacked([[tiles[d, 4 * a + c] for a in range(4)] for c in range(4)])
        y = dot(w0, x).astype(jnp.bfloat16)
        x = stacked([[tile(y, e, a, r, n) for e in range(4)] for a in range(4)])
        y = dot(w1, x).astype(jnp.bfloat16)
        start = 0
        for piece, size in enumerate(sizes):
            for h in range(size):
                a, e = divmod(start + h, 4)
                outs[4 * piece + d][h] = tile(y, a, e, r, n)
            start += size


def adjoint_local_kernel(masks, sizes, index, w0t_ref, w1t_ref, *refs):
    ins, out_ref, tiles, sems = refs[: 4 * len(sizes)], refs[-4], refs[-2], refs[-1]
    r, n = tiles.shape[-2:]
    w0t, w1t = w0t_ref[...], w1t_ref[...]
    places = [(piece, h) for piece, size in enumerate(sizes) for h in range(size)]
    k0 = own_index(masks)[0]
    copies = []
    for d in range(4):

        def piece_of(a, e):
            piece, h = places[4 * a + e]
            return ins[4 * piece + d][h]

        x = stacked([[piece_of(a, e) for e in range(4)] for a in range(4)])
        y = dot(w1t, x).astype(jnp.bfloat16)
        x = stacked([[tile(y, a, e, r, n) for a in range(4)] for e in range(4)])
        y = dot(w0t, x).astype(jnp.bfloat16)
        for a in range(4):
            for c in range(4):
                tiles[d, 4 * a + c] = tile(y, c, a, r, n)
        copies.append(
            pltpu.make_async_copy(tiles.at[d], out_ref.at[k0 ^ d, index], sems.at[d])
        )
        copies[-1].start()
    for copy in copies:
        copy.wait()


def merge_kernel(w_ref, *refs):
    ins, outs = refs[:4], refs[-5:-1]
    size, r, n = ins[0].shape
    w = w_ref[...]
    for i in range(0, size, 4):
        x = stacked([[ref[i + j] for j in range(4)] for ref in ins])
        y = dot(w, x).astype(jnp.bfloat16)
        for d in range(4):
            for j in range(4):
                outs[d][i + j] = tile(y, d, j, r, n)


def residual_kernel(start, b_ref, bt_ref, phases_ref, observed_ref, *refs):
    ins, outs, (angles, data, sems) = refs[:4], refs[-8:-4], refs[-3:]
    size, r, n = ins[0].shape
    copies = []
    for i in range(size // 4):
        here, there = pl.ds(4 * i, 4), pl.ds(start + 4 * i, 4)
        copies.append(
            (
                pltpu.make_async_copy(phases_ref.at[:, there], angles.at[:, here], sems.at[0, i]),
                pltpu.make_async_copy(observed_ref.at[:, there], data.at[:, here], sems.at[1, i]),
            )
        )
        for copy in copies[-1]:
            copy.start()
    for i in range(size // 4):
        x = stacked([[ref[4 * i + j] for j in range(4)] for ref in ins])
        predicted = dot(b_ref[...], x)
        for copy in copies[i]:
            copy.wait()
        weighted = []
        for s in range(4):
            row = []
            for j in range(4):
                wave = cas(angles[s, 4 * i + j])
                residual = wave * tile(predicted, s, j, r, n)
                residual = residual - data[s, 4 * i + j].astype(jnp.float32)
                residual = residual.astype(jnp.bfloat16).astype(jnp.float32)
                row.append((wave * residual).astype(jnp.bfloat16))
            weighted.append(row)
        y = dot(bt_ref[...], stacked(weighted)).astype(jnp.bfloat16)
        for d in range(4):
            for j in range(4):
                outs[d][4 * i + j] = tile(y, d, j, r, n)


VMEM = pl.BlockSpec(memory_space=pltpu.VMEM)
ANY = pl.BlockSpec(memory_space=pl.ANY)
HBM = pl.BlockSpec(memory_space=pltpu.HBM)


KERNEL_COST = pl.CostEstimate(flops=0, bytes_accessed=0, transcendentals=0)
GATE_COST = pl.CostEstimate(flops=10**9, bytes_accessed=1, transcendentals=0)


class Chain:
    def __init__(self, masks):
        self.token = None
        self.done = []
        count_x, count_y = lax.axis_size("qx"), lax.axis_size("qy")
        self.pairs = []
        for mask_x, mask_y in masks:
            along_y = [(s, s ^ mask_y) for s in range(count_y)]
            along_x = [(s, s ^ mask_x) for s in range(count_x)]
            both = [
                (x * count_y + y, (x ^ mask_x) * count_y + (y ^ mask_y))
                for x in range(count_x)
                for y in range(count_y)
            ]
            self.pairs.append((None, ("qy", along_y), ("qx", along_x), (("qx", "qy"), both)))

    def kernel(
        self, body, operands, specs, out_shapes, out_specs, aliases=None, gate=False, **options
    ):
        extra = [x for x in self.done if not any(x is y for y in operands)]
        self.done = []
        aliases = dict(aliases or {})
        token = [] if self.token is None else [self.token]
        if token:
            aliases[len(operands)] = len(out_shapes)
        outs = pl.pallas_call(
            body,
            out_shape=[*out_shapes, TOKEN],
            in_specs=[*specs, *[ANY] * (len(token) + len(extra))],
            out_specs=[*out_specs, ANY],
            input_output_aliases=aliases,
            compiler_params=pltpu.CompilerParams(vmem_limit_bytes=2**20 if gate else VMEM_GRANT),
            cost_estimate=GATE_COST if gate else KERNEL_COST,
            **options,
        )(*operands, *token, *extra)
        self.token = outs[-1]
        return outs[:-1]

    def send(self, block, level, d):
        shape = jax.ShapeDtypeStruct(block.shape, block.dtype)
        (block,) = self.kernel(gate_kernel, [block], [ANY], [shape], [ANY], {0: 0}, True)
        axis, pairs = self.pairs[level][d]
        return lax.ppermute(block, axis, pairs)


def local(image_tiles, observed, phases, interpolate, local_weights, merge_weights, output_weight):
    groups, r, n = image_tiles.shape[2:]
    depth = merge_weights.shape[2]
    chunks = len(PIECES)
    quarter = groups // 4
    chunk = quarter // chunks
    bf16 = jnp.bfloat16
    box = r * n * 2

    masks = []
    for level in range(depth):
        bit_x = level_bit(lax.axis_size("qx"), level, depth)
        bit_y = level_bit(lax.axis_size("qy"), level, depth)
        masks.append((2**bit_x, 2**bit_y))
    square = jax.ShapeDtypeStruct((4 * r, 4 * r), bf16)
    chain = Chain(masks)

    def pinned(x, shape):
        return pltpu.with_memory_space_constraint(x.reshape(shape), pltpu.HBM)

    image = pinned(image_tiles, (4, chunks, chunk, r, n))
    phase4 = pinned(phases, (4, quarter, r, n))
    observed4 = pinned(observed, (4, quarter, r, n))
    levels = pinned(local_weights, local_weights.shape[2:])
    inner = pinned(interpolate, interpolate.shape)

    def shapes(size):
        return [jax.ShapeDtypeStruct((size, r, n), bf16)] * 4

    def forward_local(index):
        sizes = PIECES[index]
        first = not prepared
        weights = [levels, inner] if first else list(prepared["local"])
        scratch = [pltpu.VMEM((4, chunk, r, n), bf16), pltpu.SemaphoreType.DMA((6,))]
        if first:
            scratch += [pltpu.VMEM(levels.shape, bf16), pltpu.VMEM((r, r), bf16)]
        outs_count = 4 * len(sizes) + 2 * first
        with jax.named_scope(f"local_forward_{index}"):
            outs = chain.kernel(
                functools.partial(forward_local_kernel, masks, sizes, index, first),
                [image, *weights],
                [HBM] + [HBM if first else VMEM] * 2,
                sum([shapes(size) for size in sizes], []) + [square] * (2 * first),
                [VMEM] * outs_count,
                scratch_shapes=scratch,
            )
        if first:
            prepared["local"] = outs[-2:]
        for piece in range(len(sizes)):
            ready["X0", first_piece[index] + piece] = outs[4 * piece : 4 * piece + 4]

    def prepare_merges():
        with jax.named_scope("prep_merge"):
            prepared["merge"] = chain.kernel(
                functools.partial(prep_merge_kernel, masks),
                [merge_weights[0, 0], output_weight],
                [VMEM, VMEM],
                [square] * 4,
                [VMEM] * 4,
            )

    def prepare_adjoint():
        with jax.named_scope("prep_adjoint"):
            prepared["adjoint"] = chain.kernel(
                prep_adjoint_kernel,
                [local_weights[0, 0], interpolate],
                [VMEM, VMEM],
                [square] * 2,
                [VMEM] * 2,
            )

    def merge(weight, blocks):
        size = blocks[0].shape[0]
        return chain.kernel(
            merge_kernel,
            [weight, *blocks],
            [VMEM] * 5,
            shapes(size),
            [VMEM] * 4,
        )

    def through_data(blocks, start):
        size = blocks[0].shape[0]
        return chain.kernel(
            functools.partial(residual_kernel, start),
            [*prepared["merge"][2:], phase4, observed4, *blocks],
            [VMEM, VMEM, HBM, HBM] + [VMEM] * 4,
            shapes(size),
            [VMEM] * 4,
            scratch_shapes=[
                pltpu.VMEM((4, size, r, n), jnp.float32),
                pltpu.VMEM((4, size, r, n), bf16),
                pltpu.SemaphoreType.DMA((2, size // 4)),
            ],
        )

    def adjoint_local(index):
        sizes = PIECES[index]
        blocks = sum([state["Y0", first_piece[index] + i] for i in range(len(sizes))], [])
        operands = [*prepared["adjoint"], *blocks]
        specs = [VMEM] * len(operands)
        aliases = {}
        if "gradient" in prepared:
            aliases = {len(operands): 0}
            operands.append(prepared["gradient"])
            specs.append(HBM)
        with jax.named_scope(f"local_adjoint_{index}"):
            (prepared["gradient"],) = chain.kernel(
                functools.partial(adjoint_local_kernel, masks, sizes, index),
                operands,
                specs,
                [jax.ShapeDtypeStruct((4, chunks, chunk, r, n), bf16)],
                [HBM],
                aliases,
                scratch_shapes=[
                    pltpu.VMEM((4, chunk, r, n), bf16),
                    pltpu.SemaphoreType.DMA((4,)),
                ],
            )

    all_sizes = sum(PIECES, ())
    starts = [sum(all_sizes[:i]) for i in range(len(all_sizes))]
    first_piece = [sum(len(p) for p in PIECES[:i]) for i in range(chunks)]
    prepared, ready, state = {}, {}, {}

    for action in ACTIONS:
        mark, name, number = action[0], action[-4:-2], int(action[-2])
        if mark == ".":
            with jax.named_scope(f"{name}_{number}"):
                if name == "K1":
                    forward_local(number)
                elif name == "PM":
                    prepare_merges()
                elif name == "PA":
                    prepare_adjoint()
                elif name == "X1":
                    ready["X1", number] = merge(prepared["merge"][0], state["X0", number])
                elif name == "Y1":
                    ready["Y1", number] = through_data(state["X1", number], starts[number])
                elif name == "Y0":
                    ready["Y0", number] = merge(prepared["merge"][1], state["Y1", number])
                else:
                    adjoint_local(number)
            continue
        d = {"z": 1, "x": 2, "d": 3}[action[-1]]
        if mark == "+":
            blocks = ready[name, number]
            got = state.setdefault((name, number), [blocks[0], None, None, None])
            with jax.named_scope(f"{name}_{number}"):
                got[d] = chain.send(blocks[d], 1 if name in ("X1", "Y1") else 0, d)
        else:
            chain.done.append(state[name, number][d])
    return prepared["gradient"].reshape(1, 1, groups, r, n)


def solution(mesh):
    split = P("qx", "qy", None, None, None)
    weights = P("qx", "qy", None, None, None, None, None)
    return jax.shard_map(
        local,
        mesh=mesh,
        in_specs=(split, split, split, P(), weights, weights, P()),
        out_specs=split,
        check_vma=False,
    )
```

time: 293 us -> 232 us (0.79)
  waiting for transfers between devices: 163 us -> 138 us
  starting transfers between devices: 67.5 us -> 50.2 us
  local copies, waits for them, and re-layouts: 16.7 us -> 0.02 us
    ppermute x72 -> x48, waiting for transfers between devices: 163 us -> 138 us  [send(): return lax.ppermute(block, axis, pairs)]
    ppermute x72 -> x48, starting transfers between devices: 67.5 us -> 50.2 us  [send(): return lax.ppermute(block, axis, pairs)]
    unnamed x44 -> x8, local copies, waits for them, and re-layouts: 16.7 us -> 0.02 us
    pallas_call x28 -> x70, Pallas kernels: 44.5 us -> 43.1 us  [kernel(): pl.pallas_call(body, out_shape=[*out_shapes, TOKEN], in_specs=[*specs, *[...]
  transfers between devices with their start and end apart: 72 -> 48, of which waited for: 30 -> 20; matrix products, arithmetic and copies ran while one was open for 0% -> 0% of each run, Pallas kernels for 13% -> 16%
where the time goes in v2:
time: 232 us
  waiting for transfers between devices  138 us (59%)
  starting transfers between devices  50.2 us (22%)
  Pallas kernels  43.1 us (19%)
    ppermute x48, waiting for transfers between devices, send(): return lax.ppermute(block, axis, pairs)  138 us
    ppermute x48, starting transfers between devices, send(): return lax.ppermute(block, axis, pairs)  50.2 us
    pallas_call x70, Pallas kernels, kernel(): pl.pallas_call(body, out_shape=[*out_shapes, TOKEN], in_specs=[*specs, *[...  43.1 us
  transfers between devices with their start and end apart: 48, of which 20 were waited for; matrix products, arithmetic and copies ran while one was open for 0% of the time, Pallas kernels for 16%

profile of v2, /device:TPU:0, one launch (start us, length us, event | category | flops | bytes accessed | tf_op | source)
XLA Modules:
  0.0 232.1 jit_solution(13830533595077497733)
XLA Ops:
  0.0 3.2 %local_forward_0.1 = (bf16[16,64,128]{2,1,0:T(8,128)(2,1)S(1)}, bf16[16,64,128]{2,1,0:T(8,128)(2,1)S(1)}, bf16[16,64,128]{2,1,0:T(8,128)(2,1)S(1)}, bf16[16,64,1...) custom-call(bf16[4,4,16,64,128]{4,3,2,1,0:T(8,128)(2,1)} %bitcast.13, ...), custom_call_target="tpu_custom_call" | custom-call | tf_op jit(solution)/shard_map/K1_0/local_forward_0/pallas_call | solution.py:265
  12.7 2.8 %local_forward_1.1 = (bf16[16,64,128]{2,1,0:T(8,128)(2,1)S(1)}, bf16[16,64,128]{2,1,0:T(8,128)(2,1)S(1)}, bf16[16,64,128]{2,1,0:T(8,128)(2,1)S(1)}, bf16[16,64,128]{2,1,0:T(8,128)(2,1)S(1)}, f32[8,128]{1,0:T(8,128)S(1)}) custom-call(bf16[4,4,16,64,128]{4,3,2,1,0:T(8,128)(2,1)} %bitcast.16, ...), custom_call_target="tpu_custom_call", output_to_operand_aliasing={{4}: (3, {})} | custom-call | tf_op jit(solution)/shard_map/K1_1/local_forward_1/pallas_call | solution.py:265
  18.7 4.3 %collective-permute-start.8 = (bf16[16,64,128]{2,1,0:T(8,128)(2,1)S(1)}, bf16[16,64,128]{2,1,0:T(8,128)(2,1)S(1)}, u32[]{:S(2)}, u32[]{:S(2)}) collective-permute-start(bf16[16,64,128]{2,1,0:T(8,128)(2,1)S(1)} %get-tuple-element.241), channel_id=1, source_target_pairs={{0,18},{1,19},{2,16},{3,17},{4,22},{5,23},{6,20},{7,21},{8,26},{9,... | collective-permute-start | bytes 786440 | tf_op jit(solution)/shard_map/X1_0/ppermute | solution.py:282
  25.6 10.3 %collective-permute-done.8.refs_5_.refs_3_ = bf16[16,64,128]{2,1,0:T(8,128)(2,1)S(1)} collective-permute-done((bf16[16,64,128]{2,1,0:T(8,128)(2,1)S(1)}, bf16[16,64,128]{2,1,0:T(8,128)(2,1)S(1)}, u32[]{:S(2)}, u32[]{:S(2)}) %collective-permute-start.8) | collective-permute-done | bytes 262176 | tf_op jit(solution)/shard_map/X1_0/ppermute | solution.py:282
  35.9 6.4 %collective-permute-done.9.refs_1_ = bf16[16,64,128]{2,1,0:T(8,128)(2,1)S(1)} collective-permute-done((bf16[16,64,128]{2,1,0:T(8,128)(2,1)S(1)}, bf16[16,64,128]{2,1,0:T(8,128)(2,1)S(1)}, u32[]{:S(2)}, u32[]{:S(2)}) %collective-permute-start.9) | collective-permute-done | bytes 262176 | tf_op jit(solution)/shard_map/X0_1/ppermute | solution.py:282
  42.3 3.0 %collective-permute-done.10.refs_3_ = bf16[16,64,128]{2,1,0:T(8,128)(2,1)S(1)} collective-permute-done((bf16[16,64,128]{2,1,0:T(8,128)(2,1)S(1)}, bf16[16,64,128]{2,1,0:T(8,128)(2,1)S(1)}, u32[]{:S(2)}, u32[]{:S(2)}) %collective-permute-start.10) | collective-permute-done | bytes 262176 | tf_op jit(solution)/shard_map/X0_1/ppermute | solution.py:282
  49.4 4.6 %Y1_0.4 = (bf16[16,64,128]{2,1,0:T(8,128)(2,1)S(1)}, bf16[16,64,128]{2,1,0:T(8,128)(2,1)S(1)}, bf16[16,64,128]{2,1,0:T(8,128)(2,1)S(1)}, bf16[16,64,128]{2,1,0:T(8,128)(2,1)S(1)}, f32[8,128]{1,0:T(8,128)S(1)}) custom-call(bf16[256,256]{1,0:T(8,128)(2,1)S(1)} %get-tuple-element.215.b_ref, ...), custom_call_target="tpu_custom_call", output_to_operand_aliasing={{4}: (8, {})} | custom-call | tf_op jit(solution)/shard_map/Y1_0/pallas_call | solution.py:265
  56.2 6.5 %collective-permute-done.11.refs_2_.refs_3_ = bf16[16,64,128]{2,1,0:T(8,128)(2,1)S(1)} collective-permute-done((bf16[16,64,128]{2,1,0:T(8,128)(2,1)S(1)}, bf16[16,64,128]{2,1,0:T(8,128)(2,1)S(1)}, u32[]{:S(2)}, u32[]{:S(2)}) %collective-permute-start.11) | collective-permute-done | bytes 262176 | tf_op jit(solution)/shard_map/X1_1/ppermute | solution.py:282
  63.4 3.0 %collective-permute-start.18 = (bf16[16,64,128]{2,1,0:T(8,128)(2,1)S(1)}, bf16[16,64,128]{2,1,0:T(8,128)(2,1)S(1)}, u32[]{:S(2)}, u32[]{:S(2)}) collective-permute-start(bf16[16,64,128]{2,1,0:T(8,128)(2,1)S(1)} %get-tuple-element.284), channel_id=1, source_target_pairs={{0,2},{1,3},{2,0},{3,1},{4,6},{5,7},{6,4},{7,5},{8,10},{9,11},{10,... | collective-permute-start | bytes 786440 | tf_op jit(solution)/shard_map/Y1_0/ppermute | solution.py:282
  67.5 5.4 %collective-permute-done.14.refs_2_ = bf16[16,64,128]{2,1,0:T(8,128)(2,1)S(1)} collective-permute-done((bf16[16,64,128]{2,1,0:T(8,128)(2,1)S(1)}, bf16[16,64,128]{2,1,0:T(8,128)(2,1)S(1)}, u32[]{:S(2)}, u32[]{:S(2)}) %collective-permute-start.14) | collective-permute-done | bytes 262176 | tf_op jit(solution)/shard_map/X1_1/ppermute | solution.py:282
  75.1 4.7 %Y1_1.4 = (bf16[16,64,128]{2,1,0:T(8,128)(2,1)S(1)}, bf16[16,64,128]{2,1,0:T(8,128)(2,1)S(1)}, bf16[16,64,128]{2,1,0:T(8,128)(2,1)S(1)}, bf16[16,64,128]{2,1,0:T(8,128)(2,1)S(1)}, f32[8,128]{1,0:T(8,128)S(1)}) custom-call(bf16[256,256]{1,0:T(8,128)(2,1)S(1)} %get-tuple-element.215.b_ref, ...), custom_call_target="tpu_custom_call", output_to_operand_aliasing={{4}: (8, {})} | custom-call | tf_op jit(solution)/shard_map/Y1_1/pallas_call | solution.py:265
  86.6 14.7 %collective-permute-done.19.refs_2_.refs_3_ = bf16[16,64,128]{2,1,0:T(8,128)(2,1)S(1)} collective-permute-done((bf16[16,64,128]{2,1,0:T(8,128)(2,1)S(1)}, bf16[16,64,128]{2,1,0:T(8,128)(2,1)S(1)}, u32[]{:S(2)}, u32[]{:S(2)}) %collective-permute-start.19) | collective-permute-done | bytes 262176 | tf_op jit(solution)/shard_map/Y1_0/ppermute | solution.py:282
  103.6 3.4 %collective-permute-done.21.refs_2_.refs_3_ = bf16[16,64,128]{2,1,0:T(8,128)(2,1)S(1)} collective-permute-done((bf16[16,64,128]{2,1,0:T(8,128)(2,1)S(1)}, bf16[16,64,128]{2,1,0:T(8,128)(2,1)S(1)}, u32[]{:S(2)}, u32[]{:S(2)}) %collective-permute-start.21) | collective-permute-done | bytes 262176 | tf_op jit(solution)/shard_map/Y1_1/ppermute | solution.py:282
  109.6 13.9 %collective-permute-done.24.refs_2_.refs_1_ = bf16[16,64,128]{2,1,0:T(8,128)(2,1)S(1)} collective-permute-done((bf16[16,64,128]{2,1,0:T(8,128)(2,1)S(1)}, bf16[16,64,128]{2,1,0:T(8,128)(2,1)S(1)}, u32[]{:S(2)}, u32[]{:S(2)}) %collective-permute-start.24) | collective-permute-done | bytes 262176 | tf_op jit(solution)/shard_map/X1_2/ppermute | solution.py:282
  124.0 3.4 %collective-permute-start.29 = (bf16[16,64,128]{2,1,0:T(8,128)(2,1)S(1)}, bf16[16,64,128]{2,1,0:T(8,128)(2,1)S(1)}, u32[]{:S(2)}, u32[]{:S(2)}) collective-permute-start(bf16[16,64,128]{2,1,0:T(8,128)(2,1)S(1)} %get-tuple-element.329), channel_id=1, source_target_pairs={{0,18},{1,19},{2,16},{3,17},{4,22},{5,23},{6,20},{7,21},{8,26},{9,... | collective-permute-start | bytes 786440 | tf_op jit(solution)/shard_map/X1_3/ppermute | solution.py:282
  129.5 4.6 %Y1_2.4 = (bf16[16,64,128]{2,1,0:T(8,128)(2,1)S(1)}, bf16[16,64,128]{2,1,0:T(8,128)(2,1)S(1)}, bf16[16,64,128]{2,1,0:T(8,128)(2,1)S(1)}, bf16[16,64,128]{2,1,0:T(8,128)(2,1)S(1)}, f32[8,128]{1,0:T(8,128)S(1)}) custom-call(bf16[256,256]{1,0:T(8,128)(2,1)S(1)} %get-tuple-element.215.b_ref, ...), custom_call_target="tpu_custom_call", output_to_operand_aliasing={{4}: (8, {})} | custom-call | tf_op jit(solution)/shard_map/Y1_2/pallas_call | solution.py:265
  137.7 13.8 %collective-permute-done.25.refs_1_ = bf16[16,64,128]{2,1,0:T(8,128)(2,1)S(1)} collective-permute-done((bf16[16,64,128]{2,1,0:T(8,128)(2,1)S(1)}, bf16[16,64,128]{2,1,0:T(8,128)(2,1)S(1)}, u32[]{:S(2)}, u32[]{:S(2)}) %collective-permute-start.25) | collective-permute-done | bytes 262176 | tf_op jit(solution)/shard_map/Y1_1/ppermute | solution.py:282
  152.0 5.5 %collective-permute-done.29.refs_2_.refs_3_ = bf16[16,64,128]{2,1,0:T(8,128)(2,1)S(1)} collective-permute-done((bf16[16,64,128]{2,1,0:T(8,128)(2,1)S(1)}, bf16[16,64,128]{2,1,0:T(8,128)(2,1)S(1)}, u32[]{:S(2)}, u32[]{:S(2)}) %collective-permute-start.29) | collective-permute-done | bytes 262176 | tf_op jit(solution)/shard_map/X1_3/ppermute | solution.py:282
  159.2 9.7 %collective-permute-done.33.refs_2_.refs_3_ = bf16[16,64,128]{2,1,0:T(8,128)(2,1)S(1)} collective-permute-done((bf16[16,64,128]{2,1,0:T(8,128)(2,1)S(1)}, bf16[16,64,128]{2,1,0:T(8,128)(2,1)S(1)}, u32[]{:S(2)}, u32[]{:S(2)}) %collective-permute-start.33) | collective-permute-done | bytes 262176 | tf_op jit(solution)/shard_map/Y1_2/ppermute | solution.py:282
  174.1 4.8 %Y1_3.4 = (bf16[16,64,128]{2,1,0:T(8,128)(2,1)S(1)}, bf16[16,64,128]{2,1,0:T(8,128)(2,1)S(1)}, bf16[16,64,128]{2,1,0:T(8,128)(2,1)S(1)}, bf16[16,64,128]{2,1,0:T(8,128)(2,1)S(1)}, f32[8,128]{1,0:T(8,128)S(1)}) custom-call(bf16[256,256]{1,0:T(8,128)(2,1)S(1)} %get-tuple-element.215.b_ref, ...), custom_call_target="tpu_custom_call", output_to_operand_aliasing={{4}: (8, {})} | custom-call | tf_op jit(solution)/shard_map/Y1_3/pallas_call | solution.py:265
  187.5 14.0 %collective-permute-done.37.refs_1_ = bf16[16,64,128]{2,1,0:T(8,128)(2,1)S(1)} collective-permute-done((bf16[16,64,128]{2,1,0:T(8,128)(2,1)S(1)}, bf16[16,64,128]{2,1,0:T(8,128)(2,1)S(1)}, u32[]{:S(2)}, u32[]{:S(2)}) %collective-permute-start.37) | collective-permute-done | bytes 262176 | tf_op jit(solution)/shard_map/Y1_3/ppermute | solution.py:282
  201.5 6.1 %collective-permute-done.39.refs_3_ = bf16[16,64,128]{2,1,0:T(8,128)(2,1)S(1)} collective-permute-done((bf16[16,64,128]{2,1,0:T(8,128)(2,1)S(1)}, bf16[16,64,128]{2,1,0:T(8,128)(2,1)S(1)}, u32[]{:S(2)}, u32[]{:S(2)}) %collective-permute-start.39) | collective-permute-done | bytes 262176 | tf_op jit(solution)/shard_map/Y1_3/ppermute | solution.py:282
  212.2 11.8 %collective-permute-done.47.refs_3_ = bf16[16,64,128]{2,1,0:T(8,128)(2,1)S(1)} collective-permute-done((bf16[16,64,128]{2,1,0:T(8,128)(2,1)S(1)}, bf16[16,64,128]{2,1,0:T(8,128)(2,1)S(1)}, u32[]{:S(2)}, u32[]{:S(2)}) %collective-permute-start.47) | collective-permute-done | bytes 262176 | tf_op jit(solution)/shard_map/Y0_2/ppermute | solution.py:282
  226.0 3.9 %collective-permute-done.43.refs_1_ = bf16[16,64,128]{2,1,0:T(8,128)(2,1)S(1)} collective-permute-done((bf16[16,64,128]{2,1,0:T(8,128)(2,1)S(1)}, bf16[16,64,128]{2,1,0:T(8,128)(2,1)S(1)}, u32[]{:S(2)}, u32[]{:S(2)}) %collective-permute-start.43) | collective-permute-done | bytes 262176 | tf_op jit(solution)/shard_map/Y0_3/ppermute | solution.py:282
  (150 shorter events, 67.7 us)
Async XLA Ops:
  23.1 19.2 %collective-permute-start.9 = (bf16[16,64,128]{2,1,0:T(8,128)(2,1)S(1)}, bf16[16,64,128]{2,1,0:T(8,128)(2,1)S(1)}, u32[]{:S(2)}, u32[]{:S(2)}) collective-permute-start(bf16[16,64,128]{2,1,0:T(8,128)(2,1)S(1)} %get-tuple-element.244), channel_id=1, source_target_pairs={{0,1},{1,0},{2,3},{3,2},{4,5},{5,4},{6,7},{7,6},{8,9},{9,8},{10,11... | collective-permute-start | bytes 786440 | tf_op jit(solution)/shard_map/X0_1/ppermute | solution.py:282
  24.6 20.7 %collective-permute-start.10 = (bf16[16,64,128]{2,1,0:T(8,128)(2,1)S(1)}, bf16[16,64,128]{2,1,0:T(8,128)(2,1)S(1)}, u32[]{:S(2)}, u32[]{:S(2)}) collective-permute-start(bf16[16,64,128]{2,1,0:T(8,128)(2,1)S(1)} %get-tuple-element.245), channel_id=1, source_target_pairs={{0,5},{1,4},{2,7},{3,6},{4,1},{5,0},{6,3},{7,2},{8,13},{9,12},{10,... | collective-permute-start | bytes 786440 | tf_op jit(solution)/shard_map/X0_1/ppermute | solution.py:282
  24.7 24.7 %collective-permute-start.7 = (bf16[16,64,128]{2,1,0:T(8,128)(2,1)S(1)}, bf16[16,64,128]{2,1,0:T(8,128)(2,1)S(1)}, u32[]{:S(2)}, u32[]{:S(2)}) collective-permute-start(bf16[16,64,128]{2,1,0:T(8,128)(2,1)S(1)} %get-tuple-element.240), channel_id=1, source_target_pairs={{0,16},{4,20},{8,24},{12,28},{16,0},{20,4},{24,8},{28,12},{1,17},{... | collective-permute-start | bytes 786440 | tf_op jit(solution)/shard_map/X1_0/ppermute | solution.py:282
  25.2 24.1 %collective-permute-start.6 = (bf16[16,64,128]{2,1,0:T(8,128)(2,1)S(1)}, bf16[16,64,128]{2,1,0:T(8,128)(2,1)S(1)}, u32[]{:S(2)}, u32[]{:S(2)}) collective-permute-start(bf16[16,64,128]{2,1,0:T(8,128)(2,1)S(1)} %get-tuple-element.239), channel_id=1, source_target_pairs={{0,2},{1,3},{2,0},{3,1},{4,6},{5,7},{6,4},{7,5},{8,10},{9,11},{10,... | collective-permute-start | bytes 786440 | tf_op jit(solution)/shard_map/X1_0/ppermute | solution.py:282
  63.3 21.9 %collective-permute-start.16 = (bf16[16,64,128]{2,1,0:T(8,128)(2,1)S(1)}, bf16[16,64,128]{2,1,0:T(8,128)(2,1)S(1)}, u32[]{:S(2)}, u32[]{:S(2)}) collective-permute-start(bf16[16,64,128]{2,1,0:T(8,128)(2,1)S(1)} %get-tuple-element.276), channel_id=1, source_target_pairs={{0,5},{1,4},{2,7},{3,6},{4,1},{5,0},{6,3},{7,2},{8,13},{9,12},{10,... | collective-permute-start | bytes 786440 | tf_op jit(solution)/shard_map/X0_2/ppermute | solution.py:282
  63.4 20.7 %collective-permute-start.18 = (bf16[16,64,128]{2,1,0:T(8,128)(2,1)S(1)}, bf16[16,64,128]{2,1,0:T(8,128)(2,1)S(1)}, u32[]{:S(2)}, u32[]{:S(2)}) collective-permute-start(bf16[16,64,128]{2,1,0:T(8,128)(2,1)S(1)} %get-tuple-element.284), channel_id=1, source_target_pairs={{0,2},{1,3},{2,0},{3,1},{4,6},{5,7},{6,4},{7,5},{8,10},{9,11},{10,... | collective-permute-start | bytes 786440 | tf_op jit(solution)/shard_map/Y1_0/ppermute | solution.py:282
  72.9 28.4 %collective-permute-start.15 = (bf16[16,64,128]{2,1,0:T(8,128)(2,1)S(1)}, bf16[16,64,128]{2,1,0:T(8,128)(2,1)S(1)}, u32[]{:S(2)}, u32[]{:S(2)}) collective-permute-start(bf16[16,64,128]{2,1,0:T(8,128)(2,1)S(1)} %get-tuple-element.273), channel_id=1, source_target_pairs={{0,1},{1,0},{2,3},{3,2},{4,5},{5,4},{6,7},{7,6},{8,9},{9,8},{10,11... | collective-permute-start | bytes 786440 | tf_op jit(solution)/shard_map/X0_3/ppermute | solution.py:282
  72.9 28.4 %collective-permute-start.19 = (bf16[16,64,128]{2,1,0:T(8,128)(2,1)S(1)}, bf16[16,64,128]{2,1,0:T(8,128)(2,1)S(1)}, u32[]{:S(2)}, u32[]{:S(2)}) collective-permute-start(bf16[16,64,128]{2,1,0:T(8,128)(2,1)S(1)} %get-tuple-element.290), channel_id=1, source_target_pairs={{0,18},{1,19},{2,16},{3,17},{4,22},{5,23},{6,20},{7,21},{8,26},{9,... | collective-permute-start | bytes 786440 | tf_op jit(solution)/shard_map/Y1_0/ppermute | solution.py:282
  79.8 27.2 %collective-permute-start.21 = (bf16[16,64,128]{2,1,0:T(8,128)(2,1)S(1)}, bf16[16,64,128]{2,1,0:T(8,128)(2,1)S(1)}, u32[]{:S(2)}, u32[]{:S(2)}) collective-permute-start(bf16[16,64,128]{2,1,0:T(8,128)(2,1)S(1)} %get-tuple-element.300), channel_id=1, source_target_pairs={{0,18},{1,19},{2,16},{3,17},{4,22},{5,23},{6,20},{7,21},{8,26},{9,... | collective-permute-start | bytes 786440 | tf_op jit(solution)/shard_map/Y1_1/ppermute | solution.py:282
  84.0 23.0 %collective-permute-start.22 = (bf16[16,64,128]{2,1,0:T(8,128)(2,1)S(1)}, bf16[16,64,128]{2,1,0:T(8,128)(2,1)S(1)}, u32[]{:S(2)}, u32[]{:S(2)}) collective-permute-start(bf16[16,64,128]{2,1,0:T(8,128)(2,1)S(1)} %get-tuple-element.302), channel_id=1, source_target_pairs={{0,16},{4,20},{8,24},{12,28},{16,0},{20,4},{24,8},{28,12},{1,17},{... | collective-permute-start | bytes 786440 | tf_op jit(solution)/shard_map/Y1_1/ppermute | solution.py:282
  85.7 23.9 %collective-permute-start.23 = (bf16[16,64,128]{2,1,0:T(8,128)(2,1)S(1)}, bf16[16,64,128]{2,1,0:T(8,128)(2,1)S(1)}, u32[]{:S(2)}, u32[]{:S(2)}) collective-permute-start(bf16[16,64,128]{2,1,0:T(8,128)(2,1)S(1)} %get-tuple-element.304), channel_id=1, source_target_pairs={{0,16},{4,20},{8,24},{12,28},{16,0},{20,4},{24,8},{28,12},{1,17},{... | collective-permute-start | bytes 786440 | tf_op jit(solution)/shard_map/X1_2/ppermute | solution.py:282
  101.3 22.2 %collective-permute-start.20 = (bf16[16,64,128]{2,1,0:T(8,128)(2,1)S(1)}, bf16[16,64,128]{2,1,0:T(8,128)(2,1)S(1)}, u32[]{:S(2)}, u32[]{:S(2)}) collective-permute-start(bf16[16,64,128]{2,1,0:T(8,128)(2,1)S(1)} %get-tuple-element.292), channel_id=1, source_target_pairs={{0,5},{1,4},{2,7},{3,6},{4,1},{5,0},{6,3},{7,2},{8,13},{9,12},{10,... | collective-permute-start | bytes 786440 | tf_op jit(solution)/shard_map/X0_3/ppermute | solution.py:282
  101.3 22.2 %collective-permute-start.24 = (bf16[16,64,128]{2,1,0:T(8,128)(2,1)S(1)}, bf16[16,64,128]{2,1,0:T(8,128)(2,1)S(1)}, u32[]{:S(2)}, u32[]{:S(2)}) collective-permute-start(bf16[16,64,128]{2,1,0:T(8,128)(2,1)S(1)} %get-tuple-element.306), channel_id=1, source_target_pairs={{0,2},{1,3},{2,0},{3,1},{4,6},{5,7},{6,4},{7,5},{8,10},{9,11},{10,... | collective-permute-start | bytes 786440 | tf_op jit(solution)/shard_map/X1_2/ppermute | solution.py:282
  107.0 22.5 %collective-permute-start.26 = (bf16[16,64,128]{2,1,0:T(8,128)(2,1)S(1)}, bf16[16,64,128]{2,1,0:T(8,128)(2,1)S(1)}, u32[]{:S(2)}, u32[]{:S(2)}) collective-permute-start(bf16[16,64,128]{2,1,0:T(8,128)(2,1)S(1)} %get-tuple-element.315), channel_id=1, source_target_pairs={{0,18},{1,19},{2,16},{3,17},{4,22},{5,23},{6,20},{7,21},{8,26},{9,... | collective-permute-start | bytes 786440 | tf_op jit(solution)/shard_map/X1_2/ppermute | solution.py:282
  107.0 27.0 %collective-permute-start.27 = (bf16[16,64,128]{2,1,0:T(8,128)(2,1)S(1)}, bf16[16,64,128]{2,1,0:T(8,128)(2,1)S(1)}, u32[]{:S(2)}, u32[]{:S(2)}) collective-permute-start(bf16[16,64,128]{2,1,0:T(8,128)(2,1)S(1)} %get-tuple-element.322), channel_id=1, source_target_pairs={{0,1},{1,0},{2,3},{3,2},{4,5},{5,4},{6,7},{7,6},{8,9},{9,8},{10,11... | collective-permute-start | bytes 786440 | tf_op jit(solution)/shard_map/Y0_0/ppermute | solution.py:282
  109.6 28.0 %collective-permute-start.28 = (bf16[16,64,128]{2,1,0:T(8,128)(2,1)S(1)}, bf16[16,64,128]{2,1,0:T(8,128)(2,1)S(1)}, u32[]{:S(2)}, u32[]{:S(2)}) collective-permute-start(bf16[16,64,128]{2,1,0:T(8,128)(2,1)S(1)} %get-tuple-element.324), channel_id=1, source_target_pairs={{0,5},{1,4},{2,7},{3,6},{4,1},{5,0},{6,3},{7,2},{8,13},{9,12},{10,... | collective-permute-start | bytes 786440 | tf_op jit(solution)/shard_map/Y0_0/ppermute | solution.py:282
  123.5 28.0 %collective-permute-start.25 = (bf16[16,64,128]{2,1,0:T(8,128)(2,1)S(1)}, bf16[16,64,128]{2,1,0:T(8,128)(2,1)S(1)}, u32[]{:S(2)}, u32[]{:S(2)}) collective-permute-start(bf16[16,64,128]{2,1,0:T(8,128)(2,1)S(1)} %get-tuple-element.311), channel_id=1, source_target_pairs={{0,2},{1,3},{2,0},{3,1},{4,6},{5,7},{6,4},{7,5},{8,10},{9,11},{10,... | collective-permute-start | bytes 786440 | tf_op jit(solution)/shard_map/Y1_1/ppermute | solution.py:282
  124.0 33.6 %collective-permute-start.29 = (bf16[16,64,128]{2,1,0:T(8,128)(2,1)S(1)}, bf16[16,64,128]{2,1,0:T(8,128)(2,1)S(1)}, u32[]{:S(2)}, u32[]{:S(2)}) collective-permute-start(bf16[16,64,128]{2,1,0:T(8,128)(2,1)S(1)} %get-tuple-element.329), channel_id=1, source_target_pairs={{0,18},{1,19},{2,16},{3,17},{4,22},{5,23},{6,20},{7,21},{8,26},{9,... | collective-permute-start | bytes 786440 | tf_op jit(solution)/shard_map/X1_3/ppermute | solution.py:282
  134.1 34.8 %collective-permute-start.31 = (bf16[16,64,128]{2,1,0:T(8,128)(2,1)S(1)}, bf16[16,64,128]{2,1,0:T(8,128)(2,1)S(1)}, u32[]{:S(2)}, u32[]{:S(2)}) collective-permute-start(bf16[16,64,128]{2,1,0:T(8,128)(2,1)S(1)} %get-tuple-element.331), channel_id=1, source_target_pairs={{0,16},{4,20},{8,24},{12,28},{16,0},{20,4},{24,8},{28,12},{1,17},{... | collective-permute-start | bytes 786440 | tf_op jit(solution)/shard_map/X1_3/ppermute | solution.py:282
  135.2 33.6 %collective-permute-start.33 = (bf16[16,64,128]{2,1,0:T(8,128)(2,1)S(1)}, bf16[16,64,128]{2,1,0:T(8,128)(2,1)S(1)}, u32[]{:S(2)}, u32[]{:S(2)}) collective-permute-start(bf16[16,64,128]{2,1,0:T(8,128)(2,1)S(1)} %get-tuple-element.339), channel_id=1, source_target_pairs={{0,18},{1,19},{2,16},{3,17},{4,22},{5,23},{6,20},{7,21},{8,26},{9,... | collective-permute-start | bytes 786440 | tf_op jit(solution)/shard_map/Y1_2/ppermute | solution.py:282
  137.6 32.5 %collective-permute-start.32 = (bf16[16,64,128]{2,1,0:T(8,128)(2,1)S(1)}, bf16[16,64,128]{2,1,0:T(8,128)(2,1)S(1)}, u32[]{:S(2)}, u32[]{:S(2)}) collective-permute-start(bf16[16,64,128]{2,1,0:T(8,128)(2,1)S(1)} %get-tuple-element.333), channel_id=1, source_target_pairs={{0,4},{4,0},{8,12},{12,8},{16,20},{20,16},{24,28},{28,24},{1,5},{5... | collective-permute-start | bytes 786440 | tf_op jit(solution)/shard_map/Y0_0/ppermute | solution.py:282
  180.1 21.4 %collective-permute-start.37 = (bf16[16,64,128]{2,1,0:T(8,128)(2,1)S(1)}, bf16[16,64,128]{2,1,0:T(8,128)(2,1)S(1)}, u32[]{:S(2)}, u32[]{:S(2)}) collective-permute-start(bf16[16,64,128]{2,1,0:T(8,128)(2,1)S(1)} %get-tuple-element.355), channel_id=1, source_target_pairs={{0,2},{1,3},{2,0},{3,1},{4,6},{5,7},{6,4},{7,5},{8,10},{9,11},{10,... | collective-permute-start | bytes 786440 | tf_op jit(solution)/shard_map/Y1_3/ppermute | solution.py:282
  180.9 26.7 %collective-permute-start.39 = (bf16[16,64,128]{2,1,0:T(8,128)(2,1)S(1)}, bf16[16,64,128]{2,1,0:T(8,128)(2,1)S(1)}, u32[]{:S(2)}, u32[]{:S(2)}) collective-permute-start(bf16[16,64,128]{2,1,0:T(8,128)(2,1)S(1)} %get-tuple-element.357), channel_id=1, source_target_pairs={{0,18},{1,19},{2,16},{3,17},{4,22},{5,23},{6,20},{7,21},{8,26},{9,... | collective-permute-start | bytes 786440 | tf_op jit(solution)/shard_map/Y1_3/ppermute | solution.py:282
  185.9 25.9 %collective-permute-start.42 = (bf16[16,64,128]{2,1,0:T(8,128)(2,1)S(1)}, bf16[16,64,128]{2,1,0:T(8,128)(2,1)S(1)}, u32[]{:S(2)}, u32[]{:S(2)}) collective-permute-start(bf16[16,64,128]{2,1,0:T(8,128)(2,1)S(1)} %get-tuple-element.379), channel_id=1, source_target_pairs={{0,1},{1,0},{2,3},{3,2},{4,5},{5,4},{6,7},{7,6},{8,9},{9,8},{10,11... | collective-permute-start | bytes 786440 | tf_op jit(solution)/shard_map/Y0_2/ppermute | solution.py:282
  (28 other events, 347.3 us)

commit v3 on v2

--- a/solution.py
+++ b/solution.py
@@ -8,29 +8,35 @@
 from jax.experimental.pallas import tpu as pltpu
 from jax.sharding import PartitionSpec as P
 
-PIECES = ((16,), (16,), (16,), (16,))
+X_PIECES = ((16,), (16,), (16,), (16,))
+Y_PIECES = ((16,), (16,), (16,), (8, 8))
 ACTIONS = (
-    ".K10_", "+X00d", "+X00x", "+X00z", ".K13_", "+X03x", ".K12_", "+X02x", ".K11_", ".PM0_",
-    "-X00d", "+X01x", "-X00x", "+X01z", "-X00z", ".X10_", "+X10d", "-X03x", "+X01d", "-X02x",
-    "+X10x", "-X01x", "+X10z", "-X01z", "-X10d", "-X01d", ".X11_", "+X11d", "+X02z", "-X10x",
-    "-X10z", ".Y10_", "+Y10x", "+X11x", "+X11z", "-X11d", "+Y10z", "-X02z", "+X02d", ".PA0_",
-    "-Y10x", "+Y10d", "-X11x", "+X03z", "-X11z", ".Y11_", "+Y11d", "-Y10z", "+Y11x", "-X02d",
-    ".X12_", "+X12x", "-Y10d", "+X12z", "-X03z", "+X03d", ".Y00_", "-Y11d", "+X12d", "-Y11x",
-    "+Y00z", "-X12x", "+Y00d", "-X12z", "+Y11z", "-X03d", ".X13_", "+X13d", "-X12d", ".Y12_",
-    "+Y12d", "-Y00z", "+X13x", "-Y00d", "+Y00x", "-Y11z", ".Y01_", "+Y01d", "-X13d", "+X13z",
-    "-Y12d", "+Y01x", "-X13x", "+Y12x", "-Y00x", "+Y01z", "-Y01d", "+Y12z", ".K50_", "-X13z",
-    ".Y13_", "+Y13x", "-Y01x", "+Y13d", "-Y12x", "+Y13z", "-Y01z", ".K51_", "-Y12z", ".Y02_",
-    "+Y02z", "+Y02d", "-Y13x", "+Y02x", "-Y13d", "-Y13z", ".Y03_", "+Y03d", "+Y03x", "-Y02z",
-    "+Y03z", "-Y02d", "-Y02x", ".K52_", "-Y03d", "-Y03x", "-Y03z", ".K53_",
+    ".K10_", "+X00z", ".K13_", "+X03x", "+X00d", ".K11_", "+X01x", "+X00x", ".PM0_", ".K12_",
+    "-X00z", "+X01d", "-X03x", "+X01z", "-X00d", "-X01x", "-X00x", ".X10_", "+X10d", "+X10x",
+    "+X10z", "-X01d", "-X01z", ".X11_", "+X11x", "+X02d", "-X10d", "+X11z", "-X10x", "+X02x",
+    ".PA0_", "-X10z", "+X02z", "-X11x", "+X11d", ".Y10_", "-X02d", "+Y10z", "-X11z", "+X03z",
+    "-X02x", "+X03d", "-X02z", ".X12_", "+X12d", "-X11d", "+Y10x", ".Y11_", "-Y10z", "+X12z",
+    "-X03z", "+Y11d", "-X03d", "+Y10d", "-X12d", "+Y11x", ".X13_", "-Y10x", "+X13z", "-X12z",
+    "+X12x", "-Y11d", "+Y11z", "-Y10d", "+X13x", ".Y00_", "-Y11x", "+Y00d", "-X13z", "+X13d",
+    "-X12x", "+Y00z", ".Y12_", "-Y11z", "+Y12x", "-X13x", "+Y12z", ".Y01_", "-Y00d", "+Y01d",
+    "-X13d", ".Y13_", "+Y13x", "-Y00z", "+Y12d", "-Y12x", "+Y01z", ".Y14_", "-Y12z", "+Y01x",
+    "-Y01d", "+Y14z", "-Y13x", "+Y14x", "-Y12d", ".Y02_", "+Y02d", "-Y01z", "+Y13z", "-Y01x",
+    "+Y14d", "-Y14z", "+Y02z", "-Y14x", "+Y13d", ".K51_", "-Y02d", "-Y13z", "-Y14d", ".Y04_",
+    "+Y04z", "+Y00x", "+Y02x", "-Y02z", "+Y04d", "-Y13d", ".Y03_", "+Y03d", "-Y04z", "+Y04x",
+    "-Y00x", "+Y03z", "-Y02x", "+Y03x", ".K50_", ".K52_", "-Y04d", "-Y03d", "-Y04x", "-Y03z",
+    "-Y03x", ".K53_",
 )
 VMEM_GRANT = 16 * 2**20
 TOKEN = jax.ShapeDtypeStruct((8, 128), jnp.float32)
-ROOT2 = float(np.sqrt(2.0))
-QUARTER_PI = float(np.pi / 4)
-INV_PI = float(1.0 / np.pi)
-PI_HIGH = 3.140625
-PI_MID = float(np.float32(np.pi - 3.140625))
-PI_LOW = float(np.pi - 3.140625 - float(np.float32(np.pi - 3.140625)))
+QUARTER_PI, HALF_PI = float(np.pi / 4), float(np.pi / 2)
+SINE = (
+    -1.4142135381698608,
+    0.23570221662521362,
+    -0.011785031296312809,
+    0.00028053473215550184,
+    -3.875064521707827e-06,
+    3.182795182965492e-08,
+)
 
 
 def level_bit(axis_count, level_index, depth):
@@ -43,16 +49,12 @@
 
 
 def cas(angle):
-    turns = jnp.floor(angle * INV_PI + 0.75)
-    rest = ((angle - turns * PI_HIGH) - turns * PI_MID) - turns * PI_LOW + QUARTER_PI
+    rest = jnp.abs(angle - QUARTER_PI) - HALF_PI
     square = rest * rest
-    poly = jnp.float32(-2.5052108e-8)
-    for c in (2.7557319e-6, -1.9841270e-4, 8.3333333e-3, -1.6666667e-1, 1.0):
+    poly = jnp.float32(SINE[-1])
+    for c in SINE[-2::-1]:
         poly = poly * square + jnp.float32(c)
-    half = turns * 0.5
-    odd = half - jnp.floor(half)
-    sign = ROOT2 - (4.0 * ROOT2) * odd
-    return poly * rest * sign
+    return poly * rest
 
 
 def stacked(columns):
@@ -193,11 +195,11 @@
                 outs[d][i + j] = tile(y, d, j, r, n)
 
 
-def residual_kernel(start, b_ref, bt_ref, phases_ref, observed_ref, *refs):
-    ins, outs, (angles, data, sems) = refs[:4], refs[-8:-4], refs[-3:]
-    size, r, n = ins[0].shape
+def residual_kernel(start, sources, b_ref, bt_ref, phases_ref, observed_ref, *refs):
+    outs, (angles, data, sems) = refs[-8:-4], refs[-3:]
+    r, n = outs[0].shape[1:]
     copies = []
-    for i in range(size // 4):
+    for i in range(len(sources)):
         here, there = pl.ds(4 * i, 4), pl.ds(start + 4 * i, 4)
         copies.append(
             (
@@ -207,8 +209,9 @@
         )
         for copy in copies[-1]:
             copy.start()
-    for i in range(size // 4):
-        x = stacked([[ref[4 * i + j] for j in range(4)] for ref in ins])
+    for i, (source, first) in enumerate(sources):
+        ins = refs[4 * source : 4 * source + 4]
+        x = stacked([[ref[first + j] for j in range(4)] for ref in ins])
         predicted = dot(b_ref[...], x)
         for copy in copies[i]:
             copy.wait()
@@ -234,7 +237,7 @@
 
 
 KERNEL_COST = pl.CostEstimate(flops=0, bytes_accessed=0, transcendentals=0)
-GATE_COST = pl.CostEstimate(flops=10**9, bytes_accessed=1, transcendentals=0)
+GATE_COST = pl.CostEstimate(flops=1000000000, bytes_accessed=1, transcendentals=0)
 
 
 class Chain:
@@ -277,7 +280,8 @@
 
     def send(self, block, level, d):
         shape = jax.ShapeDtypeStruct(block.shape, block.dtype)
-        (block,) = self.kernel(gate_kernel, [block], [ANY], [shape], [ANY], {0: 0}, True)
+        with jax.named_scope("gate_mark"):
+            (block,) = self.kernel(gate_kernel, [block], [ANY], [shape], [ANY], {0: 0}, True)
         axis, pairs = self.pairs[level][d]
         return lax.ppermute(block, axis, pairs)
 
@@ -285,11 +289,10 @@
 def local(image_tiles, observed, phases, interpolate, local_weights, merge_weights, output_weight):
     groups, r, n = image_tiles.shape[2:]
     depth = merge_weights.shape[2]
-    chunks = len(PIECES)
+    chunks = len(X_PIECES)
     quarter = groups // 4
     chunk = quarter // chunks
     bf16 = jnp.bfloat16
-    box = r * n * 2
 
     masks = []
     for level in range(depth):
@@ -312,7 +315,7 @@
         return [jax.ShapeDtypeStruct((size, r, n), bf16)] * 4
 
     def forward_local(index):
-        sizes = PIECES[index]
+        sizes = X_PIECES[index]
         first = not prepared
         weights = [levels, inner] if first else list(prepared["local"])
         scratch = [pltpu.VMEM((4, chunk, r, n), bf16), pltpu.SemaphoreType.DMA((6,))]
@@ -331,7 +334,7 @@
         if first:
             prepared["local"] = outs[-2:]
         for piece in range(len(sizes)):
-            ready["X0", first_piece[index] + piece] = outs[4 * piece : 4 * piece + 4]
+            ready["X0", x_first[index] + piece] = outs[4 * piece : 4 * piece + 4]
 
     def prepare_merges():
         with jax.named_scope("prep_merge"):
@@ -363,12 +366,20 @@
             [VMEM] * 4,
         )
 
-    def through_data(blocks, start):
-        size = blocks[0].shape[0]
+    def through_data(number):
+        start, size = y_starts[number], y_sizes[number]
+        inside = [
+            p for p, (a, m) in enumerate(zip(x_starts, x_sizes)) if a < start + size and start < a + m
+        ]
+        sources = []
+        for box in range(start, start + size, 4):
+            k = [i for i, p in enumerate(inside) if 0 <= box - x_starts[p] < x_sizes[p]][0]
+            sources.append((k, box - x_starts[inside[k]]))
+        blocks = sum([state["X1", p] for p in inside], [])
         return chain.kernel(
-            functools.partial(residual_kernel, start),
+            functools.partial(residual_kernel, start, sources),
             [*prepared["merge"][2:], phase4, observed4, *blocks],
-            [VMEM, VMEM, HBM, HBM] + [VMEM] * 4,
+            [VMEM, VMEM, HBM, HBM] + [VMEM] * len(blocks),
             shapes(size),
             [VMEM] * 4,
             scratch_shapes=[
@@ -379,8 +390,8 @@
         )
 
     def adjoint_local(index):
-        sizes = PIECES[index]
-        blocks = sum([state["Y0", first_piece[index] + i] for i in range(len(sizes))], [])
+        sizes = Y_PIECES[index]
+        blocks = sum([state["Y0", y_first[index] + i] for i in range(len(sizes))], [])
         operands = [*prepared["adjoint"], *blocks]
         specs = [VMEM] * len(operands)
         aliases = {}
@@ -402,9 +413,11 @@
                 ],
             )
 
-    all_sizes = sum(PIECES, ())
-    starts = [sum(all_sizes[:i]) for i in range(len(all_sizes))]
-    first_piece = [sum(len(p) for p in PIECES[:i]) for i in range(chunks)]
+    x_sizes, y_sizes = sum(X_PIECES, ()), sum(Y_PIECES, ())
+    x_starts = [sum(x_sizes[:i]) for i in range(len(x_sizes))]
+    y_starts = [sum(y_sizes[:i]) for i in range(len(y_sizes))]
+    x_first = [sum(len(p) for p in X_PIECES[:i]) for i in range(chunks)]
+    y_first = [sum(len(p) for p in Y_PIECES[:i]) for i in range(chunks)]
     prepared, ready, state = {}, {}, {}
 
     for action in ACTIONS:
@@ -420,7 +433,7 @@
                 elif name == "X1":
                     ready["X1", number] = merge(prepared["merge"][0], state["X0", number])
                 elif name == "Y1":
-                    ready["Y1", number] = through_data(state["X1", number], starts[number])
+                    ready["Y1", number] = through_data(number)
                 elif name == "Y0":
                     ready["Y0", number] = merge(prepared["merge"][1], state["Y1", number])
                 else:

time: 232 us -> 224 us (0.966)
  waiting for transfers between devices: 138 us -> 129 us
  Pallas kernels: 43.1 us -> 40.6 us
    ppermute x48 -> x54, waiting for transfers between devices: 138 us -> 129 us  [send(): return lax.ppermute(block, axis, pairs)]
    pallas_call x70 -> x78, Pallas kernels: 43.1 us -> 40.6 us  [kernel(): pl.pallas_call(body, out_shape=[*out_shapes, TOKEN], in_specs=[*specs, *[...]
    ppermute x48 -> x54, starting transfers between devices: 50.2 us -> 52.2 us  [send(): return lax.ppermute(block, axis, pairs)]
  transfers between devices with their start and end apart: 48 -> 54, of which waited for: 20 -> 25; matrix products, arithmetic and copies ran while one was open for 0% -> 0% of each run, Pallas kernels for 16% -> 16%
where the time goes in v3:
time: 224 us
  waiting for transfers between devices  129 us (58%)
  starting transfers between devices  52.2 us (23%)
  Pallas kernels  40.6 us (18%)
    ppermute x54, waiting for transfers between devices, send(): return lax.ppermute(block, axis, pairs)  129 us
    ppermute x54, starting transfers between devices, send(): return lax.ppermute(block, axis, pairs)  52.2 us
    pallas_call x78, Pallas kernels, kernel(): pl.pallas_call(body, out_shape=[*out_shapes, TOKEN], in_specs=[*specs, *[...  40.6 us
  transfers between devices with their start and end apart: 54, of which 25 were waited for; matrix products, arithmetic and copies ran while one was open for 0% of the time, Pallas kernels for 16%

profile of v3, /device:TPU:0, one launch (start us, length us, event | category | flops | bytes accessed | tf_op | source)
XLA Modules:
  0.0 224.0 jit_solution(16308332553544420743)
XLA Ops:
  21.2 3.6 %collective-permute-start.7 = (bf16[16,64,128]{2,1,0:T(8,128)(2,1)S(1)}, bf16[16,64,128]{2,1,0:T(8,128)(2,1)S(1)}, u32[]{:S(2)}, u32[]{:S(2)}) collective-permute-start(bf16[16,64,128]{2,1,0:T(8,128)(2,1)S(1)} %get-tuple-element.265), channel_id=1, source_target_pairs={{0,18},{1,19},{2,16},{3,17},{4,22},{5,23},{6,20},{7,21},{8,26},{9,... | collective-permute-start | bytes 786440 | tf_op jit(solution)/shard_map/X1_0/ppermute | solution.py:286
  25.7 9.7 %collective-permute-done.2.refs_1_ = bf16[16,64,128]{2,1,0:T(8,128)(2,1)S(1)} collective-permute-done((bf16[16,64,128]{2,1,0:T(8,128)(2,1)S(1)}, bf16[16,64,128]{2,1,0:T(8,128)(2,1)S(1)}, u32[]{:S(2)}, u32[]{:S(2)}) %collective-permute-start.2) | collective-permute-done | bytes 262176 | tf_op jit(solution)/shard_map/X0_1/ppermute | solution.py:286
  35.4 4.5 %collective-permute-done.4.refs_3_ = bf16[16,64,128]{2,1,0:T(8,128)(2,1)S(1)} collective-permute-done((bf16[16,64,128]{2,1,0:T(8,128)(2,1)S(1)}, bf16[16,64,128]{2,1,0:T(8,128)(2,1)S(1)}, u32[]{:S(2)}, u32[]{:S(2)}) %collective-permute-start.4) | collective-permute-done | bytes 262176 | tf_op jit(solution)/shard_map/X0_1/ppermute | solution.py:286
  45.1 4.3 %collective-permute-done.9.refs_2_.refs_1_ = bf16[16,64,128]{2,1,0:T(8,128)(2,1)S(1)} collective-permute-done((bf16[16,64,128]{2,1,0:T(8,128)(2,1)S(1)}, bf16[16,64,128]{2,1,0:T(8,128)(2,1)S(1)}, u32[]{:S(2)}, u32[]{:S(2)}) %collective-permute-start.9) | collective-permute-done | bytes 262176 | tf_op jit(solution)/shard_map/X1_0/ppermute | solution.py:286
  52.5 3.7 %Y1_0.1 = (bf16[16,64,128]{2,1,0:T(8,128)(2,1)S(1)}, bf16[16,64,128]{2,1,0:T(8,128)(2,1)S(1)}, bf16[16,64,128]{2,1,0:T(8,128)(2,1)S(1)}, bf16[16,64,128]{2,1,0:T(8,128)(2,1)S(1)}, f32[8,128]{1,0:T(8,128)S(1)}) custom-call(bf16[256,256]{1,0:T(8,128)(2,1)S(1)} %get-tuple-element.272.b_ref, ...), custom_call_target="tpu_custom_call", output_to_operand_aliasing={{4}: (8, {})} | custom-call | tf_op jit(solution)/shard_map/Y1_0/pallas_call | solution.py:268
  56.6 4.1 %collective-permute-done.12.refs_2_.refs_1_ = bf16[16,64,128]{2,1,0:T(8,128)(2,1)S(1)} collective-permute-done((bf16[16,64,128]{2,1,0:T(8,128)(2,1)S(1)}, bf16[16,64,128]{2,1,0:T(8,128)(2,1)S(1)}, u32[]{:S(2)}, u32[]{:S(2)}) %collective-permute-start.12) | collective-permute-done | bytes 262176 | tf_op jit(solution)/shard_map/X1_1/ppermute | solution.py:286
  63.9 5.1 %collective-permute-done.17.refs_1_ = bf16[16,64,128]{2,1,0:T(8,128)(2,1)S(1)} collective-permute-done((bf16[16,64,128]{2,1,0:T(8,128)(2,1)S(1)}, bf16[16,64,128]{2,1,0:T(8,128)(2,1)S(1)}, u32[]{:S(2)}, u32[]{:S(2)}) %collective-permute-start.17) | collective-permute-done | bytes 262176 | tf_op jit(solution)/shard_map/X0_2/ppermute | solution.py:286
  73.4 3.9 %Y1_1.1 = (bf16[16,64,128]{2,1,0:T(8,128)(2,1)S(1)}, bf16[16,64,128]{2,1,0:T(8,128)(2,1)S(1)}, bf16[16,64,128]{2,1,0:T(8,128)(2,1)S(1)}, bf16[16,64,128]{2,1,0:T(8,128)(2,1)S(1)}, f32[8,128]{1,0:T(8,128)S(1)}) custom-call(bf16[256,256]{1,0:T(8,128)(2,1)S(1)} %get-tuple-element.272.b_ref, ...), custom_call_target="tpu_custom_call", output_to_operand_aliasing={{4}: (8, {})} | custom-call | tf_op jit(solution)/shard_map/Y1_1/pallas_call | solution.py:268
  77.3 5.9 %collective-permute-done.18.refs_2_.refs_1_ = bf16[16,64,128]{2,1,0:T(8,128)(2,1)S(1)} collective-permute-done((bf16[16,64,128]{2,1,0:T(8,128)(2,1)S(1)}, bf16[16,64,128]{2,1,0:T(8,128)(2,1)S(1)}, u32[]{:S(2)}, u32[]{:S(2)}) %collective-permute-start.18) | collective-permute-done | bytes 262176 | tf_op jit(solution)/shard_map/Y1_0/ppermute | solution.py:286
  86.1 4.2 %collective-permute-done.15.refs_2_.refs_3_ = bf16[16,64,128]{2,1,0:T(8,128)(2,1)S(1)} collective-permute-done((bf16[16,64,128]{2,1,0:T(8,128)(2,1)S(1)}, bf16[16,64,128]{2,1,0:T(8,128)(2,1)S(1)}, u32[]{:S(2)}, u32[]{:S(2)}) %collective-permute-start.15) | collective-permute-done | bytes 262176 | tf_op jit(solution)/shard_map/X0_3/ppermute | solution.py:286
  90.3 20.9 %collective-permute-done.19.refs_2_.refs_3_ = bf16[16,64,128]{2,1,0:T(8,128)(2,1)S(1)} collective-permute-done((bf16[16,64,128]{2,1,0:T(8,128)(2,1)S(1)}, bf16[16,64,128]{2,1,0:T(8,128)(2,1)S(1)}, u32[]{:S(2)}, u32[]{:S(2)}) %collective-permute-start.19) | collective-permute-done | bytes 262176 | tf_op jit(solution)/shard_map/X1_2/ppermute | solution.py:286
  113.2 9.2 %collective-permute-done.22.refs_2_.refs_1_ = bf16[16,64,128]{2,1,0:T(8,128)(2,1)S(1)} collective-permute-done((bf16[16,64,128]{2,1,0:T(8,128)(2,1)S(1)}, bf16[16,64,128]{2,1,0:T(8,128)(2,1)S(1)}, u32[]{:S(2)}, u32[]{:S(2)}) %collective-permute-start.22) | collective-permute-done | bytes 262176 | tf_op jit(solution)/shard_map/X1_2/ppermute | solution.py:286
  123.0 5.2 %collective-permute-done.23.refs_2_.refs_3_ = bf16[16,64,128]{2,1,0:T(8,128)(2,1)S(1)} collective-permute-done((bf16[16,64,128]{2,1,0:T(8,128)(2,1)S(1)}, bf16[16,64,128]{2,1,0:T(8,128)(2,1)S(1)}, u32[]{:S(2)}, u32[]{:S(2)}) %collective-permute-start.23) | collective-permute-done | bytes 262176 | tf_op jit(solution)/shard_map/Y1_1/ppermute | solution.py:286
  128.1 5.6 %collective-permute-done.24.refs_2_.refs_3_ = bf16[16,64,128]{2,1,0:T(8,128)(2,1)S(1)} collective-permute-done((bf16[16,64,128]{2,1,0:T(8,128)(2,1)S(1)}, bf16[16,64,128]{2,1,0:T(8,128)(2,1)S(1)}, u32[]{:S(2)}, u32[]{:S(2)}) %collective-permute-start.24) | collective-permute-done | bytes 262176 | tf_op jit(solution)/shard_map/Y1_0/ppermute | solution.py:286
  137.6 7.2 %collective-permute-done.21.refs_2_.refs_1_ = bf16[16,64,128]{2,1,0:T(8,128)(2,1)S(1)} collective-permute-done((bf16[16,64,128]{2,1,0:T(8,128)(2,1)S(1)}, bf16[16,64,128]{2,1,0:T(8,128)(2,1)S(1)}, u32[]{:S(2)}, u32[]{:S(2)}) %collective-permute-start.21) | collective-permute-done | bytes 262176 | tf_op jit(solution)/shard_map/X1_3/ppermute | solution.py:286
  144.8 3.8 %collective-permute-start.33 = (bf16[16,64,128]{2,1,0:T(8,128)(2,1)S(1)}, bf16[16,64,128]{2,1,0:T(8,128)(2,1)S(1)}, u32[]{:S(2)}, u32[]{:S(2)}) collective-permute-start(bf16[16,64,128]{2,1,0:T(8,128)(2,1)S(1)} %get-tuple-element.363), channel_id=1, source_target_pairs={{0,1},{1,0},{2,3},{3,2},{4,5},{5,4},{6,7},{7,6},{8,9},{9,8},{10,11... | collective-permute-start | bytes 786440 | tf_op jit(solution)/shard_map/Y0_0/ppermute | solution.py:286
  148.7 3.7 %Y1_2.1 = (bf16[16,64,128]{2,1,0:T(8,128)(2,1)S(1)}, bf16[16,64,128]{2,1,0:T(8,128)(2,1)S(1)}, bf16[16,64,128]{2,1,0:T(8,128)(2,1)S(1)}, bf16[16,64,128]{2,1,0:T(8,128)(2,1)S(1)}, f32[8,128]{1,0:T(8,128)S(1)}) custom-call(bf16[256,256]{1,0:T(8,128)(2,1)S(1)} %get-tuple-element.272.b_ref, ...), custom_call_target="tpu_custom_call", output_to_operand_aliasing={{4}: (8, {})} | custom-call | tf_op jit(solution)/shard_map/Y1_2/pallas_call | solution.py:268
  152.3 4.0 %collective-permute-done.28.refs_2_.refs_1_ = bf16[16,64,128]{2,1,0:T(8,128)(2,1)S(1)} collective-permute-done((bf16[16,64,128]{2,1,0:T(8,128)(2,1)S(1)}, bf16[16,64,128]{2,1,0:T(8,128)(2,1)S(1)}, u32[]{:S(2)}, u32[]{:S(2)}) %collective-permute-start.28) | collective-permute-done | bytes 262176 | tf_op jit(solution)/shard_map/Y1_1/ppermute | solution.py:286
  158.9 8.6 %collective-permute-done.27.refs_3_ = bf16[16,64,128]{2,1,0:T(8,128)(2,1)S(1)} collective-permute-done((bf16[16,64,128]{2,1,0:T(8,128)(2,1)S(1)}, bf16[16,64,128]{2,1,0:T(8,128)(2,1)S(1)}, u32[]{:S(2)}, u32[]{:S(2)}) %collective-permute-start.27) | collective-permute-done | bytes 262176 | tf_op jit(solution)/shard_map/X1_3/ppermute | solution.py:286
  171.6 3.5 %collective-permute-start.37 = (bf16[16,64,128]{2,1,0:T(8,128)(2,1)S(1)}, bf16[16,64,128]{2,1,0:T(8,128)(2,1)S(1)}, u32[]{:S(2)}, u32[]{:S(2)}) collective-permute-start(bf16[16,64,128]{2,1,0:T(8,128)(2,1)S(1)} %get-tuple-element.380), channel_id=1, source_target_pairs={{0,1},{1,0},{2,3},{3,2},{4,5},{5,4},{6,7},{7,6},{8,9},{9,8},{10,11... | collective-permute-start | bytes 786440 | tf_op jit(solution)/shard_map/Y0_1/ppermute | solution.py:286
  178.9 7.7 %collective-permute-done.34.refs_3_ = bf16[16,64,128]{2,1,0:T(8,128)(2,1)S(1)} collective-permute-done((bf16[16,64,128]{2,1,0:T(8,128)(2,1)S(1)}, bf16[16,64,128]{2,1,0:T(8,128)(2,1)S(1)}, u32[]{:S(2)}, u32[]{:S(2)}) %collective-permute-start.34) | collective-permute-done | bytes 262176 | tf_op jit(solution)/shard_map/Y1_2/ppermute | solution.py:286
  187.8 3.9 %collective-permute-start.43 = (bf16[8,64,128]{2,1,0:T(8,128)(2,1)S(1)}, bf16[8,64,128]{2,1,0:T(8,128)(2,1)S(1)}, u32[]{:S(2)}, u32[]{:S(2)}) collective-permute-start(bf16[8,64,128]{2,1,0:T(8,128)(2,1)S(1)} %get-tuple-element.393), channel_id=1, source_target_pairs={{0,18},{1,19},{2,16},{3,17},{4,22},{5,23},{6,20},{7,21},{8,26},{9,... | collective-permute-start | bytes 393224 | tf_op jit(solution)/shard_map/Y1_4/ppermute | solution.py:286
  195.9 5.1 %collective-permute-done.43.refs_3_ = bf16[8,64,128]{2,1,0:T(8,128)(2,1)S(1)} collective-permute-done((bf16[8,64,128]{2,1,0:T(8,128)(2,1)S(1)}, bf16[8,64,128]{2,1,0:T(8,128)(2,1)S(1)}, u32[]{:S(2)}, u32[]{:S(2)}) %collective-permute-start.43) | collective-permute-done | bytes 131104 | tf_op jit(solution)/shard_map/Y1_4/ppermute | solution.py:286
  205.4 4.6 %collective-permute-done.45.refs_2_.refs_1_ = bf16[16,64,128]{2,1,0:T(8,128)(2,1)S(1)} collective-permute-done((bf16[16,64,128]{2,1,0:T(8,128)(2,1)S(1)}, bf16[16,64,128]{2,1,0:T(8,128)(2,1)S(1)}, u32[]{:S(2)}, u32[]{:S(2)}) %collective-permute-start.45) | collective-permute-done | bytes 262176 | tf_op jit(solution)/shard_map/Y0_2/ppermute | solution.py:286
  (170 shorter events, 81.3 us)
Async XLA Ops:
  18.4 21.5 %collective-permute-start.4 = (bf16[16,64,128]{2,1,0:T(8,128)(2,1)S(1)}, bf16[16,64,128]{2,1,0:T(8,128)(2,1)S(1)}, u32[]{:S(2)}, u32[]{:S(2)}) collective-permute-start(bf16[16,64,128]{2,1,0:T(8,128)(2,1)S(1)} %get-tuple-element.247), channel_id=1, source_target_pairs={{0,5},{1,4},{2,7},{3,6},{4,1},{5,0},{6,3},{7,2},{8,13},{9,12},{10,... | collective-permute-start | bytes 786440 | tf_op jit(solution)/shard_map/X0_1/ppermute | solution.py:286
  21.2 21.8 %collective-permute-start.7 = (bf16[16,64,128]{2,1,0:T(8,128)(2,1)S(1)}, bf16[16,64,128]{2,1,0:T(8,128)(2,1)S(1)}, u32[]{:S(2)}, u32[]{:S(2)}) collective-permute-start(bf16[16,64,128]{2,1,0:T(8,128)(2,1)S(1)} %get-tuple-element.265), channel_id=1, source_target_pairs={{0,18},{1,19},{2,16},{3,17},{4,22},{5,23},{6,20},{7,21},{8,26},{9,... | collective-permute-start | bytes 786440 | tf_op jit(solution)/shard_map/X1_0/ppermute | solution.py:286
  25.3 24.0 %collective-permute-start.9 = (bf16[16,64,128]{2,1,0:T(8,128)(2,1)S(1)}, bf16[16,64,128]{2,1,0:T(8,128)(2,1)S(1)}, u32[]{:S(2)}, u32[]{:S(2)}) collective-permute-start(bf16[16,64,128]{2,1,0:T(8,128)(2,1)S(1)} %get-tuple-element.277), channel_id=1, source_target_pairs={{0,2},{1,3},{2,0},{3,1},{4,6},{5,7},{6,4},{7,5},{8,10},{9,11},{10,... | collective-permute-start | bytes 786440 | tf_op jit(solution)/shard_map/X1_0/ppermute | solution.py:286
  44.6 19.2 %collective-permute-start.14 = (bf16[16,64,128]{2,1,0:T(8,128)(2,1)S(1)}, bf16[16,64,128]{2,1,0:T(8,128)(2,1)S(1)}, u32[]{:S(2)}, u32[]{:S(2)}) collective-permute-start(bf16[16,64,128]{2,1,0:T(8,128)(2,1)S(1)} %get-tuple-element.292), channel_id=1, source_target_pairs={{0,4},{4,0},{8,12},{12,8},{16,20},{20,16},{24,28},{28,24},{1,5},{5... | collective-permute-start | bytes 786440 | tf_op jit(solution)/shard_map/X0_2/ppermute | solution.py:286
  49.4 19.6 %collective-permute-start.17 = (bf16[16,64,128]{2,1,0:T(8,128)(2,1)S(1)}, bf16[16,64,128]{2,1,0:T(8,128)(2,1)S(1)}, u32[]{:S(2)}, u32[]{:S(2)}) collective-permute-start(bf16[16,64,128]{2,1,0:T(8,128)(2,1)S(1)} %get-tuple-element.298), channel_id=1, source_target_pairs={{0,1},{1,0},{2,3},{3,2},{4,5},{5,4},{6,7},{7,6},{8,9},{9,8},{10,11... | collective-permute-start | bytes 786440 | tf_op jit(solution)/shard_map/X0_2/ppermute | solution.py:286
  50.1 21.8 %collective-permute-start.16 = (bf16[16,64,128]{2,1,0:T(8,128)(2,1)S(1)}, bf16[16,64,128]{2,1,0:T(8,128)(2,1)S(1)}, u32[]{:S(2)}, u32[]{:S(2)}) collective-permute-start(bf16[16,64,128]{2,1,0:T(8,128)(2,1)S(1)} %get-tuple-element.295), channel_id=1, source_target_pairs={{0,18},{1,19},{2,16},{3,17},{4,22},{5,23},{6,20},{7,21},{8,26},{9,... | collective-permute-start | bytes 786440 | tf_op jit(solution)/shard_map/X1_1/ppermute | solution.py:286
  60.6 22.6 %collective-permute-start.13 = (bf16[16,64,128]{2,1,0:T(8,128)(2,1)S(1)}, bf16[16,64,128]{2,1,0:T(8,128)(2,1)S(1)}, u32[]{:S(2)}, u32[]{:S(2)}) collective-permute-start(bf16[16,64,128]{2,1,0:T(8,128)(2,1)S(1)} %get-tuple-element.289), channel_id=1, source_target_pairs={{0,1},{1,0},{2,3},{3,2},{4,5},{5,4},{6,7},{7,6},{8,9},{9,8},{10,11... | collective-permute-start | bytes 786440 | tf_op jit(solution)/shard_map/X0_3/ppermute | solution.py:286
  60.6 22.6 %collective-permute-start.18 = (bf16[16,64,128]{2,1,0:T(8,128)(2,1)S(1)}, bf16[16,64,128]{2,1,0:T(8,128)(2,1)S(1)}, u32[]{:S(2)}, u32[]{:S(2)}) collective-permute-start(bf16[16,64,128]{2,1,0:T(8,128)(2,1)S(1)} %get-tuple-element.309), channel_id=1, source_target_pairs={{0,2},{1,3},{2,0},{3,1},{4,6},{5,7},{6,4},{7,5},{8,10},{9,11},{10,... | collective-permute-start | bytes 786440 | tf_op jit(solution)/shard_map/Y1_0/ppermute | solution.py:286
  63.9 26.4 %collective-permute-start.15 = (bf16[16,64,128]{2,1,0:T(8,128)(2,1)S(1)}, bf16[16,64,128]{2,1,0:T(8,128)(2,1)S(1)}, u32[]{:S(2)}, u32[]{:S(2)}) collective-permute-start(bf16[16,64,128]{2,1,0:T(8,128)(2,1)S(1)} %get-tuple-element.293), channel_id=1, source_target_pairs={{0,5},{1,4},{2,7},{3,6},{4,1},{5,0},{6,3},{7,2},{8,13},{9,12},{10,... | collective-permute-start | bytes 786440 | tf_op jit(solution)/shard_map/X0_3/ppermute | solution.py:286
  69.5 41.7 %collective-permute-start.19 = (bf16[16,64,128]{2,1,0:T(8,128)(2,1)S(1)}, bf16[16,64,128]{2,1,0:T(8,128)(2,1)S(1)}, u32[]{:S(2)}, u32[]{:S(2)}) collective-permute-start(bf16[16,64,128]{2,1,0:T(8,128)(2,1)S(1)} %get-tuple-element.313), channel_id=1, source_target_pairs={{0,18},{1,19},{2,16},{3,17},{4,22},{5,23},{6,20},{7,21},{8,26},{9,... | collective-permute-start | bytes 786440 | tf_op jit(solution)/shard_map/X1_2/ppermute | solution.py:286
  71.9 41.3 %collective-permute-start.20 = (bf16[16,64,128]{2,1,0:T(8,128)(2,1)S(1)}, bf16[16,64,128]{2,1,0:T(8,128)(2,1)S(1)}, u32[]{:S(2)}, u32[]{:S(2)}) collective-permute-start(bf16[16,64,128]{2,1,0:T(8,128)(2,1)S(1)} %get-tuple-element.318), channel_id=1, source_target_pairs={{0,16},{4,20},{8,24},{12,28},{16,0},{20,4},{24,8},{28,12},{1,17},{... | collective-permute-start | bytes 786440 | tf_op jit(solution)/shard_map/Y1_0/ppermute | solution.py:286
  83.2 39.3 %collective-permute-start.22 = (bf16[16,64,128]{2,1,0:T(8,128)(2,1)S(1)}, bf16[16,64,128]{2,1,0:T(8,128)(2,1)S(1)}, u32[]{:S(2)}, u32[]{:S(2)}) collective-permute-start(bf16[16,64,128]{2,1,0:T(8,128)(2,1)S(1)} %get-tuple-element.324), channel_id=1, source_target_pairs={{0,2},{1,3},{2,0},{3,1},{4,6},{5,7},{6,4},{7,5},{8,10},{9,11},{10,... | collective-permute-start | bytes 786440 | tf_op jit(solution)/shard_map/X1_2/ppermute | solution.py:286
  83.2 44.9 %collective-permute-start.23 = (bf16[16,64,128]{2,1,0:T(8,128)(2,1)S(1)}, bf16[16,64,128]{2,1,0:T(8,128)(2,1)S(1)}, u32[]{:S(2)}, u32[]{:S(2)}) collective-permute-start(bf16[16,64,128]{2,1,0:T(8,128)(2,1)S(1)} %get-tuple-element.326), channel_id=1, source_target_pairs={{0,18},{1,19},{2,16},{3,17},{4,22},{5,23},{6,20},{7,21},{8,26},{9,... | collective-permute-start | bytes 786440 | tf_op jit(solution)/shard_map/Y1_1/ppermute | solution.py:286
  90.3 43.5 %collective-permute-start.24 = (bf16[16,64,128]{2,1,0:T(8,128)(2,1)S(1)}, bf16[16,64,128]{2,1,0:T(8,128)(2,1)S(1)}, u32[]{:S(2)}, u32[]{:S(2)}) collective-permute-start(bf16[16,64,128]{2,1,0:T(8,128)(2,1)S(1)} %get-tuple-element.328), channel_id=1, source_target_pairs={{0,18},{1,19},{2,16},{3,17},{4,22},{5,23},{6,20},{7,21},{8,26},{9,... | collective-permute-start | bytes 786440 | tf_op jit(solution)/shard_map/Y1_0/ppermute | solution.py:286
  111.2 24.5 %collective-permute-start.26 = (bf16[16,64,128]{2,1,0:T(8,128)(2,1)S(1)}, bf16[16,64,128]{2,1,0:T(8,128)(2,1)S(1)}, u32[]{:S(2)}, u32[]{:S(2)}) collective-permute-start(bf16[16,64,128]{2,1,0:T(8,128)(2,1)S(1)} %get-tuple-element.335), channel_id=1, source_target_pairs={{0,16},{4,20},{8,24},{12,28},{16,0},{20,4},{24,8},{28,12},{1,17},{... | collective-permute-start | bytes 786440 | tf_op jit(solution)/shard_map/Y1_1/ppermute | solution.py:286
  113.2 31.6 %collective-permute-start.21 = (bf16[16,64,128]{2,1,0:T(8,128)(2,1)S(1)}, bf16[16,64,128]{2,1,0:T(8,128)(2,1)S(1)}, u32[]{:S(2)}, u32[]{:S(2)}) collective-permute-start(bf16[16,64,128]{2,1,0:T(8,128)(2,1)S(1)} %get-tuple-element.319), channel_id=1, source_target_pairs={{0,2},{1,3},{2,0},{3,1},{4,6},{5,7},{6,4},{7,5},{8,10},{9,11},{10,... | collective-permute-start | bytes 786440 | tf_op jit(solution)/shard_map/X1_3/ppermute | solution.py:286
  122.5 22.3 %collective-permute-start.29 = (bf16[16,64,128]{2,1,0:T(8,128)(2,1)S(1)}, bf16[16,64,128]{2,1,0:T(8,128)(2,1)S(1)}, u32[]{:S(2)}, u32[]{:S(2)}) collective-permute-start(bf16[16,64,128]{2,1,0:T(8,128)(2,1)S(1)} %get-tuple-element.341), channel_id=1, source_target_pairs={{0,16},{4,20},{8,24},{12,28},{16,0},{20,4},{24,8},{28,12},{1,17},{... | collective-permute-start | bytes 786440 | tf_op jit(solution)/shard_map/X1_2/ppermute | solution.py:286
  133.7 22.6 %collective-permute-start.25 = (bf16[16,64,128]{2,1,0:T(8,128)(2,1)S(1)}, bf16[16,64,128]{2,1,0:T(8,128)(2,1)S(1)}, u32[]{:S(2)}, u32[]{:S(2)}) collective-permute-start(bf16[16,64,128]{2,1,0:T(8,128)(2,1)S(1)} %get-tuple-element.329), channel_id=1, source_target_pairs={{0,16},{4,20},{8,24},{12,28},{16,0},{20,4},{24,8},{28,12},{1,17},{... | collective-permute-start | bytes 786440 | tf_op jit(solution)/shard_map/X1_3/ppermute | solution.py:286
  135.3 21.1 %collective-permute-start.28 = (bf16[16,64,128]{2,1,0:T(8,128)(2,1)S(1)}, bf16[16,64,128]{2,1,0:T(8,128)(2,1)S(1)}, u32[]{:S(2)}, u32[]{:S(2)}) collective-permute-start(bf16[16,64,128]{2,1,0:T(8,128)(2,1)S(1)} %get-tuple-element.339), channel_id=1, source_target_pairs={{0,2},{1,3},{2,0},{3,1},{4,6},{5,7},{6,4},{7,5},{8,10},{9,11},{10,... | collective-permute-start | bytes 786440 | tf_op jit(solution)/shard_map/Y1_1/ppermute | solution.py:286
  135.7 21.6 %collective-permute-start.30 = (bf16[16,64,128]{2,1,0:T(8,128)(2,1)S(1)}, bf16[16,64,128]{2,1,0:T(8,128)(2,1)S(1)}, u32[]{:S(2)}, u32[]{:S(2)}) collective-permute-start(bf16[16,64,128]{2,1,0:T(8,128)(2,1)S(1)} %get-tuple-element.352), channel_id=1, source_target_pairs={{0,5},{1,4},{2,7},{3,6},{4,1},{5,0},{6,3},{7,2},{8,13},{9,12},{10,... | collective-permute-start | bytes 786440 | tf_op jit(solution)/shard_map/Y0_0/ppermute | solution.py:286
  144.8 22.7 %collective-permute-start.27 = (bf16[16,64,128]{2,1,0:T(8,128)(2,1)S(1)}, bf16[16,64,128]{2,1,0:T(8,128)(2,1)S(1)}, u32[]{:S(2)}, u32[]{:S(2)}) collective-permute-start(bf16[16,64,128]{2,1,0:T(8,128)(2,1)S(1)} %get-tuple-element.337), channel_id=1, source_target_pairs={{0,18},{1,19},{2,16},{3,17},{4,22},{5,23},{6,20},{7,21},{8,26},{9,... | collective-permute-start | bytes 786440 | tf_op jit(solution)/shard_map/X1_3/ppermute | solution.py:286
  144.8 25.1 %collective-permute-start.33 = (bf16[16,64,128]{2,1,0:T(8,128)(2,1)S(1)}, bf16[16,64,128]{2,1,0:T(8,128)(2,1)S(1)}, u32[]{:S(2)}, u32[]{:S(2)}) collective-permute-start(bf16[16,64,128]{2,1,0:T(8,128)(2,1)S(1)} %get-tuple-element.363), channel_id=1, source_target_pairs={{0,1},{1,0},{2,3},{3,2},{4,5},{5,4},{6,7},{7,6},{8,9},{9,8},{10,11... | collective-permute-start | bytes 786440 | tf_op jit(solution)/shard_map/Y0_0/ppermute | solution.py:286
  156.3 21.2 %collective-permute-start.31 = (bf16[16,64,128]{2,1,0:T(8,128)(2,1)S(1)}, bf16[16,64,128]{2,1,0:T(8,128)(2,1)S(1)}, u32[]{:S(2)}, u32[]{:S(2)}) collective-permute-start(bf16[16,64,128]{2,1,0:T(8,128)(2,1)S(1)} %get-tuple-element.357), channel_id=1, source_target_pairs={{0,2},{1,3},{2,0},{3,1},{4,6},{5,7},{6,4},{7,5},{8,10},{9,11},{10,... | collective-permute-start | bytes 786440 | tf_op jit(solution)/shard_map/Y1_2/ppermute | solution.py:286
  157.4 20.2 %collective-permute-start.35 = (bf16[16,64,128]{2,1,0:T(8,128)(2,1)S(1)}, bf16[16,64,128]{2,1,0:T(8,128)(2,1)S(1)}, u32[]{:S(2)}, u32[]{:S(2)}) collective-permute-start(bf16[16,64,128]{2,1,0:T(8,128)(2,1)S(1)} %get-tuple-element.373), channel_id=1, source_target_pairs={{0,5},{1,4},{2,7},{3,6},{4,1},{5,0},{6,3},{7,2},{8,13},{9,12},{10,... | collective-permute-start | bytes 786440 | tf_op jit(solution)/shard_map/Y0_1/ppermute | solution.py:286
  (34 other events, 354.9 us)

commit v4 on v3

--- a/solution.py
+++ b/solution.py
@@ -117,8 +117,11 @@
     refs, (tiles, sems, *held) = (refs[:-4], refs[-4:]) if first else (refs[:-2], refs[-2:])
     copies = []
     k0 = own_index(masks)[0]
-    for i, (source, target) in enumerate(zip((first_ref, second_ref), held)):
-        copies.append(pltpu.make_async_copy(source, target, sems.at[4 + i]))
+    if first:
+        for i, (source, target) in enumerate(
+            ((first_ref.at[0], held[0].at[0]), (second_ref, held[1]), (first_ref.at[1], held[0].at[1]))
+        ):
+            copies.append(pltpu.make_async_copy(source, target, sems.at[4 + i]))
     for d in range(4):
         copies.append(
             pltpu.make_async_copy(image_ref.at[k0 ^ d, index], tiles.at[d], sems.at[d])
@@ -132,11 +135,10 @@
         r = inner.shape[0]
         for copy in copies[:2]:
             copy.wait()
-        copies = copies[2:]
+        late, copies = copies[2], copies[3:]
         folded = dot(levels[0].reshape(16 * r, r), inner[...]).astype(jnp.bfloat16)
         w0 = jnp.concatenate(blocks_of(folded.reshape(16, r, r), r), axis=0)
-        w1 = jnp.concatenate(blocks_of(levels[1].reshape(16, r, r), r), axis=0)
-        w0_ref[...], w1_ref[...] = w0, w1
+        w0_ref[...] = w0
     else:
         w0, w1 = first_ref[...], second_ref[...]
         outs = refs[-1 - 4 * len(sizes) : -1]
@@ -145,6 +147,10 @@
         copies[d].wait()
         x = stacked([[tiles[d, 4 * a + c] for a in range(4)] for c in range(4)])
         y = dot(w0, x).astype(jnp.bfloat16)
+        if first and d == 0:
+            late.wait()
+            w1 = jnp.concatenate(blocks_of(levels[1].reshape(16, r, r), r), axis=0)
+            w1_ref[...] = w1
         x = stacked([[tile(y, e, a, r, n) for e in range(4)] for a in range(4)])
         y = dot(w1, x).astype(jnp.bfloat16)
         start = 0
@@ -318,7 +324,7 @@
         sizes = X_PIECES[index]
         first = not prepared
         weights = [levels, inner] if first else list(prepared["local"])
-        scratch = [pltpu.VMEM((4, chunk, r, n), bf16), pltpu.SemaphoreType.DMA((6,))]
+        scratch = [pltpu.VMEM((4, chunk, r, n), bf16), pltpu.SemaphoreType.DMA((7,))]
         if first:
             scratch += [pltpu.VMEM(levels.shape, bf16), pltpu.VMEM((r, r), bf16)]
         outs_count = 4 * len(sizes) + 2 * first

time: 224 us -> 224 us (level)
  no operation moved by 1% of the time
where the time goes in v4:
time: 224 us
  waiting for transfers between devices  129 us (58%)
  starting transfers between devices  52.2 us (23%)
  Pallas kernels  40.8 us (18%)
    ppermute x54, waiting for transfers between devices, send(): return lax.ppermute(block, axis, pairs)  129 us
    ppermute x54, starting transfers between devices, send(): return lax.ppermute(block, axis, pairs)  52.2 us
    pallas_call x78, Pallas kernels, kernel(): pl.pallas_call(body, out_shape=[*out_shapes, TOKEN], in_specs=[*specs, *[...  40.8 us
  transfers between devices with their start and end apart: 54, of which 25 were waited for; matrix products, arithmetic and copies ran while one was open for 0% of the time, Pallas kernels for 16%

profile of v4, /device:TPU:0, one launch (start us, length us, event | category | flops | bytes accessed | tf_op | source)
XLA Modules:
  0.0 224.0 jit_solution(2818561937791542721)
XLA Ops:
  21.2 3.6 %collective-permute-start.7 = (bf16[16,64,128]{2,1,0:T(8,128)(2,1)S(1)}, bf16[16,64,128]{2,1,0:T(8,128)(2,1)S(1)}, u32[]{:S(2)}, u32[]{:S(2)}) collective-permute-start(bf16[16,64,128]{2,1,0:T(8,128)(2,1)S(1)} %get-tuple-element.265), channel_id=1, source_target_pairs={{0,18},{1,19},{2,16},{3,17},{4,22},{5,23},{6,20},{7,21},{8,26},{9,... | collective-permute-start | bytes 786440 | tf_op jit(solution)/shard_map/X1_0/ppermute | solution.py:292
  25.7 9.7 %collective-permute-done.2.refs_1_ = bf16[16,64,128]{2,1,0:T(8,128)(2,1)S(1)} collective-permute-done((bf16[16,64,128]{2,1,0:T(8,128)(2,1)S(1)}, bf16[16,64,128]{2,1,0:T(8,128)(2,1)S(1)}, u32[]{:S(2)}, u32[]{:S(2)}) %collective-permute-start.2) | collective-permute-done | bytes 262176 | tf_op jit(solution)/shard_map/X0_1/ppermute | solution.py:292
  35.4 4.5 %collective-permute-done.4.refs_3_ = bf16[16,64,128]{2,1,0:T(8,128)(2,1)S(1)} collective-permute-done((bf16[16,64,128]{2,1,0:T(8,128)(2,1)S(1)}, bf16[16,64,128]{2,1,0:T(8,128)(2,1)S(1)}, u32[]{:S(2)}, u32[]{:S(2)}) %collective-permute-start.4) | collective-permute-done | bytes 262176 | tf_op jit(solution)/shard_map/X0_1/ppermute | solution.py:292
  45.1 4.3 %collective-permute-done.9.refs_2_.refs_1_ = bf16[16,64,128]{2,1,0:T(8,128)(2,1)S(1)} collective-permute-done((bf16[16,64,128]{2,1,0:T(8,128)(2,1)S(1)}, bf16[16,64,128]{2,1,0:T(8,128)(2,1)S(1)}, u32[]{:S(2)}, u32[]{:S(2)}) %collective-permute-start.9) | collective-permute-done | bytes 262176 | tf_op jit(solution)/shard_map/X1_0/ppermute | solution.py:292
  52.5 3.7 %Y1_0.1 = (bf16[16,64,128]{2,1,0:T(8,128)(2,1)S(1)}, bf16[16,64,128]{2,1,0:T(8,128)(2,1)S(1)}, bf16[16,64,128]{2,1,0:T(8,128)(2,1)S(1)}, bf16[16,64,128]{2,1,0:T(8,128)(2,1)S(1)}, f32[8,128]{1,0:T(8,128)S(1)}) custom-call(bf16[256,256]{1,0:T(8,128)(2,1)S(1)} %get-tuple-element.272.b_ref, ...), custom_call_target="tpu_custom_call", output_to_operand_aliasing={{4}: (8, {})} | custom-call | tf_op jit(solution)/shard_map/Y1_0/pallas_call | solution.py:274
  56.6 4.1 %collective-permute-done.12.refs_2_.refs_1_ = bf16[16,64,128]{2,1,0:T(8,128)(2,1)S(1)} collective-permute-done((bf16[16,64,128]{2,1,0:T(8,128)(2,1)S(1)}, bf16[16,64,128]{2,1,0:T(8,128)(2,1)S(1)}, u32[]{:S(2)}, u32[]{:S(2)}) %collective-permute-start.12) | collective-permute-done | bytes 262176 | tf_op jit(solution)/shard_map/X1_1/ppermute | solution.py:292
  63.9 5.1 %collective-permute-done.17.refs_1_ = bf16[16,64,128]{2,1,0:T(8,128)(2,1)S(1)} collective-permute-done((bf16[16,64,128]{2,1,0:T(8,128)(2,1)S(1)}, bf16[16,64,128]{2,1,0:T(8,128)(2,1)S(1)}, u32[]{:S(2)}, u32[]{:S(2)}) %collective-permute-start.17) | collective-permute-done | bytes 262176 | tf_op jit(solution)/shard_map/X0_2/ppermute | solution.py:292
  73.4 3.9 %Y1_1.1 = (bf16[16,64,128]{2,1,0:T(8,128)(2,1)S(1)}, bf16[16,64,128]{2,1,0:T(8,128)(2,1)S(1)}, bf16[16,64,128]{2,1,0:T(8,128)(2,1)S(1)}, bf16[16,64,128]{2,1,0:T(8,128)(2,1)S(1)}, f32[8,128]{1,0:T(8,128)S(1)}) custom-call(bf16[256,256]{1,0:T(8,128)(2,1)S(1)} %get-tuple-element.272.b_ref, ...), custom_call_target="tpu_custom_call", output_to_operand_aliasing={{4}: (8, {})} | custom-call | tf_op jit(solution)/shard_map/Y1_1/pallas_call | solution.py:274
  77.3 5.9 %collective-permute-done.18.refs_2_.refs_1_ = bf16[16,64,128]{2,1,0:T(8,128)(2,1)S(1)} collective-permute-done((bf16[16,64,128]{2,1,0:T(8,128)(2,1)S(1)}, bf16[16,64,128]{2,1,0:T(8,128)(2,1)S(1)}, u32[]{:S(2)}, u32[]{:S(2)}) %collective-permute-start.18) | collective-permute-done | bytes 262176 | tf_op jit(solution)/shard_map/Y1_0/ppermute | solution.py:292
  86.1 4.2 %collective-permute-done.15.refs_2_.refs_3_ = bf16[16,64,128]{2,1,0:T(8,128)(2,1)S(1)} collective-permute-done((bf16[16,64,128]{2,1,0:T(8,128)(2,1)S(1)}, bf16[16,64,128]{2,1,0:T(8,128)(2,1)S(1)}, u32[]{:S(2)}, u32[]{:S(2)}) %collective-permute-start.15) | collective-permute-done | bytes 262176 | tf_op jit(solution)/shard_map/X0_3/ppermute | solution.py:292
  90.3 20.9 %collective-permute-done.19.refs_2_.refs_3_ = bf16[16,64,128]{2,1,0:T(8,128)(2,1)S(1)} collective-permute-done((bf16[16,64,128]{2,1,0:T(8,128)(2,1)S(1)}, bf16[16,64,128]{2,1,0:T(8,128)(2,1)S(1)}, u32[]{:S(2)}, u32[]{:S(2)}) %collective-permute-start.19) | collective-permute-done | bytes 262176 | tf_op jit(solution)/shard_map/X1_2/ppermute | solution.py:292
  113.2 9.2 %collective-permute-done.22.refs_2_.refs_1_ = bf16[16,64,128]{2,1,0:T(8,128)(2,1)S(1)} collective-permute-done((bf16[16,64,128]{2,1,0:T(8,128)(2,1)S(1)}, bf16[16,64,128]{2,1,0:T(8,128)(2,1)S(1)}, u32[]{:S(2)}, u32[]{:S(2)}) %collective-permute-start.22) | collective-permute-done | bytes 262176 | tf_op jit(solution)/shard_map/X1_2/ppermute | solution.py:292
  123.0 5.2 %collective-permute-done.23.refs_2_.refs_3_ = bf16[16,64,128]{2,1,0:T(8,128)(2,1)S(1)} collective-permute-done((bf16[16,64,128]{2,1,0:T(8,128)(2,1)S(1)}, bf16[16,64,128]{2,1,0:T(8,128)(2,1)S(1)}, u32[]{:S(2)}, u32[]{:S(2)}) %collective-permute-start.23) | collective-permute-done | bytes 262176 | tf_op jit(solution)/shard_map/Y1_1/ppermute | solution.py:292
  128.1 5.6 %collective-permute-done.24.refs_2_.refs_3_ = bf16[16,64,128]{2,1,0:T(8,128)(2,1)S(1)} collective-permute-done((bf16[16,64,128]{2,1,0:T(8,128)(2,1)S(1)}, bf16[16,64,128]{2,1,0:T(8,128)(2,1)S(1)}, u32[]{:S(2)}, u32[]{:S(2)}) %collective-permute-start.24) | collective-permute-done | bytes 262176 | tf_op jit(solution)/shard_map/Y1_0/ppermute | solution.py:292
  137.6 7.2 %collective-permute-done.21.refs_2_.refs_1_ = bf16[16,64,128]{2,1,0:T(8,128)(2,1)S(1)} collective-permute-done((bf16[16,64,128]{2,1,0:T(8,128)(2,1)S(1)}, bf16[16,64,128]{2,1,0:T(8,128)(2,1)S(1)}, u32[]{:S(2)}, u32[]{:S(2)}) %collective-permute-start.21) | collective-permute-done | bytes 262176 | tf_op jit(solution)/shard_map/X1_3/ppermute | solution.py:292
  144.8 3.8 %collective-permute-start.33 = (bf16[16,64,128]{2,1,0:T(8,128)(2,1)S(1)}, bf16[16,64,128]{2,1,0:T(8,128)(2,1)S(1)}, u32[]{:S(2)}, u32[]{:S(2)}) collective-permute-start(bf16[16,64,128]{2,1,0:T(8,128)(2,1)S(1)} %get-tuple-element.363), channel_id=1, source_target_pairs={{0,1},{1,0},{2,3},{3,2},{4,5},{5,4},{6,7},{7,6},{8,9},{9,8},{10,11... | collective-permute-start | bytes 786440 | tf_op jit(solution)/shard_map/Y0_0/ppermute | solution.py:292
  148.7 3.7 %Y1_2.1 = (bf16[16,64,128]{2,1,0:T(8,128)(2,1)S(1)}, bf16[16,64,128]{2,1,0:T(8,128)(2,1)S(1)}, bf16[16,64,128]{2,1,0:T(8,128)(2,1)S(1)}, bf16[16,64,128]{2,1,0:T(8,128)(2,1)S(1)}, f32[8,128]{1,0:T(8,128)S(1)}) custom-call(bf16[256,256]{1,0:T(8,128)(2,1)S(1)} %get-tuple-element.272.b_ref, ...), custom_call_target="tpu_custom_call", output_to_operand_aliasing={{4}: (8, {})} | custom-call | tf_op jit(solution)/shard_map/Y1_2/pallas_call | solution.py:274
  152.3 4.0 %collective-permute-done.28.refs_2_.refs_1_ = bf16[16,64,128]{2,1,0:T(8,128)(2,1)S(1)} collective-permute-done((bf16[16,64,128]{2,1,0:T(8,128)(2,1)S(1)}, bf16[16,64,128]{2,1,0:T(8,128)(2,1)S(1)}, u32[]{:S(2)}, u32[]{:S(2)}) %collective-permute-start.28) | collective-permute-done | bytes 262176 | tf_op jit(solution)/shard_map/Y1_1/ppermute | solution.py:292
  159.0 8.6 %collective-permute-done.27.refs_3_ = bf16[16,64,128]{2,1,0:T(8,128)(2,1)S(1)} collective-permute-done((bf16[16,64,128]{2,1,0:T(8,128)(2,1)S(1)}, bf16[16,64,128]{2,1,0:T(8,128)(2,1)S(1)}, u32[]{:S(2)}, u32[]{:S(2)}) %collective-permute-start.27) | collective-permute-done | bytes 262176 | tf_op jit(solution)/shard_map/X1_3/ppermute | solution.py:292
  171.6 3.5 %collective-permute-start.37 = (bf16[16,64,128]{2,1,0:T(8,128)(2,1)S(1)}, bf16[16,64,128]{2,1,0:T(8,128)(2,1)S(1)}, u32[]{:S(2)}, u32[]{:S(2)}) collective-permute-start(bf16[16,64,128]{2,1,0:T(8,128)(2,1)S(1)} %get-tuple-element.380), channel_id=1, source_target_pairs={{0,1},{1,0},{2,3},{3,2},{4,5},{5,4},{6,7},{7,6},{8,9},{9,8},{10,11... | collective-permute-start | bytes 786440 | tf_op jit(solution)/shard_map/Y0_1/ppermute | solution.py:292
  178.9 7.7 %collective-permute-done.34.refs_3_ = bf16[16,64,128]{2,1,0:T(8,128)(2,1)S(1)} collective-permute-done((bf16[16,64,128]{2,1,0:T(8,128)(2,1)S(1)}, bf16[16,64,128]{2,1,0:T(8,128)(2,1)S(1)}, u32[]{:S(2)}, u32[]{:S(2)}) %collective-permute-start.34) | collective-permute-done | bytes 262176 | tf_op jit(solution)/shard_map/Y1_2/ppermute | solution.py:292
  187.8 3.9 %collective-permute-start.43 = (bf16[8,64,128]{2,1,0:T(8,128)(2,1)S(1)}, bf16[8,64,128]{2,1,0:T(8,128)(2,1)S(1)}, u32[]{:S(2)}, u32[]{:S(2)}) collective-permute-start(bf16[8,64,128]{2,1,0:T(8,128)(2,1)S(1)} %get-tuple-element.393), channel_id=1, source_target_pairs={{0,18},{1,19},{2,16},{3,17},{4,22},{5,23},{6,20},{7,21},{8,26},{9,... | collective-permute-start | bytes 393224 | tf_op jit(solution)/shard_map/Y1_4/ppermute | solution.py:292
  195.9 5.1 %collective-permute-done.43.refs_3_ = bf16[8,64,128]{2,1,0:T(8,128)(2,1)S(1)} collective-permute-done((bf16[8,64,128]{2,1,0:T(8,128)(2,1)S(1)}, bf16[8,64,128]{2,1,0:T(8,128)(2,1)S(1)}, u32[]{:S(2)}, u32[]{:S(2)}) %collective-permute-start.43) | collective-permute-done | bytes 131104 | tf_op jit(solution)/shard_map/Y1_4/ppermute | solution.py:292
  205.4 4.6 %collective-permute-done.45.refs_2_.refs_1_ = bf16[16,64,128]{2,1,0:T(8,128)(2,1)S(1)} collective-permute-done((bf16[16,64,128]{2,1,0:T(8,128)(2,1)S(1)}, bf16[16,64,128]{2,1,0:T(8,128)(2,1)S(1)}, u32[]{:S(2)}, u32[]{:S(2)}) %collective-permute-start.45) | collective-permute-done | bytes 262176 | tf_op jit(solution)/shard_map/Y0_2/ppermute | solution.py:292
  (170 shorter events, 81.2 us)
Async XLA Ops:
  18.4 21.5 %collective-permute-start.4 = (bf16[16,64,128]{2,1,0:T(8,128)(2,1)S(1)}, bf16[16,64,128]{2,1,0:T(8,128)(2,1)S(1)}, u32[]{:S(2)}, u32[]{:S(2)}) collective-permute-start(bf16[16,64,128]{2,1,0:T(8,128)(2,1)S(1)} %get-tuple-element.247), channel_id=1, source_target_pairs={{0,5},{1,4},{2,7},{3,6},{4,1},{5,0},{6,3},{7,2},{8,13},{9,12},{10,... | collective-permute-start | bytes 786440 | tf_op jit(solution)/shard_map/X0_1/ppermute | solution.py:292
  21.2 21.8 %collective-permute-start.7 = (bf16[16,64,128]{2,1,0:T(8,128)(2,1)S(1)}, bf16[16,64,128]{2,1,0:T(8,128)(2,1)S(1)}, u32[]{:S(2)}, u32[]{:S(2)}) collective-permute-start(bf16[16,64,128]{2,1,0:T(8,128)(2,1)S(1)} %get-tuple-element.265), channel_id=1, source_target_pairs={{0,18},{1,19},{2,16},{3,17},{4,22},{5,23},{6,20},{7,21},{8,26},{9,... | collective-permute-start | bytes 786440 | tf_op jit(solution)/shard_map/X1_0/ppermute | solution.py:292
  25.3 24.0 %collective-permute-start.9 = (bf16[16,64,128]{2,1,0:T(8,128)(2,1)S(1)}, bf16[16,64,128]{2,1,0:T(8,128)(2,1)S(1)}, u32[]{:S(2)}, u32[]{:S(2)}) collective-permute-start(bf16[16,64,128]{2,1,0:T(8,128)(2,1)S(1)} %get-tuple-element.277), channel_id=1, source_target_pairs={{0,2},{1,3},{2,0},{3,1},{4,6},{5,7},{6,4},{7,5},{8,10},{9,11},{10,... | collective-permute-start | bytes 786440 | tf_op jit(solution)/shard_map/X1_0/ppermute | solution.py:292
  44.6 19.2 %collective-permute-start.14 = (bf16[16,64,128]{2,1,0:T(8,128)(2,1)S(1)}, bf16[16,64,128]{2,1,0:T(8,128)(2,1)S(1)}, u32[]{:S(2)}, u32[]{:S(2)}) collective-permute-start(bf16[16,64,128]{2,1,0:T(8,128)(2,1)S(1)} %get-tuple-element.292), channel_id=1, source_target_pairs={{0,4},{4,0},{8,12},{12,8},{16,20},{20,16},{24,28},{28,24},{1,5},{5... | collective-permute-start | bytes 786440 | tf_op jit(solution)/shard_map/X0_2/ppermute | solution.py:292
  49.4 19.6 %collective-permute-start.17 = (bf16[16,64,128]{2,1,0:T(8,128)(2,1)S(1)}, bf16[16,64,128]{2,1,0:T(8,128)(2,1)S(1)}, u32[]{:S(2)}, u32[]{:S(2)}) collective-permute-start(bf16[16,64,128]{2,1,0:T(8,128)(2,1)S(1)} %get-tuple-element.298), channel_id=1, source_target_pairs={{0,1},{1,0},{2,3},{3,2},{4,5},{5,4},{6,7},{7,6},{8,9},{9,8},{10,11... | collective-permute-start | bytes 786440 | tf_op jit(solution)/shard_map/X0_2/ppermute | solution.py:292
  50.1 21.8 %collective-permute-start.16 = (bf16[16,64,128]{2,1,0:T(8,128)(2,1)S(1)}, bf16[16,64,128]{2,1,0:T(8,128)(2,1)S(1)}, u32[]{:S(2)}, u32[]{:S(2)}) collective-permute-start(bf16[16,64,128]{2,1,0:T(8,128)(2,1)S(1)} %get-tuple-element.295), channel_id=1, source_target_pairs={{0,18},{1,19},{2,16},{3,17},{4,22},{5,23},{6,20},{7,21},{8,26},{9,... | collective-permute-start | bytes 786440 | tf_op jit(solution)/shard_map/X1_1/ppermute | solution.py:292
  60.6 22.6 %collective-permute-start.13 = (bf16[16,64,128]{2,1,0:T(8,128)(2,1)S(1)}, bf16[16,64,128]{2,1,0:T(8,128)(2,1)S(1)}, u32[]{:S(2)}, u32[]{:S(2)}) collective-permute-start(bf16[16,64,128]{2,1,0:T(8,128)(2,1)S(1)} %get-tuple-element.289), channel_id=1, source_target_pairs={{0,1},{1,0},{2,3},{3,2},{4,5},{5,4},{6,7},{7,6},{8,9},{9,8},{10,11... | collective-permute-start | bytes 786440 | tf_op jit(solution)/shard_map/X0_3/ppermute | solution.py:292
  60.7 22.6 %collective-permute-start.18 = (bf16[16,64,128]{2,1,0:T(8,128)(2,1)S(1)}, bf16[16,64,128]{2,1,0:T(8,128)(2,1)S(1)}, u32[]{:S(2)}, u32[]{:S(2)}) collective-permute-start(bf16[16,64,128]{2,1,0:T(8,128)(2,1)S(1)} %get-tuple-element.309), channel_id=1, source_target_pairs={{0,2},{1,3},{2,0},{3,1},{4,6},{5,7},{6,4},{7,5},{8,10},{9,11},{10,... | collective-permute-start | bytes 786440 | tf_op jit(solution)/shard_map/Y1_0/ppermute | solution.py:292
  63.9 26.4 %collective-permute-start.15 = (bf16[16,64,128]{2,1,0:T(8,128)(2,1)S(1)}, bf16[16,64,128]{2,1,0:T(8,128)(2,1)S(1)}, u32[]{:S(2)}, u32[]{:S(2)}) collective-permute-start(bf16[16,64,128]{2,1,0:T(8,128)(2,1)S(1)} %get-tuple-element.293), channel_id=1, source_target_pairs={{0,5},{1,4},{2,7},{3,6},{4,1},{5,0},{6,3},{7,2},{8,13},{9,12},{10,... | collective-permute-start | bytes 786440 | tf_op jit(solution)/shard_map/X0_3/ppermute | solution.py:292
  69.5 41.7 %collective-permute-start.19 = (bf16[16,64,128]{2,1,0:T(8,128)(2,1)S(1)}, bf16[16,64,128]{2,1,0:T(8,128)(2,1)S(1)}, u32[]{:S(2)}, u32[]{:S(2)}) collective-permute-start(bf16[16,64,128]{2,1,0:T(8,128)(2,1)S(1)} %get-tuple-element.313), channel_id=1, source_target_pairs={{0,18},{1,19},{2,16},{3,17},{4,22},{5,23},{6,20},{7,21},{8,26},{9,... | collective-permute-start | bytes 786440 | tf_op jit(solution)/shard_map/X1_2/ppermute | solution.py:292
  71.9 41.3 %collective-permute-start.20 = (bf16[16,64,128]{2,1,0:T(8,128)(2,1)S(1)}, bf16[16,64,128]{2,1,0:T(8,128)(2,1)S(1)}, u32[]{:S(2)}, u32[]{:S(2)}) collective-permute-start(bf16[16,64,128]{2,1,0:T(8,128)(2,1)S(1)} %get-tuple-element.318), channel_id=1, source_target_pairs={{0,16},{4,20},{8,24},{12,28},{16,0},{20,4},{24,8},{28,12},{1,17},{... | collective-permute-start | bytes 786440 | tf_op jit(solution)/shard_map/Y1_0/ppermute | solution.py:292
  83.2 39.3 %collective-permute-start.22 = (bf16[16,64,128]{2,1,0:T(8,128)(2,1)S(1)}, bf16[16,64,128]{2,1,0:T(8,128)(2,1)S(1)}, u32[]{:S(2)}, u32[]{:S(2)}) collective-permute-start(bf16[16,64,128]{2,1,0:T(8,128)(2,1)S(1)} %get-tuple-element.324), channel_id=1, source_target_pairs={{0,2},{1,3},{2,0},{3,1},{4,6},{5,7},{6,4},{7,5},{8,10},{9,11},{10,... | collective-permute-start | bytes 786440 | tf_op jit(solution)/shard_map/X1_2/ppermute | solution.py:292
  83.2 44.9 %collective-permute-start.23 = (bf16[16,64,128]{2,1,0:T(8,128)(2,1)S(1)}, bf16[16,64,128]{2,1,0:T(8,128)(2,1)S(1)}, u32[]{:S(2)}, u32[]{:S(2)}) collective-permute-start(bf16[16,64,128]{2,1,0:T(8,128)(2,1)S(1)} %get-tuple-element.326), channel_id=1, source_target_pairs={{0,18},{1,19},{2,16},{3,17},{4,22},{5,23},{6,20},{7,21},{8,26},{9,... | collective-permute-start | bytes 786440 | tf_op jit(solution)/shard_map/Y1_1/ppermute | solution.py:292
  90.3 43.5 %collective-permute-start.24 = (bf16[16,64,128]{2,1,0:T(8,128)(2,1)S(1)}, bf16[16,64,128]{2,1,0:T(8,128)(2,1)S(1)}, u32[]{:S(2)}, u32[]{:S(2)}) collective-permute-start(bf16[16,64,128]{2,1,0:T(8,128)(2,1)S(1)} %get-tuple-element.328), channel_id=1, source_target_pairs={{0,18},{1,19},{2,16},{3,17},{4,22},{5,23},{6,20},{7,21},{8,26},{9,... | collective-permute-start | bytes 786440 | tf_op jit(solution)/shard_map/Y1_0/ppermute | solution.py:292
  111.2 24.5 %collective-permute-start.26 = (bf16[16,64,128]{2,1,0:T(8,128)(2,1)S(1)}, bf16[16,64,128]{2,1,0:T(8,128)(2,1)S(1)}, u32[]{:S(2)}, u32[]{:S(2)}) collective-permute-start(bf16[16,64,128]{2,1,0:T(8,128)(2,1)S(1)} %get-tuple-element.335), channel_id=1, source_target_pairs={{0,16},{4,20},{8,24},{12,28},{16,0},{20,4},{24,8},{28,12},{1,17},{... | collective-permute-start | bytes 786440 | tf_op jit(solution)/shard_map/Y1_1/ppermute | solution.py:292
  113.2 31.6 %collective-permute-start.21 = (bf16[16,64,128]{2,1,0:T(8,128)(2,1)S(1)}, bf16[16,64,128]{2,1,0:T(8,128)(2,1)S(1)}, u32[]{:S(2)}, u32[]{:S(2)}) collective-permute-start(bf16[16,64,128]{2,1,0:T(8,128)(2,1)S(1)} %get-tuple-element.319), channel_id=1, source_target_pairs={{0,2},{1,3},{2,0},{3,1},{4,6},{5,7},{6,4},{7,5},{8,10},{9,11},{10,... | collective-permute-start | bytes 786440 | tf_op jit(solution)/shard_map/X1_3/ppermute | solution.py:292
  122.5 22.3 %collective-permute-start.29 = (bf16[16,64,128]{2,1,0:T(8,128)(2,1)S(1)}, bf16[16,64,128]{2,1,0:T(8,128)(2,1)S(1)}, u32[]{:S(2)}, u32[]{:S(2)}) collective-permute-start(bf16[16,64,128]{2,1,0:T(8,128)(2,1)S(1)} %get-tuple-element.341), channel_id=1, source_target_pairs={{0,16},{4,20},{8,24},{12,28},{16,0},{20,4},{24,8},{28,12},{1,17},{... | collective-permute-start | bytes 786440 | tf_op jit(solution)/shard_map/X1_2/ppermute | solution.py:292
  133.8 22.6 %collective-permute-start.25 = (bf16[16,64,128]{2,1,0:T(8,128)(2,1)S(1)}, bf16[16,64,128]{2,1,0:T(8,128)(2,1)S(1)}, u32[]{:S(2)}, u32[]{:S(2)}) collective-permute-start(bf16[16,64,128]{2,1,0:T(8,128)(2,1)S(1)} %get-tuple-element.329), channel_id=1, source_target_pairs={{0,16},{4,20},{8,24},{12,28},{16,0},{20,4},{24,8},{28,12},{1,17},{... | collective-permute-start | bytes 786440 | tf_op jit(solution)/shard_map/X1_3/ppermute | solution.py:292
  135.3 21.1 %collective-permute-start.28 = (bf16[16,64,128]{2,1,0:T(8,128)(2,1)S(1)}, bf16[16,64,128]{2,1,0:T(8,128)(2,1)S(1)}, u32[]{:S(2)}, u32[]{:S(2)}) collective-permute-start(bf16[16,64,128]{2,1,0:T(8,128)(2,1)S(1)} %get-tuple-element.339), channel_id=1, source_target_pairs={{0,2},{1,3},{2,0},{3,1},{4,6},{5,7},{6,4},{7,5},{8,10},{9,11},{10,... | collective-permute-start | bytes 786440 | tf_op jit(solution)/shard_map/Y1_1/ppermute | solution.py:292
  135.7 21.6 %collective-permute-start.30 = (bf16[16,64,128]{2,1,0:T(8,128)(2,1)S(1)}, bf16[16,64,128]{2,1,0:T(8,128)(2,1)S(1)}, u32[]{:S(2)}, u32[]{:S(2)}) collective-permute-start(bf16[16,64,128]{2,1,0:T(8,128)(2,1)S(1)} %get-tuple-element.352), channel_id=1, source_target_pairs={{0,5},{1,4},{2,7},{3,6},{4,1},{5,0},{6,3},{7,2},{8,13},{9,12},{10,... | collective-permute-start | bytes 786440 | tf_op jit(solution)/shard_map/Y0_0/ppermute | solution.py:292
  144.8 22.7 %collective-permute-start.27 = (bf16[16,64,128]{2,1,0:T(8,128)(2,1)S(1)}, bf16[16,64,128]{2,1,0:T(8,128)(2,1)S(1)}, u32[]{:S(2)}, u32[]{:S(2)}) collective-permute-start(bf16[16,64,128]{2,1,0:T(8,128)(2,1)S(1)} %get-tuple-element.337), channel_id=1, source_target_pairs={{0,18},{1,19},{2,16},{3,17},{4,22},{5,23},{6,20},{7,21},{8,26},{9,... | collective-permute-start | bytes 786440 | tf_op jit(solution)/shard_map/X1_3/ppermute | solution.py:292
  144.8 25.1 %collective-permute-start.33 = (bf16[16,64,128]{2,1,0:T(8,128)(2,1)S(1)}, bf16[16,64,128]{2,1,0:T(8,128)(2,1)S(1)}, u32[]{:S(2)}, u32[]{:S(2)}) collective-permute-start(bf16[16,64,128]{2,1,0:T(8,128)(2,1)S(1)} %get-tuple-element.363), channel_id=1, source_target_pairs={{0,1},{1,0},{2,3},{3,2},{4,5},{5,4},{6,7},{7,6},{8,9},{9,8},{10,11... | collective-permute-start | bytes 786440 | tf_op jit(solution)/shard_map/Y0_0/ppermute | solution.py:292
  156.3 21.2 %collective-permute-start.31 = (bf16[16,64,128]{2,1,0:T(8,128)(2,1)S(1)}, bf16[16,64,128]{2,1,0:T(8,128)(2,1)S(1)}, u32[]{:S(2)}, u32[]{:S(2)}) collective-permute-start(bf16[16,64,128]{2,1,0:T(8,128)(2,1)S(1)} %get-tuple-element.357), channel_id=1, source_target_pairs={{0,2},{1,3},{2,0},{3,1},{4,6},{5,7},{6,4},{7,5},{8,10},{9,11},{10,... | collective-permute-start | bytes 786440 | tf_op jit(solution)/shard_map/Y1_2/ppermute | solution.py:292
  157.4 20.2 %collective-permute-start.35 = (bf16[16,64,128]{2,1,0:T(8,128)(2,1)S(1)}, bf16[16,64,128]{2,1,0:T(8,128)(2,1)S(1)}, u32[]{:S(2)}, u32[]{:S(2)}) collective-permute-start(bf16[16,64,128]{2,1,0:T(8,128)(2,1)S(1)} %get-tuple-element.373), channel_id=1, source_target_pairs={{0,5},{1,4},{2,7},{3,6},{4,1},{5,0},{6,3},{7,2},{8,13},{9,12},{10,... | collective-permute-start | bytes 786440 | tf_op jit(solution)/shard_map/Y0_1/ppermute | solution.py:292
  (34 other events, 355.8 us)

commit v5 on v3

--- a/solution.py
+++ b/solution.py
@@ -22,8 +22,8 @@
     "-X13d", ".Y13_", "+Y13x", "-Y00z", "+Y12d", "-Y12x", "+Y01z", ".Y14_", "-Y12z", "+Y01x",
     "-Y01d", "+Y14z", "-Y13x", "+Y14x", "-Y12d", ".Y02_", "+Y02d", "-Y01z", "+Y13z", "-Y01x",
     "+Y14d", "-Y14z", "+Y02z", "-Y14x", "+Y13d", ".K51_", "-Y02d", "-Y13z", "-Y14d", ".Y04_",
-    "+Y04z", "+Y00x", "+Y02x", "-Y02z", "+Y04d", "-Y13d", ".Y03_", "+Y03d", "-Y04z", "+Y04x",
-    "-Y00x", "+Y03z", "-Y02x", "+Y03x", ".K50_", ".K52_", "-Y04d", "-Y03d", "-Y04x", "-Y03z",
+    "+Y04z", "+Y00x", "+Y02x", "-Y02z", "+Y04d", "-Y13d", ".Y03_", "+Y03d", "-Y04z", "+Y03z",
+    "-Y00x", "+Y04x", "-Y02x", "+Y03x", ".K50_", ".K52_", "-Y04d", "-Y03d", "-Y04x", "-Y03z",
     "-Y03x", ".K53_",
 )
 VMEM_GRANT = 16 * 2**20

time: 224 us -> 224 us (level)
  no operation moved by 1% of the time
where the time goes in v5:
time: 224 us
  waiting for transfers between devices  129 us (58%)
  starting transfers between devices  52.6 us (23%)
  Pallas kernels  40.5 us (18%)
    ppermute x54, waiting for transfers between devices, send(): return lax.ppermute(block, axis, pairs)  129 us
    ppermute x54, starting transfers between devices, send(): return lax.ppermute(block, axis, pairs)  52.6 us
    pallas_call x78, Pallas kernels, kernel(): pl.pallas_call(body, out_shape=[*out_shapes, TOKEN], in_specs=[*specs, *[...  40.5 us
  transfers between devices with their start and end apart: 54, of which 25 were waited for; matrix products, arithmetic and copies ran while one was open for 0% of the time, Pallas kernels for 16%

profile of v5, /device:TPU:0, one launch (start us, length us, event | category | flops | bytes accessed | tf_op | source)
XLA Modules:
  0.0 224.0 jit_solution(8676999859256107228)
XLA Ops:
  21.2 3.6 %collective-permute-start.7 = (bf16[16,64,128]{2,1,0:T(8,128)(2,1)S(1)}, bf16[16,64,128]{2,1,0:T(8,128)(2,1)S(1)}, u32[]{:S(2)}, u32[]{:S(2)}) collective-permute-start(bf16[16,64,128]{2,1,0:T(8,128)(2,1)S(1)} %get-tuple-element.265), channel_id=1, source_target_pairs={{0,18},{1,19},{2,16},{3,17},{4,22},{5,23},{6,20},{7,21},{8,26},{9,... | collective-permute-start | bytes 786440 | tf_op jit(solution)/shard_map/X1_0/ppermute | solution.py:286
  25.7 9.7 %collective-permute-done.2.refs_1_ = bf16[16,64,128]{2,1,0:T(8,128)(2,1)S(1)} collective-permute-done((bf16[16,64,128]{2,1,0:T(8,128)(2,1)S(1)}, bf16[16,64,128]{2,1,0:T(8,128)(2,1)S(1)}, u32[]{:S(2)}, u32[]{:S(2)}) %collective-permute-start.2) | collective-permute-done | bytes 262176 | tf_op jit(solution)/shard_map/X0_1/ppermute | solution.py:286
  35.4 4.5 %collective-permute-done.4.refs_3_ = bf16[16,64,128]{2,1,0:T(8,128)(2,1)S(1)} collective-permute-done((bf16[16,64,128]{2,1,0:T(8,128)(2,1)S(1)}, bf16[16,64,128]{2,1,0:T(8,128)(2,1)S(1)}, u32[]{:S(2)}, u32[]{:S(2)}) %collective-permute-start.4) | collective-permute-done | bytes 262176 | tf_op jit(solution)/shard_map/X0_1/ppermute | solution.py:286
  45.1 4.3 %collective-permute-done.9.refs_2_.refs_1_ = bf16[16,64,128]{2,1,0:T(8,128)(2,1)S(1)} collective-permute-done((bf16[16,64,128]{2,1,0:T(8,128)(2,1)S(1)}, bf16[16,64,128]{2,1,0:T(8,128)(2,1)S(1)}, u32[]{:S(2)}, u32[]{:S(2)}) %collective-permute-start.9) | collective-permute-done | bytes 262176 | tf_op jit(solution)/shard_map/X1_0/ppermute | solution.py:286
  52.5 3.7 %Y1_0.1 = (bf16[16,64,128]{2,1,0:T(8,128)(2,1)S(1)}, bf16[16,64,128]{2,1,0:T(8,128)(2,1)S(1)}, bf16[16,64,128]{2,1,0:T(8,128)(2,1)S(1)}, bf16[16,64,128]{2,1,0:T(8,128)(2,1)S(1)}, f32[8,128]{1,0:T(8,128)S(1)}) custom-call(bf16[256,256]{1,0:T(8,128)(2,1)S(1)} %get-tuple-element.272.b_ref, ...), custom_call_target="tpu_custom_call", output_to_operand_aliasing={{4}: (8, {})} | custom-call | tf_op jit(solution)/shard_map/Y1_0/pallas_call | solution.py:268
  56.6 4.1 %collective-permute-done.12.refs_2_.refs_1_ = bf16[16,64,128]{2,1,0:T(8,128)(2,1)S(1)} collective-permute-done((bf16[16,64,128]{2,1,0:T(8,128)(2,1)S(1)}, bf16[16,64,128]{2,1,0:T(8,128)(2,1)S(1)}, u32[]{:S(2)}, u32[]{:S(2)}) %collective-permute-start.12) | collective-permute-done | bytes 262176 | tf_op jit(solution)/shard_map/X1_1/ppermute | solution.py:286
  63.9 5.1 %collective-permute-done.17.refs_1_ = bf16[16,64,128]{2,1,0:T(8,128)(2,1)S(1)} collective-permute-done((bf16[16,64,128]{2,1,0:T(8,128)(2,1)S(1)}, bf16[16,64,128]{2,1,0:T(8,128)(2,1)S(1)}, u32[]{:S(2)}, u32[]{:S(2)}) %collective-permute-start.17) | collective-permute-done | bytes 262176 | tf_op jit(solution)/shard_map/X0_2/ppermute | solution.py:286
  73.4 3.9 %Y1_1.1 = (bf16[16,64,128]{2,1,0:T(8,128)(2,1)S(1)}, bf16[16,64,128]{2,1,0:T(8,128)(2,1)S(1)}, bf16[16,64,128]{2,1,0:T(8,128)(2,1)S(1)}, bf16[16,64,128]{2,1,0:T(8,128)(2,1)S(1)}, f32[8,128]{1,0:T(8,128)S(1)}) custom-call(bf16[256,256]{1,0:T(8,128)(2,1)S(1)} %get-tuple-element.272.b_ref, ...), custom_call_target="tpu_custom_call", output_to_operand_aliasing={{4}: (8, {})} | custom-call | tf_op jit(solution)/shard_map/Y1_1/pallas_call | solution.py:268
  77.3 5.9 %collective-permute-done.18.refs_2_.refs_1_ = bf16[16,64,128]{2,1,0:T(8,128)(2,1)S(1)} collective-permute-done((bf16[16,64,128]{2,1,0:T(8,128)(2,1)S(1)}, bf16[16,64,128]{2,1,0:T(8,128)(2,1)S(1)}, u32[]{:S(2)}, u32[]{:S(2)}) %collective-permute-start.18) | collective-permute-done | bytes 262176 | tf_op jit(solution)/shard_map/Y1_0/ppermute | solution.py:286
  86.1 4.2 %collective-permute-done.15.refs_2_.refs_3_ = bf16[16,64,128]{2,1,0:T(8,128)(2,1)S(1)} collective-permute-done((bf16[16,64,128]{2,1,0:T(8,128)(2,1)S(1)}, bf16[16,64,128]{2,1,0:T(8,128)(2,1)S(1)}, u32[]{:S(2)}, u32[]{:S(2)}) %collective-permute-start.15) | collective-permute-done | bytes 262176 | tf_op jit(solution)/shard_map/X0_3/ppermute | solution.py:286
  90.3 20.9 %collective-permute-done.19.refs_2_.refs_3_ = bf16[16,64,128]{2,1,0:T(8,128)(2,1)S(1)} collective-permute-done((bf16[16,64,128]{2,1,0:T(8,128)(2,1)S(1)}, bf16[16,64,128]{2,1,0:T(8,128)(2,1)S(1)}, u32[]{:S(2)}, u32[]{:S(2)}) %collective-permute-start.19) | collective-permute-done | bytes 262176 | tf_op jit(solution)/shard_map/X1_2/ppermute | solution.py:286
  113.2 9.2 %collective-permute-done.22.refs_2_.refs_1_ = bf16[16,64,128]{2,1,0:T(8,128)(2,1)S(1)} collective-permute-done((bf16[16,64,128]{2,1,0:T(8,128)(2,1)S(1)}, bf16[16,64,128]{2,1,0:T(8,128)(2,1)S(1)}, u32[]{:S(2)}, u32[]{:S(2)}) %collective-permute-start.22) | collective-permute-done | bytes 262176 | tf_op jit(solution)/shard_map/X1_2/ppermute | solution.py:286
  123.0 5.2 %collective-permute-done.23.refs_2_.refs_3_ = bf16[16,64,128]{2,1,0:T(8,128)(2,1)S(1)} collective-permute-done((bf16[16,64,128]{2,1,0:T(8,128)(2,1)S(1)}, bf16[16,64,128]{2,1,0:T(8,128)(2,1)S(1)}, u32[]{:S(2)}, u32[]{:S(2)}) %collective-permute-start.23) | collective-permute-done | bytes 262176 | tf_op jit(solution)/shard_map/Y1_1/ppermute | solution.py:286
  128.1 5.6 %collective-permute-done.24.refs_2_.refs_3_ = bf16[16,64,128]{2,1,0:T(8,128)(2,1)S(1)} collective-permute-done((bf16[16,64,128]{2,1,0:T(8,128)(2,1)S(1)}, bf16[16,64,128]{2,1,0:T(8,128)(2,1)S(1)}, u32[]{:S(2)}, u32[]{:S(2)}) %collective-permute-start.24) | collective-permute-done | bytes 262176 | tf_op jit(solution)/shard_map/Y1_0/ppermute | solution.py:286
  137.6 7.2 %collective-permute-done.21.refs_2_.refs_1_ = bf16[16,64,128]{2,1,0:T(8,128)(2,1)S(1)} collective-permute-done((bf16[16,64,128]{2,1,0:T(8,128)(2,1)S(1)}, bf16[16,64,128]{2,1,0:T(8,128)(2,1)S(1)}, u32[]{:S(2)}, u32[]{:S(2)}) %collective-permute-start.21) | collective-permute-done | bytes 262176 | tf_op jit(solution)/shard_map/X1_3/ppermute | solution.py:286
  144.8 3.8 %collective-permute-start.33 = (bf16[16,64,128]{2,1,0:T(8,128)(2,1)S(1)}, bf16[16,64,128]{2,1,0:T(8,128)(2,1)S(1)}, u32[]{:S(2)}, u32[]{:S(2)}) collective-permute-start(bf16[16,64,128]{2,1,0:T(8,128)(2,1)S(1)} %get-tuple-element.363), channel_id=1, source_target_pairs={{0,1},{1,0},{2,3},{3,2},{4,5},{5,4},{6,7},{7,6},{8,9},{9,8},{10,11... | collective-permute-start | bytes 786440 | tf_op jit(solution)/shard_map/Y0_0/ppermute | solution.py:286
  148.7 3.7 %Y1_2.1 = (bf16[16,64,128]{2,1,0:T(8,128)(2,1)S(1)}, bf16[16,64,128]{2,1,0:T(8,128)(2,1)S(1)}, bf16[16,64,128]{2,1,0:T(8,128)(2,1)S(1)}, bf16[16,64,128]{2,1,0:T(8,128)(2,1)S(1)}, f32[8,128]{1,0:T(8,128)S(1)}) custom-call(bf16[256,256]{1,0:T(8,128)(2,1)S(1)} %get-tuple-element.272.b_ref, ...), custom_call_target="tpu_custom_call", output_to_operand_aliasing={{4}: (8, {})} | custom-call | tf_op jit(solution)/shard_map/Y1_2/pallas_call | solution.py:268
  152.3 4.0 %collective-permute-done.28.refs_2_.refs_1_ = bf16[16,64,128]{2,1,0:T(8,128)(2,1)S(1)} collective-permute-done((bf16[16,64,128]{2,1,0:T(8,128)(2,1)S(1)}, bf16[16,64,128]{2,1,0:T(8,128)(2,1)S(1)}, u32[]{:S(2)}, u32[]{:S(2)}) %collective-permute-start.28) | collective-permute-done | bytes 262176 | tf_op jit(solution)/shard_map/Y1_1/ppermute | solution.py:286
  158.9 8.6 %collective-permute-done.27.refs_3_ = bf16[16,64,128]{2,1,0:T(8,128)(2,1)S(1)} collective-permute-done((bf16[16,64,128]{2,1,0:T(8,128)(2,1)S(1)}, bf16[16,64,128]{2,1,0:T(8,128)(2,1)S(1)}, u32[]{:S(2)}, u32[]{:S(2)}) %collective-permute-start.27) | collective-permute-done | bytes 262176 | tf_op jit(solution)/shard_map/X1_3/ppermute | solution.py:286
  171.6 3.5 %collective-permute-start.37 = (bf16[16,64,128]{2,1,0:T(8,128)(2,1)S(1)}, bf16[16,64,128]{2,1,0:T(8,128)(2,1)S(1)}, u32[]{:S(2)}, u32[]{:S(2)}) collective-permute-start(bf16[16,64,128]{2,1,0:T(8,128)(2,1)S(1)} %get-tuple-element.380), channel_id=1, source_target_pairs={{0,1},{1,0},{2,3},{3,2},{4,5},{5,4},{6,7},{7,6},{8,9},{9,8},{10,11... | collective-permute-start | bytes 786440 | tf_op jit(solution)/shard_map/Y0_1/ppermute | solution.py:286
  178.9 7.7 %collective-permute-done.34.refs_3_ = bf16[16,64,128]{2,1,0:T(8,128)(2,1)S(1)} collective-permute-done((bf16[16,64,128]{2,1,0:T(8,128)(2,1)S(1)}, bf16[16,64,128]{2,1,0:T(8,128)(2,1)S(1)}, u32[]{:S(2)}, u32[]{:S(2)}) %collective-permute-start.34) | collective-permute-done | bytes 262176 | tf_op jit(solution)/shard_map/Y1_2/ppermute | solution.py:286
  187.8 3.9 %collective-permute-start.43 = (bf16[8,64,128]{2,1,0:T(8,128)(2,1)S(1)}, bf16[8,64,128]{2,1,0:T(8,128)(2,1)S(1)}, u32[]{:S(2)}, u32[]{:S(2)}) collective-permute-start(bf16[8,64,128]{2,1,0:T(8,128)(2,1)S(1)} %get-tuple-element.393), channel_id=1, source_target_pairs={{0,18},{1,19},{2,16},{3,17},{4,22},{5,23},{6,20},{7,21},{8,26},{9,... | collective-permute-start | bytes 393224 | tf_op jit(solution)/shard_map/Y1_4/ppermute | solution.py:286
  195.9 5.1 %collective-permute-done.43.refs_3_ = bf16[8,64,128]{2,1,0:T(8,128)(2,1)S(1)} collective-permute-done((bf16[8,64,128]{2,1,0:T(8,128)(2,1)S(1)}, bf16[8,64,128]{2,1,0:T(8,128)(2,1)S(1)}, u32[]{:S(2)}, u32[]{:S(2)}) %collective-permute-start.43) | collective-permute-done | bytes 131104 | tf_op jit(solution)/shard_map/Y1_4/ppermute | solution.py:286
  205.4 4.6 %collective-permute-done.45.refs_2_.refs_1_ = bf16[16,64,128]{2,1,0:T(8,128)(2,1)S(1)} collective-permute-done((bf16[16,64,128]{2,1,0:T(8,128)(2,1)S(1)}, bf16[16,64,128]{2,1,0:T(8,128)(2,1)S(1)}, u32[]{:S(2)}, u32[]{:S(2)}) %collective-permute-start.45) | collective-permute-done | bytes 262176 | tf_op jit(solution)/shard_map/Y0_2/ppermute | solution.py:286
  (170 shorter events, 81.3 us)
Async XLA Ops:
  18.4 21.5 %collective-permute-start.4 = (bf16[16,64,128]{2,1,0:T(8,128)(2,1)S(1)}, bf16[16,64,128]{2,1,0:T(8,128)(2,1)S(1)}, u32[]{:S(2)}, u32[]{:S(2)}) collective-permute-start(bf16[16,64,128]{2,1,0:T(8,128)(2,1)S(1)} %get-tuple-element.247), channel_id=1, source_target_pairs={{0,5},{1,4},{2,7},{3,6},{4,1},{5,0},{6,3},{7,2},{8,13},{9,12},{10,... | collective-permute-start | bytes 786440 | tf_op jit(solution)/shard_map/X0_1/ppermute | solution.py:286
  21.2 21.8 %collective-permute-start.7 = (bf16[16,64,128]{2,1,0:T(8,128)(2,1)S(1)}, bf16[16,64,128]{2,1,0:T(8,128)(2,1)S(1)}, u32[]{:S(2)}, u32[]{:S(2)}) collective-permute-start(bf16[16,64,128]{2,1,0:T(8,128)(2,1)S(1)} %get-tuple-element.265), channel_id=1, source_target_pairs={{0,18},{1,19},{2,16},{3,17},{4,22},{5,23},{6,20},{7,21},{8,26},{9,... | collective-permute-start | bytes 786440 | tf_op jit(solution)/shard_map/X1_0/ppermute | solution.py:286
  25.3 24.0 %collective-permute-start.9 = (bf16[16,64,128]{2,1,0:T(8,128)(2,1)S(1)}, bf16[16,64,128]{2,1,0:T(8,128)(2,1)S(1)}, u32[]{:S(2)}, u32[]{:S(2)}) collective-permute-start(bf16[16,64,128]{2,1,0:T(8,128)(2,1)S(1)} %get-tuple-element.277), channel_id=1, source_target_pairs={{0,2},{1,3},{2,0},{3,1},{4,6},{5,7},{6,4},{7,5},{8,10},{9,11},{10,... | collective-permute-start | bytes 786440 | tf_op jit(solution)/shard_map/X1_0/ppermute | solution.py:286
  44.6 19.2 %collective-permute-start.14 = (bf16[16,64,128]{2,1,0:T(8,128)(2,1)S(1)}, bf16[16,64,128]{2,1,0:T(8,128)(2,1)S(1)}, u32[]{:S(2)}, u32[]{:S(2)}) collective-permute-start(bf16[16,64,128]{2,1,0:T(8,128)(2,1)S(1)} %get-tuple-element.292), channel_id=1, source_target_pairs={{0,4},{4,0},{8,12},{12,8},{16,20},{20,16},{24,28},{28,24},{1,5},{5... | collective-permute-start | bytes 786440 | tf_op jit(solution)/shard_map/X0_2/ppermute | solution.py:286
  49.4 19.6 %collective-permute-start.17 = (bf16[16,64,128]{2,1,0:T(8,128)(2,1)S(1)}, bf16[16,64,128]{2,1,0:T(8,128)(2,1)S(1)}, u32[]{:S(2)}, u32[]{:S(2)}) collective-permute-start(bf16[16,64,128]{2,1,0:T(8,128)(2,1)S(1)} %get-tuple-element.298), channel_id=1, source_target_pairs={{0,1},{1,0},{2,3},{3,2},{4,5},{5,4},{6,7},{7,6},{8,9},{9,8},{10,11... | collective-permute-start | bytes 786440 | tf_op jit(solution)/shard_map/X0_2/ppermute | solution.py:286
  50.1 21.8 %collective-permute-start.16 = (bf16[16,64,128]{2,1,0:T(8,128)(2,1)S(1)}, bf16[16,64,128]{2,1,0:T(8,128)(2,1)S(1)}, u32[]{:S(2)}, u32[]{:S(2)}) collective-permute-start(bf16[16,64,128]{2,1,0:T(8,128)(2,1)S(1)} %get-tuple-element.295), channel_id=1, source_target_pairs={{0,18},{1,19},{2,16},{3,17},{4,22},{5,23},{6,20},{7,21},{8,26},{9,... | collective-permute-start | bytes 786440 | tf_op jit(solution)/shard_map/X1_1/ppermute | solution.py:286
  60.6 22.6 %collective-permute-start.13 = (bf16[16,64,128]{2,1,0:T(8,128)(2,1)S(1)}, bf16[16,64,128]{2,1,0:T(8,128)(2,1)S(1)}, u32[]{:S(2)}, u32[]{:S(2)}) collective-permute-start(bf16[16,64,128]{2,1,0:T(8,128)(2,1)S(1)} %get-tuple-element.289), channel_id=1, source_target_pairs={{0,1},{1,0},{2,3},{3,2},{4,5},{5,4},{6,7},{7,6},{8,9},{9,8},{10,11... | collective-permute-start | bytes 786440 | tf_op jit(solution)/shard_map/X0_3/ppermute | solution.py:286
  60.6 22.6 %collective-permute-start.18 = (bf16[16,64,128]{2,1,0:T(8,128)(2,1)S(1)}, bf16[16,64,128]{2,1,0:T(8,128)(2,1)S(1)}, u32[]{:S(2)}, u32[]{:S(2)}) collective-permute-start(bf16[16,64,128]{2,1,0:T(8,128)(2,1)S(1)} %get-tuple-element.309), channel_id=1, source_target_pairs={{0,2},{1,3},{2,0},{3,1},{4,6},{5,7},{6,4},{7,5},{8,10},{9,11},{10,... | collective-permute-start | bytes 786440 | tf_op jit(solution)/shard_map/Y1_0/ppermute | solution.py:286
  63.9 26.4 %collective-permute-start.15 = (bf16[16,64,128]{2,1,0:T(8,128)(2,1)S(1)}, bf16[16,64,128]{2,1,0:T(8,128)(2,1)S(1)}, u32[]{:S(2)}, u32[]{:S(2)}) collective-permute-start(bf16[16,64,128]{2,1,0:T(8,128)(2,1)S(1)} %get-tuple-element.293), channel_id=1, source_target_pairs={{0,5},{1,4},{2,7},{3,6},{4,1},{5,0},{6,3},{7,2},{8,13},{9,12},{10,... | collective-permute-start | bytes 786440 | tf_op jit(solution)/shard_map/X0_3/ppermute | solution.py:286
  69.5 41.7 %collective-permute-start.19 = (bf16[16,64,128]{2,1,0:T(8,128)(2,1)S(1)}, bf16[16,64,128]{2,1,0:T(8,128)(2,1)S(1)}, u32[]{:S(2)}, u32[]{:S(2)}) collective-permute-start(bf16[16,64,128]{2,1,0:T(8,128)(2,1)S(1)} %get-tuple-element.313), channel_id=1, source_target_pairs={{0,18},{1,19},{2,16},{3,17},{4,22},{5,23},{6,20},{7,21},{8,26},{9,... | collective-permute-start | bytes 786440 | tf_op jit(solution)/shard_map/X1_2/ppermute | solution.py:286
  71.9 41.3 %collective-permute-start.20 = (bf16[16,64,128]{2,1,0:T(8,128)(2,1)S(1)}, bf16[16,64,128]{2,1,0:T(8,128)(2,1)S(1)}, u32[]{:S(2)}, u32[]{:S(2)}) collective-permute-start(bf16[16,64,128]{2,1,0:T(8,128)(2,1)S(1)} %get-tuple-element.318), channel_id=1, source_target_pairs={{0,16},{4,20},{8,24},{12,28},{16,0},{20,4},{24,8},{28,12},{1,17},{... | collective-permute-start | bytes 786440 | tf_op jit(solution)/shard_map/Y1_0/ppermute | solution.py:286
  83.2 39.3 %collective-permute-start.22 = (bf16[16,64,128]{2,1,0:T(8,128)(2,1)S(1)}, bf16[16,64,128]{2,1,0:T(8,128)(2,1)S(1)}, u32[]{:S(2)}, u32[]{:S(2)}) collective-permute-start(bf16[16,64,128]{2,1,0:T(8,128)(2,1)S(1)} %get-tuple-element.324), channel_id=1, source_target_pairs={{0,2},{1,3},{2,0},{3,1},{4,6},{5,7},{6,4},{7,5},{8,10},{9,11},{10,... | collective-permute-start | bytes 786440 | tf_op jit(solution)/shard_map/X1_2/ppermute | solution.py:286
  83.2 44.9 %collective-permute-start.23 = (bf16[16,64,128]{2,1,0:T(8,128)(2,1)S(1)}, bf16[16,64,128]{2,1,0:T(8,128)(2,1)S(1)}, u32[]{:S(2)}, u32[]{:S(2)}) collective-permute-start(bf16[16,64,128]{2,1,0:T(8,128)(2,1)S(1)} %get-tuple-element.326), channel_id=1, source_target_pairs={{0,18},{1,19},{2,16},{3,17},{4,22},{5,23},{6,20},{7,21},{8,26},{9,... | collective-permute-start | bytes 786440 | tf_op jit(solution)/shard_map/Y1_1/ppermute | solution.py:286
  90.3 43.5 %collective-permute-start.24 = (bf16[16,64,128]{2,1,0:T(8,128)(2,1)S(1)}, bf16[16,64,128]{2,1,0:T(8,128)(2,1)S(1)}, u32[]{:S(2)}, u32[]{:S(2)}) collective-permute-start(bf16[16,64,128]{2,1,0:T(8,128)(2,1)S(1)} %get-tuple-element.328), channel_id=1, source_target_pairs={{0,18},{1,19},{2,16},{3,17},{4,22},{5,23},{6,20},{7,21},{8,26},{9,... | collective-permute-start | bytes 786440 | tf_op jit(solution)/shard_map/Y1_0/ppermute | solution.py:286
  111.2 24.5 %collective-permute-start.26 = (bf16[16,64,128]{2,1,0:T(8,128)(2,1)S(1)}, bf16[16,64,128]{2,1,0:T(8,128)(2,1)S(1)}, u32[]{:S(2)}, u32[]{:S(2)}) collective-permute-start(bf16[16,64,128]{2,1,0:T(8,128)(2,1)S(1)} %get-tuple-element.335), channel_id=1, source_target_pairs={{0,16},{4,20},{8,24},{12,28},{16,0},{20,4},{24,8},{28,12},{1,17},{... | collective-permute-start | bytes 786440 | tf_op jit(solution)/shard_map/Y1_1/ppermute | solution.py:286
  113.2 31.6 %collective-permute-start.21 = (bf16[16,64,128]{2,1,0:T(8,128)(2,1)S(1)}, bf16[16,64,128]{2,1,0:T(8,128)(2,1)S(1)}, u32[]{:S(2)}, u32[]{:S(2)}) collective-permute-start(bf16[16,64,128]{2,1,0:T(8,128)(2,1)S(1)} %get-tuple-element.319), channel_id=1, source_target_pairs={{0,2},{1,3},{2,0},{3,1},{4,6},{5,7},{6,4},{7,5},{8,10},{9,11},{10,... | collective-permute-start | bytes 786440 | tf_op jit(solution)/shard_map/X1_3/ppermute | solution.py:286
  122.5 22.3 %collective-permute-start.29 = (bf16[16,64,128]{2,1,0:T(8,128)(2,1)S(1)}, bf16[16,64,128]{2,1,0:T(8,128)(2,1)S(1)}, u32[]{:S(2)}, u32[]{:S(2)}) collective-permute-start(bf16[16,64,128]{2,1,0:T(8,128)(2,1)S(1)} %get-tuple-element.341), channel_id=1, source_target_pairs={{0,16},{4,20},{8,24},{12,28},{16,0},{20,4},{24,8},{28,12},{1,17},{... | collective-permute-start | bytes 786440 | tf_op jit(solution)/shard_map/X1_2/ppermute | solution.py:286
  133.7 22.6 %collective-permute-start.25 = (bf16[16,64,128]{2,1,0:T(8,128)(2,1)S(1)}, bf16[16,64,128]{2,1,0:T(8,128)(2,1)S(1)}, u32[]{:S(2)}, u32[]{:S(2)}) collective-permute-start(bf16[16,64,128]{2,1,0:T(8,128)(2,1)S(1)} %get-tuple-element.329), channel_id=1, source_target_pairs={{0,16},{4,20},{8,24},{12,28},{16,0},{20,4},{24,8},{28,12},{1,17},{... | collective-permute-start | bytes 786440 | tf_op jit(solution)/shard_map/X1_3/ppermute | solution.py:286
  135.3 21.1 %collective-permute-start.28 = (bf16[16,64,128]{2,1,0:T(8,128)(2,1)S(1)}, bf16[16,64,128]{2,1,0:T(8,128)(2,1)S(1)}, u32[]{:S(2)}, u32[]{:S(2)}) collective-permute-start(bf16[16,64,128]{2,1,0:T(8,128)(2,1)S(1)} %get-tuple-element.339), channel_id=1, source_target_pairs={{0,2},{1,3},{2,0},{3,1},{4,6},{5,7},{6,4},{7,5},{8,10},{9,11},{10,... | collective-permute-start | bytes 786440 | tf_op jit(solution)/shard_map/Y1_1/ppermute | solution.py:286
  135.7 21.6 %collective-permute-start.30 = (bf16[16,64,128]{2,1,0:T(8,128)(2,1)S(1)}, bf16[16,64,128]{2,1,0:T(8,128)(2,1)S(1)}, u32[]{:S(2)}, u32[]{:S(2)}) collective-permute-start(bf16[16,64,128]{2,1,0:T(8,128)(2,1)S(1)} %get-tuple-element.352), channel_id=1, source_target_pairs={{0,5},{1,4},{2,7},{3,6},{4,1},{5,0},{6,3},{7,2},{8,13},{9,12},{10,... | collective-permute-start | bytes 786440 | tf_op jit(solution)/shard_map/Y0_0/ppermute | solution.py:286
  144.8 22.7 %collective-permute-start.27 = (bf16[16,64,128]{2,1,0:T(8,128)(2,1)S(1)}, bf16[16,64,128]{2,1,0:T(8,128)(2,1)S(1)}, u32[]{:S(2)}, u32[]{:S(2)}) collective-permute-start(bf16[16,64,128]{2,1,0:T(8,128)(2,1)S(1)} %get-tuple-element.337), channel_id=1, source_target_pairs={{0,18},{1,19},{2,16},{3,17},{4,22},{5,23},{6,20},{7,21},{8,26},{9,... | collective-permute-start | bytes 786440 | tf_op jit(solution)/shard_map/X1_3/ppermute | solution.py:286
  144.8 25.1 %collective-permute-start.33 = (bf16[16,64,128]{2,1,0:T(8,128)(2,1)S(1)}, bf16[16,64,128]{2,1,0:T(8,128)(2,1)S(1)}, u32[]{:S(2)}, u32[]{:S(2)}) collective-permute-start(bf16[16,64,128]{2,1,0:T(8,128)(2,1)S(1)} %get-tuple-element.363), channel_id=1, source_target_pairs={{0,1},{1,0},{2,3},{3,2},{4,5},{5,4},{6,7},{7,6},{8,9},{9,8},{10,11... | collective-permute-start | bytes 786440 | tf_op jit(solution)/shard_map/Y0_0/ppermute | solution.py:286
  156.3 21.2 %collective-permute-start.31 = (bf16[16,64,128]{2,1,0:T(8,128)(2,1)S(1)}, bf16[16,64,128]{2,1,0:T(8,128)(2,1)S(1)}, u32[]{:S(2)}, u32[]{:S(2)}) collective-permute-start(bf16[16,64,128]{2,1,0:T(8,128)(2,1)S(1)} %get-tuple-element.357), channel_id=1, source_target_pairs={{0,2},{1,3},{2,0},{3,1},{4,6},{5,7},{6,4},{7,5},{8,10},{9,11},{10,... | collective-permute-start | bytes 786440 | tf_op jit(solution)/shard_map/Y1_2/ppermute | solution.py:286
  157.4 20.2 %collective-permute-start.35 = (bf16[16,64,128]{2,1,0:T(8,128)(2,1)S(1)}, bf16[16,64,128]{2,1,0:T(8,128)(2,1)S(1)}, u32[]{:S(2)}, u32[]{:S(2)}) collective-permute-start(bf16[16,64,128]{2,1,0:T(8,128)(2,1)S(1)} %get-tuple-element.373), channel_id=1, source_target_pairs={{0,5},{1,4},{2,7},{3,6},{4,1},{5,0},{6,3},{7,2},{8,13},{9,12},{10,... | collective-permute-start | bytes 786440 | tf_op jit(solution)/shard_map/Y0_1/ppermute | solution.py:286
  (34 other events, 358.2 us)
